TPU v7x, 32 devices: a whole 2x2x4 slice. The times are simulated.
32 devices in a mesh: cases: 2 (over y), gx: 16 (over z, x, core).
Axes of the slice: x: 2, y: 2, z: 4, core: 2. Of those that a mesh axis runs over, the one named last changes fastest.
Arguments:
- level_set: float32 [128, 256, 256], P(('cases', 'gx')), parts along dimension 0, may hold values from -6 to 6
- sensitivity: float32 [128, 256, 256], P(('cases', 'gx')), parts along dimension 0, may hold values from -2 to 2
- band: int32 [128, 256, 256], P(('cases', 'gx')), parts along dimension 0, may hold values 0 or 1
Outputs:
- speed: float32 [128, 256, 256], P(('cases', 'gx')), parts along dimension 0
- updated: float32 [128, 256, 256], P(('cases', 'gx')), parts along dimension 0
There are 2 independent parts, one for each index of `cases`. A program takes and returns all parts, laid end to end along the dimension named above; each array names one. Nothing has to cross between parts.
All inputs are finite; a program needn't handle non-finite values. No bound on the sum of `band` on one device may be relied on, other than what follows from the above.
Results may differ from a plain program's by a relative error of at most 0.0003.
Values sent between devices are 32-bit elements; how exact they have to be, the bound alone decides.
No kernel may reach another device: no remote copies, remote signals or barrier semaphores. Data moves between devices by JAX's collectives and lax.ppermute only.
A program may use at most 64 MiB of HBM per device.

v0:
```python
import jax
import jax.numpy as jnp
from jax import lax
from jax.sharding import PartitionSpec as P

SWEEPS = 4
REINIT = 2


weno_eps = 1e-06
advect_step = 0.15
reinit_step = 0.3


def with_halo(cells, sides, width):
    for axis, dim in sides:
        count = lax.axis_size(axis)
        head = lax.slice_in_dim(cells, 0, width, axis=dim)
        tail = lax.slice_in_dim(cells, cells.shape[dim] - width, cells.shape[dim], axis=dim)
        cells = jnp.concatenate(
            [
                lax.ppermute(tail, axis, [(i, (i + 1) % count) for i in range(count)]),
                cells,
                lax.ppermute(head, axis, [((i + 1) % count, i) for i in range(count)]),
            ],
            axis=dim,
        )
    return cells


def weno_blend(first, second, third, fourth, fifth):
    smooth_one = (
        13.0 / 12.0 * (first - 2.0 * second + third) ** 2
        + 0.25 * (first - 4.0 * second + 3.0 * third) ** 2
    )
    smooth_two = 13.0 / 12.0 * (second - 2.0 * third + fourth) ** 2 + 0.25 * (second - fourth) ** 2
    smooth_three = (
        13.0 / 12.0 * (third - 2.0 * fourth + fifth) ** 2
        + 0.25 * (3.0 * third - 4.0 * fourth + fifth) ** 2
    )
    alpha_one = 0.1 / (weno_eps + smooth_one) ** 2
    alpha_two = 0.6 / (weno_eps + smooth_two) ** 2
    alpha_three = 0.3 / (weno_eps + smooth_three) ** 2
    total = alpha_one + alpha_two + alpha_three
    blended = alpha_one * (first / 3.0 - 7.0 * second / 6.0 + 11.0 * third / 6.0)
    blended = blended + alpha_two * (-second / 6.0 + 5.0 * third / 6.0 + fourth / 3.0)
    blended = blended + alpha_three * (third / 3.0 + 5.0 * fourth / 6.0 - fifth / 6.0)
    return blended / total


def one_sided(shifted):
    diffs = [shifted[index + 1] - shifted[index] for index in range(6)]
    minus_side = weno_blend(diffs[0], diffs[1], diffs[2], diffs[3], diffs[4])
    plus_side = weno_blend(diffs[5], diffs[4], diffs[3], diffs[2], diffs[1])
    return (minus_side, plus_side)


def hamiltonian(padded, velocity):
    length = padded.shape[0]
    center = padded[3 : length - 3]
    along_x = [
        lax.slice_in_dim(padded, 3 + offset, length - 3 + offset, axis=0) for offset in range(-3, 4)
    ]
    walled = jnp.pad(center, ((0, 0), (3, 3), (0, 0)), mode="edge")
    width_y = center.shape[1]
    along_y = [
        lax.slice_in_dim(walled, 3 + offset, width_y + 3 + offset, axis=1)
        for offset in range(-3, 4)
    ]
    along_z = [jnp.roll(center, -offset, axis=2) for offset in range(-3, 4)]
    positive = velocity > 0.0
    total = jnp.zeros_like(center)
    for shifted in (along_x, along_y, along_z):
        minus_side, plus_side = one_sided(shifted)
        rising = jnp.maximum(jnp.maximum(minus_side, 0.0) ** 2, jnp.minimum(plus_side, 0.0) ** 2)
        falling = jnp.maximum(jnp.minimum(minus_side, 0.0) ** 2, jnp.maximum(plus_side, 0.0) ** 2)
        total = total + jnp.where(positive, rising, falling)
    return jnp.sqrt(total)


def neighbour_mean(padded_x, field):
    length = padded_x.shape[0]
    walled = jnp.pad(field, ((0, 0), (1, 1), (0, 0)), mode="edge")
    total = padded_x[2:] + padded_x[: length - 2]
    total = total + walled[:, 2:] + walled[:, :-2]
    total = total + jnp.roll(field, -1, axis=2) + jnp.roll(field, 1, axis=2)
    return total / 6.0


def per_device(level_set, sensitivity, band):
    weight = band.astype(jnp.float32)
    fixed = weight * sensitivity
    speed = fixed
    for sweep in range(SWEEPS):
        rimmed = with_halo(speed, (("gx", 0),), 1)
        speed = weight * fixed + (1.0 - weight) * neighbour_mean(rimmed, speed)

    def advect_rate(field):
        rimmed = with_halo(field, (("gx", 0),), 3)
        return -speed * hamiltonian(rimmed, speed)

    first = level_set + advect_step * advect_rate(level_set)
    second = 0.75 * level_set + 0.25 * (first + advect_step * advect_rate(first))
    advected = level_set / 3.0 + 2.0 / 3.0 * (second + advect_step * advect_rate(second))
    sign_field = advected / jnp.sqrt(advected * advected + 1.0)
    updated = advected
    for step in range(REINIT):
        rimmed = with_halo(updated, (("gx", 0),), 3)
        updated = updated - reinit_step * sign_field * (hamiltonian(rimmed, sign_field) - 1.0)
    return (speed, updated)


def solution(mesh):
    in_specs = (
        P(("cases", "gx"), None, None),
        P(("cases", "gx"), None, None),
        P(("cases", "gx"), None, None),
    )
    out_specs = (P(("cases", "gx"), None, None), P(("cases", "gx"), None, None))
    return jax.shard_map(
        per_device, mesh=mesh, in_specs=in_specs, out_specs=out_specs, check_vma=False
    )
```

profile of v0, /device:TPU:1, one launch (start us, length us, event | category | flops | bytes accessed | tf_op | source)
XLA Modules:
  0.0 225.3 jit_solution(14803274438447772750)
XLA Ops:
  0.6 1.8 convert_multiply_fusion.1
  2.6 2.6 %collective-permute-start.1 = (f32[1,256,256]{2,1,0:T(8,128)S(1)}, f32[1,256,256]{2,1,0:T(8,128)S(1)}, u32[]{:S(2)}, u32[]{:S(2)}) collective-permute-start(f32[1,256,256]{2,1,0:T(8,128)S(1)} %get-tuple-element.97), channel_id=1, source_target_pairs={{0,1},{1,2},{2,3},{3,4},{4,5},{5,6},{6,7},{7,8},{8,9},{9,10},{10,1... | collective-permute-start | bytes 786440 | tf_op jit(solution)/shard_map/ppermute | solution.py:22
  5.3 0.5 collective-permute-start.8
  5.8 2.4 %collective-permute-start.9 = (f32[3,256,256]{2,1,0:T(8,128)S(1)}, f32[3,256,256]{2,1,0:T(8,128)S(1)}, u32[]{:S(2)}, u32[]{:S(2)}) collective-permute-start(f32[3,256,256]{2,1,0:T(8,128)S(1)} %get-tuple-element.103), channel_id=1, source_target_pairs={{1,0},{2,1},{3,2},{4,3},{5,4},{6,5},{7,6},{8,7},{9,8},{10,9},{11,1... | collective-permute-start | bytes 2359304 | tf_op jit(solution)/shard_map/ppermute | solution.py:24
  8.3 0.2 fusion.431
  8.5 0.2 fusion.437
  8.7 0.2 fusion.439
  8.9 0.4 fusion.432
  9.2 0.4 fusion.438
  9.6 0.4 fusion.440
  10.0 0.4 fusion.442
  10.4 0.2 fusion.441
  10.6 11.9 %collective-permute-done.1 = f32[1,256,256]{2,1,0:T(8,128)S(1)} collective-permute-done((f32[1,256,256]{2,1,0:T(8,128)S(1)}, f32[1,256,256]{2,1,0:T(8,128)S(1)}, u32[]{:S(2)}, u32[]{:S(2)}) %collective-permute-start.1) | collective-permute-done | bytes 262176 | tf_op jit(solution)/shard_map/ppermute | solution.py:22
  22.5 0.7 fusion.93
  23.4 0.4 fusion.428
  23.8 2.5 %collective-permute-start.3 = (f32[1,256,256]{2,1,0:T(8,128)S(1)}, f32[1,256,256]{2,1,0:T(8,128)S(1)}, u32[]{:S(2)}, u32[]{:S(2)}) collective-permute-start(f32[1,256,256]{2,1,0:T(8,128)S(1)} %get-tuple-element.89), channel_id=1, source_target_pairs={{0,1},{1,2},{2,3},{3,4},{4,5},{5,6},{6,7},{7,8},{8,9},{9,10},{10,1... | collective-permute-start | bytes 786440 | tf_op jit(solution)/shard_map/ppermute | solution.py:22
  26.5 7.9 %collective-permute-done.2 = f32[1,256,256]{2,1,0:T(8,128)S(1)} collective-permute-done((f32[1,256,256]{2,1,0:T(8,128)S(1)}, f32[1,256,256]{2,1,0:T(8,128)S(1)}, u32[]{:S(2)}, u32[]{:S(2)}) %collective-permute-start.2) | collective-permute-done | bytes 262176 | tf_op jit(solution)/shard_map/ppermute | solution.py:24
  34.4 0.7 fusion.85
  35.3 0.4 fusion.424
  35.7 1.9 collective-permute-start.5
  37.8 3.8 %collective-permute-done.4 = f32[1,256,256]{2,1,0:T(8,128)S(1)} collective-permute-done((f32[1,256,256]{2,1,0:T(8,128)S(1)}, f32[1,256,256]{2,1,0:T(8,128)S(1)}, u32[]{:S(2)}, u32[]{:S(2)}) %collective-permute-start.4) | collective-permute-done | bytes 262176 | tf_op jit(solution)/shard_map/ppermute | solution.py:24
  41.5 0.7 fusion.77
  42.3 6.5 %collective-permute-start.6 = (f32[1,256,256]{2,1,0:T(8,128)S(1)}, f32[1,256,256]{2,1,0:T(8,128)S(1)}, u32[]{:S(2)}, u32[]{:S(2)}) collective-permute-start(f32[1,256,256]{2,1,0:T(8,128)S(1)} %get-tuple-element.68), channel_id=1, source_target_pairs={{1,0},{2,1},{3,2},{4,3},{5,4},{6,5},{7,6},{8,7},{9,8},{10,9},{11,1... | collective-permute-start | bytes 786440 | tf_op jit(solution)/shard_map/ppermute | solution.py:24
  48.8 0.2 fusion.422
  49.1 0.4 fusion.421
  49.7 0.3 collective-permute-done.6
  50.0 2.2 collective-permute-done.7
  52.2 19.6 %multiply_add_fusion.2 = (f32[4,256,256]{2,1,0:T(8,128)S(1)}, f32[4,256,256]{2,1,0:T(8,128)S(1)}) fusion(f32[4,256,256]{2,1,0:T(8,128)S(1)} %copy-done, f32[4,256,3]{2,1,0:T(8,128)S(1)} %get-tuple-element.115, f32[4,256,253]{2,1,0:T(8,128)S(1)} %get-tuple-element.117, f32[4,256,2]{2,1,0:T(8,128)S(1)} %get-tuple-element.107, ...), kind=kLoop, calls=%fused_computation.499 | loop fusion | flops 120586240 | bytes 21528576 | tf_op jit(solution)/shard_map/add | solution.py:102
  71.9 0.2 fusion.415
  72.1 0.2 fusion.417
  72.4 0.3 fusion.414
  72.8 2.5 %collective-permute-start.10 = (f32[3,256,256]{2,1,0:T(8,128)S(1)}, f32[3,256,256]{2,1,0:T(8,128)S(1)}, u32[]{:S(2)}, u32[]{:S(2)}) collective-permute-start(f32[3,256,256]{2,1,0:T(8,128)S(1)} %get-tuple-element.52), channel_id=1, source_target_pairs={{0,1},{1,2},{2,3},{3,4},{4,5},{5,6},{6,7},{7,8},{8,9},{9,10},{10,1... | collective-permute-start | bytes 2359304 | tf_op jit(solution)/shard_map/ppermute | solution.py:22
  75.3 3.0 %collective-permute-start.11 = (f32[3,256,256]{2,1,0:T(8,128)S(1)}, f32[3,256,256]{2,1,0:T(8,128)S(1)}, u32[]{:S(2)}, u32[]{:S(2)}) collective-permute-start(f32[3,256,256]{2,1,0:T(8,128)S(1)} %get-tuple-element.53), channel_id=1, source_target_pairs={{1,0},{2,1},{3,2},{4,3},{5,4},{6,5},{7,6},{8,7},{9,8},{10,9},{11,1... | collective-permute-start | bytes 2359304 | tf_op jit(solution)/shard_map/ppermute | solution.py:24
  78.5 0.4 fusion.418
  78.9 0.4 fusion.416
  79.2 12.4 %collective-permute-done.10 = f32[3,256,256]{2,1,0:T(8,128)S(1)} collective-permute-done((f32[3,256,256]{2,1,0:T(8,128)S(1)}, f32[3,256,256]{2,1,0:T(8,128)S(1)}, u32[]{:S(2)}, u32[]{:S(2)}) %collective-permute-start.10) | collective-permute-done | bytes 786464 | tf_op jit(solution)/shard_map/ppermute | solution.py:22
  91.6 3.5 %collective-permute-done.11 = f32[3,256,256]{2,1,0:T(8,128)S(1)} collective-permute-done((f32[3,256,256]{2,1,0:T(8,128)S(1)}, f32[3,256,256]{2,1,0:T(8,128)S(1)}, u32[]{:S(2)}, u32[]{:S(2)}) %collective-permute-start.11) | collective-permute-done | bytes 786464 | tf_op jit(solution)/shard_map/ppermute | solution.py:24
  95.2 18.3 %multiply_add_fusion.1 = f32[4,256,256]{2,1,0:T(8,128)S(1)} fusion(f32[4,256,256]{2,1,0:T(8,128)S(1)} %get-tuple-element.2, f32[4,256,3]{2,1,0:T(8,128)S(1)} %get-tuple-element.65, f32[4,256,253]{2,1,0:T(8,128)S(1)} %get-tuple-element.67, f32[4,256,2]{2,1,0:T(8,128)S(1)} %get-tuple-element.57, f32[4,256,254]{2,1,0:T(8,128)S(1)} %get-tuple-element.59, ...), kind=kLoop, calls=%fused_computation.428 | loop fusion | flops 118226944 | bytes 12083200 | tf_op jit(solution)/shard_map/add | solution.py:103
  113.5 0.2 fusion.407
  113.7 0.2 fusion.409
  114.0 0.3 fusion.406
  114.4 0.5 collective-permute-start.13
  115.1 0.4 fusion.410
  115.5 0.4 fusion.408
  115.8 13.2 %collective-permute-done.12 = f32[3,256,256]{2,1,0:T(8,128)S(1)} collective-permute-done((f32[3,256,256]{2,1,0:T(8,128)S(1)}, f32[3,256,256]{2,1,0:T(8,128)S(1)}, u32[]{:S(2)}, u32[]{:S(2)}) %collective-permute-start.12) | collective-permute-done | bytes 786464 | tf_op jit(solution)/shard_map/ppermute | solution.py:22
  129.0 4.3 %collective-permute-done.13 = f32[3,256,256]{2,1,0:T(8,128)S(1)} collective-permute-done((f32[3,256,256]{2,1,0:T(8,128)S(1)}, f32[3,256,256]{2,1,0:T(8,128)S(1)}, u32[]{:S(2)}, u32[]{:S(2)}) %collective-permute-start.13) | collective-permute-done | bytes 786464 | tf_op jit(solution)/shard_map/ppermute | solution.py:24
  133.4 18.3 %multiply_add_fusion = f32[4,256,256]{2,1,0:T(8,128)S(1)} fusion(f32[4,256,256]{2,1,0:T(8,128)S(1)} %multiply_add_fusion.1, f32[4,256,3]{2,1,0:T(8,128)S(1)} %get-tuple-element.49, f32[4,256,253]{2,1,0:T(8,128)S(1)} %get-tuple-element.51, f32[4,256,2]{2,1,0:T(8,128)S(1)} %get-tuple-element.41, f32[4,256,254]{2,1,0:T(8,128)S(1)} %get-tuple-element.43, ...), kind=kLoop, calls=%fused_computation.357 | loop fusion | flops 118226944 | bytes 12083200 | tf_op jit(solution)/shard_map/add | solution.py:104
  151.7 0.2 fusion.397
  151.9 0.2 fusion.401
  152.3 0.4 fusion.402
  152.7 0.5 collective-permute-start.15
  153.4 0.4 fusion.398
  153.8 0.4 fusion.400
  154.1 13.2 %collective-permute-done.14 = f32[3,256,256]{2,1,0:T(8,128)S(1)} collective-permute-done((f32[3,256,256]{2,1,0:T(8,128)S(1)}, f32[3,256,256]{2,1,0:T(8,128)S(1)}, u32[]{:S(2)}, u32[]{:S(2)}) %collective-permute-start.14) | collective-permute-done | bytes 786464 | tf_op jit(solution)/shard_map/ppermute | solution.py:22
  167.3 18.2 %multiply_subtract_fusion.1 = f32[4,256,256]{2,1,0:T(8,128)S(1)} fusion(f32[4,256,256]{2,1,0:T(8,128)S(1)} %multiply_add_fusion, f32[4,256,3]{2,1,0:T(8,128)S(1)} %get-tuple-element.33, f32[4,256,253]{2,1,0:T(8,128)S(1)} %get-tuple-element.35, f32[4,256,2]{2,1,0:T(8,128)S(1)} %get-tuple-element.25, f32[4,256,254]{2,1,0:T(8,128)S(1)} %get-tuple-element.27, ...), kind=kLoop, calls=%fused_computation.285 | loop fusion | flops 118226944 | bytes 9986048 | tf_op jit(solution)/shard_map/sub | solution.py:109
  185.5 0.2 fusion.391
  185.7 0.2 fusion.393
  186.1 0.4 fusion.390
  186.5 2.5 %collective-permute-start.16 = (f32[3,256,256]{2,1,0:T(8,128)S(1)}, f32[3,256,256]{2,1,0:T(8,128)S(1)}, u32[]{:S(2)}, u32[]{:S(2)}) collective-permute-start(f32[3,256,256]{2,1,0:T(8,128)S(1)} %get-tuple-element.4), channel_id=1, source_target_pairs={{0,1},{1,2},{2,3},{3,4},{4,5},{5,6},{6,7},{7,8},{8,9},{9,10},{10,1... | collective-permute-start | bytes 2359304 | tf_op jit(solution)/shard_map/ppermute | solution.py:22
  189.0 0.2 fusion.389
  189.2 0.4 fusion.394
  189.6 0.4 fusion.392
  189.9 16.4 %collective-permute-done.16 = f32[3,256,256]{2,1,0:T(8,128)S(1)} collective-permute-done((f32[3,256,256]{2,1,0:T(8,128)S(1)}, f32[3,256,256]{2,1,0:T(8,128)S(1)}, u32[]{:S(2)}, u32[]{:S(2)}) %collective-permute-start.16) | collective-permute-done | bytes 786464 | tf_op jit(solution)/shard_map/ppermute | solution.py:22
  206.4 18.9 %multiply_subtract_fusion = f32[4,256,256]{2,1,0:T(8,128)} fusion(f32[4,256,256]{2,1,0:T(8,128)S(1)} %multiply_subtract_fusion.1, f32[4,256,3]{2,1,0:T(8,128)S(1)} %get-tuple-element.17, f32[4,256,253]{2,1,0:T(8,128)S(1)} %get-tuple-element.19, f32[4,256,2]{2,1,0:T(8,128)S(1)} %get-tuple-element.9, f32[4,256,254]{2,1,0:T(8,128)S(1)} %get-tuple-element.11, ...), kind=kLoop, calls=%fused_computation.214 | loop fusion | flops 118226944 | bytes 11034624 | tf_op jit(solution)/shard_map/sub | solution.py:109
  (67 shorter events, 2.6 us)
Async XLA Ops:
  0.6 4.5 %copy-start = (f32[4,256,256]{2,1,0:T(8,128)S(1)}, f32[4,256,256]{2,1,0:T(8,128)}, u32[]{:S(2)}) copy-start(f32[4,256,256]{2,1,0:T(8,128)} %param.3) | copy-start | bytes 3145732
  2.5 8.1 %collective-permute-start = (f32[1,256,256]{2,1,0:T(8,128)S(1)}, f32[1,256,256]{2,1,0:T(8,128)S(1)}, u32[]{:S(2)}, u32[]{:S(2)}) collective-permute-start(f32[1,256,256]{2,1,0:T(8,128)S(1)} %get-tuple-element.96), channel_id=1, source_target_pairs={{1,0},{2,1},{3,2},{4,3},{5,4},{6,5},{7,6},{8,7},{9,8},{10,9},{11,1... | collective-permute-start | bytes 786440 | tf_op jit(solution)/shard_map/ppermute | solution.py:24
  2.6 20.0 %collective-permute-start.1 = (f32[1,256,256]{2,1,0:T(8,128)S(1)}, f32[1,256,256]{2,1,0:T(8,128)S(1)}, u32[]{:S(2)}, u32[]{:S(2)}) collective-permute-start(f32[1,256,256]{2,1,0:T(8,128)S(1)} %get-tuple-element.97), channel_id=1, source_target_pairs={{0,1},{1,2},{2,3},{3,4},{4,5},{5,6},{6,7},{7,8},{8,9},{9,10},{10,1... | collective-permute-start | bytes 786440 | tf_op jit(solution)/shard_map/ppermute | solution.py:22
  5.3 44.1 %collective-permute-start.8 = (f32[3,256,256]{2,1,0:T(8,128)S(1)}, f32[3,256,256]{2,1,0:T(8,128)S(1)}, u32[]{:S(2)}, u32[]{:S(2)}) collective-permute-start(f32[3,256,256]{2,1,0:T(8,128)S(1)} %get-tuple-element.102), channel_id=1, source_target_pairs={{0,1},{1,2},{2,3},{3,4},{4,5},{5,6},{6,7},{7,8},{8,9},{9,10},{10,1... | collective-permute-start | bytes 2359304 | tf_op jit(solution)/shard_map/ppermute | solution.py:22
  5.8 43.9 %collective-permute-start.9 = (f32[3,256,256]{2,1,0:T(8,128)S(1)}, f32[3,256,256]{2,1,0:T(8,128)S(1)}, u32[]{:S(2)}, u32[]{:S(2)}) collective-permute-start(f32[3,256,256]{2,1,0:T(8,128)S(1)} %get-tuple-element.103), channel_id=1, source_target_pairs={{1,0},{2,1},{3,2},{4,3},{5,4},{6,5},{7,6},{8,7},{9,8},{10,9},{11,1... | collective-permute-start | bytes 2359304 | tf_op jit(solution)/shard_map/ppermute | solution.py:24
  10.3 12.2 %copy-start.1 = (f32[4,256,256]{2,1,0:T(8,128)S(1)}, f32[4,256,256]{2,1,0:T(8,128)}, u32[]{:S(2)}) copy-start(f32[4,256,256]{2,1,0:T(8,128)} %param.4) | copy-start | bytes 3145732
  10.3 12.2 %copy-start.2 = (s32[4,256,256]{2,1,0:T(8,128)S(1)}, s32[4,256,256]{2,1,0:T(8,128)}, u32[]{:S(2)}) copy-start(s32[4,256,256]{2,1,0:T(8,128)} %param.5) | copy-start | bytes 3145732
  23.7 10.7 %collective-permute-start.2 = (f32[1,256,256]{2,1,0:T(8,128)S(1)}, f32[1,256,256]{2,1,0:T(8,128)S(1)}, u32[]{:S(2)}, u32[]{:S(2)}) collective-permute-start(f32[1,256,256]{2,1,0:T(8,128)S(1)} %get-tuple-element.88), channel_id=1, source_target_pairs={{1,0},{2,1},{3,2},{4,3},{5,4},{6,5},{7,6},{8,7},{9,8},{10,9},{11,1... | collective-permute-start | bytes 786440 | tf_op jit(solution)/shard_map/ppermute | solution.py:24
  23.8 10.7 %collective-permute-start.3 = (f32[1,256,256]{2,1,0:T(8,128)S(1)}, f32[1,256,256]{2,1,0:T(8,128)S(1)}, u32[]{:S(2)}, u32[]{:S(2)}) collective-permute-start(f32[1,256,256]{2,1,0:T(8,128)S(1)} %get-tuple-element.89), channel_id=1, source_target_pairs={{0,1},{1,2},{2,3},{3,4},{4,5},{5,6},{6,7},{7,8},{8,9},{9,10},{10,1... | collective-permute-start | bytes 786440 | tf_op jit(solution)/shard_map/ppermute | solution.py:22
  35.6 5.9 %collective-permute-start.4 = (f32[1,256,256]{2,1,0:T(8,128)S(1)}, f32[1,256,256]{2,1,0:T(8,128)S(1)}, u32[]{:S(2)}, u32[]{:S(2)}) collective-permute-start(f32[1,256,256]{2,1,0:T(8,128)S(1)} %get-tuple-element.80), channel_id=1, source_target_pairs={{1,0},{2,1},{3,2},{4,3},{5,4},{6,5},{7,6},{8,7},{9,8},{10,9},{11,1... | collective-permute-start | bytes 786440 | tf_op jit(solution)/shard_map/ppermute | solution.py:24
  35.7 5.9 %collective-permute-start.5 = (f32[1,256,256]{2,1,0:T(8,128)S(1)}, f32[1,256,256]{2,1,0:T(8,128)S(1)}, u32[]{:S(2)}, u32[]{:S(2)}) collective-permute-start(f32[1,256,256]{2,1,0:T(8,128)S(1)} %get-tuple-element.81), channel_id=1, source_target_pairs={{0,1},{1,2},{2,3},{3,4},{4,5},{5,6},{6,7},{7,8},{8,9},{9,10},{10,1... | collective-permute-start | bytes 786440 | tf_op jit(solution)/shard_map/ppermute | solution.py:22
  42.3 7.7 %collective-permute-start.6 = (f32[1,256,256]{2,1,0:T(8,128)S(1)}, f32[1,256,256]{2,1,0:T(8,128)S(1)}, u32[]{:S(2)}, u32[]{:S(2)}) collective-permute-start(f32[1,256,256]{2,1,0:T(8,128)S(1)} %get-tuple-element.68), channel_id=1, source_target_pairs={{1,0},{2,1},{3,2},{4,3},{5,4},{6,5},{7,6},{8,7},{9,8},{10,9},{11,1... | collective-permute-start | bytes 786440 | tf_op jit(solution)/shard_map/ppermute | solution.py:24
  48.8 3.3 %collective-permute-start.7 = (f32[1,256,256]{2,1,0:T(8,128)S(1)}, f32[1,256,256]{2,1,0:T(8,128)S(1)}, u32[]{:S(2)}, u32[]{:S(2)}) collective-permute-start(f32[1,256,256]{2,1,0:T(8,128)S(1)} %get-tuple-element.69), channel_id=1, source_target_pairs={{0,1},{1,2},{2,3},{3,4},{4,5},{5,6},{6,7},{7,8},{8,9},{9,10},{10,1... | collective-permute-start | bytes 786440 | tf_op jit(solution)/shard_map/ppermute | solution.py:22
  71.8 61.6 %copy-start.3 = (f32[4,256,256]{2,1,0:T(8,128)}, f32[4,256,256]{2,1,0:T(8,128)S(1)}, u32[]{:S(2)}) copy-start(f32[4,256,256]{2,1,0:T(8,128)S(1)} %get-tuple-element.3) | copy-start | bytes 3145732
  72.8 18.9 %collective-permute-start.10 = (f32[3,256,256]{2,1,0:T(8,128)S(1)}, f32[3,256,256]{2,1,0:T(8,128)S(1)}, u32[]{:S(2)}, u32[]{:S(2)}) collective-permute-start(f32[3,256,256]{2,1,0:T(8,128)S(1)} %get-tuple-element.52), channel_id=1, source_target_pairs={{0,1},{1,2},{2,3},{3,4},{4,5},{5,6},{6,7},{7,8},{8,9},{9,10},{10,1... | collective-permute-start | bytes 2359304 | tf_op jit(solution)/shard_map/ppermute | solution.py:22
  75.3 19.8 %collective-permute-start.11 = (f32[3,256,256]{2,1,0:T(8,128)S(1)}, f32[3,256,256]{2,1,0:T(8,128)S(1)}, u32[]{:S(2)}, u32[]{:S(2)}) collective-permute-start(f32[3,256,256]{2,1,0:T(8,128)S(1)} %get-tuple-element.53), channel_id=1, source_target_pairs={{1,0},{2,1},{3,2},{4,3},{5,4},{6,5},{7,6},{8,7},{9,8},{10,9},{11,1... | collective-permute-start | bytes 2359304 | tf_op jit(solution)/shard_map/ppermute | solution.py:24
  114.3 14.7 %collective-permute-start.12 = (f32[3,256,256]{2,1,0:T(8,128)S(1)}, f32[3,256,256]{2,1,0:T(8,128)S(1)}, u32[]{:S(2)}, u32[]{:S(2)}) collective-permute-start(f32[3,256,256]{2,1,0:T(8,128)S(1)} %get-tuple-element.36), channel_id=1, source_target_pairs={{0,1},{1,2},{2,3},{3,4},{4,5},{5,6},{6,7},{7,8},{8,9},{9,10},{10,1... | collective-permute-start | bytes 2359304 | tf_op jit(solution)/shard_map/ppermute | solution.py:22
  114.4 19.0 %collective-permute-start.13 = (f32[3,256,256]{2,1,0:T(8,128)S(1)}, f32[3,256,256]{2,1,0:T(8,128)S(1)}, u32[]{:S(2)}, u32[]{:S(2)}) collective-permute-start(f32[3,256,256]{2,1,0:T(8,128)S(1)} %get-tuple-element.37), channel_id=1, source_target_pairs={{1,0},{2,1},{3,2},{4,3},{5,4},{6,5},{7,6},{8,7},{9,8},{10,9},{11,1... | collective-permute-start | bytes 2359304 | tf_op jit(solution)/shard_map/ppermute | solution.py:24
  152.7 14.7 %collective-permute-start.14 = (f32[3,256,256]{2,1,0:T(8,128)S(1)}, f32[3,256,256]{2,1,0:T(8,128)S(1)}, u32[]{:S(2)}, u32[]{:S(2)}) collective-permute-start(f32[3,256,256]{2,1,0:T(8,128)S(1)} %get-tuple-element.20), channel_id=1, source_target_pairs={{0,1},{1,2},{2,3},{3,4},{4,5},{5,6},{6,7},{7,8},{8,9},{9,10},{10,1... | collective-permute-start | bytes 2359304 | tf_op jit(solution)/shard_map/ppermute | solution.py:22
  152.7 14.6 %collective-permute-start.15 = (f32[3,256,256]{2,1,0:T(8,128)S(1)}, f32[3,256,256]{2,1,0:T(8,128)S(1)}, u32[]{:S(2)}, u32[]{:S(2)}) collective-permute-start(f32[3,256,256]{2,1,0:T(8,128)S(1)} %get-tuple-element.21), channel_id=1, source_target_pairs={{1,0},{2,1},{3,2},{4,3},{5,4},{6,5},{7,6},{8,7},{9,8},{10,9},{11,1... | collective-permute-start | bytes 2359304 | tf_op jit(solution)/shard_map/ppermute | solution.py:24
  186.5 19.9 %collective-permute-start.16 = (f32[3,256,256]{2,1,0:T(8,128)S(1)}, f32[3,256,256]{2,1,0:T(8,128)S(1)}, u32[]{:S(2)}, u32[]{:S(2)}) collective-permute-start(f32[3,256,256]{2,1,0:T(8,128)S(1)} %get-tuple-element.4), channel_id=1, source_target_pairs={{0,1},{1,2},{2,3},{3,4},{4,5},{5,6},{6,7},{7,8},{8,9},{9,10},{10,1... | collective-permute-start | bytes 2359304 | tf_op jit(solution)/shard_map/ppermute | solution.py:22
  189.0 17.4 %collective-permute-start.17 = (f32[3,256,256]{2,1,0:T(8,128)S(1)}, f32[3,256,256]{2,1,0:T(8,128)S(1)}, u32[]{:S(2)}, u32[]{:S(2)}) collective-permute-start(f32[3,256,256]{2,1,0:T(8,128)S(1)} %get-tuple-element.5), channel_id=1, source_target_pairs={{1,0},{2,1},{3,2},{4,3},{5,4},{6,5},{7,6},{8,7},{9,8},{10,9},{11,1... | collective-permute-start | bytes 2359304 | tf_op jit(solution)/shard_map/ppermute | solution.py:24
where the time goes:
time: 227 us; the launch traced here: 225 us
  other arithmetic  97.3 us (43%)
  waiting for transfers between devices  89.2 us (39%)
  starting transfers between devices  25.8 us (11%)
  local copies, waits for them, and re-layouts  11.9 us (5%)
    ppermute x9, waiting for transfers between devices, with_halo(): lax.ppermute(tail, axis, [(i, (i + 1) % count) for i in range(count)])  69.3 us
    sub x2, other arithmetic, per_device(): updated - reinit_step * sign_field * (hamiltonian(rimmed, sign_field) - 1.0)  37.1 us
    ppermute x9, waiting for transfers between devices, with_halo(): lax.ppermute(head, axis, [((i + 1) % count, i) for i in range(count)])  19.9 us
    add x1, other arithmetic, per_device(): first = level_set + advect_step * advect_rate(level_set)  19.6 us
    add x1, other arithmetic, per_device(): level_set / 3.0 + 2.0 / 3.0 * (second + advect_step * advect_rate(second))  18.3 us
    add x1, other arithmetic, per_device(): 0.75 * level_set + 0.25 * (first + advect_step * advect_rate(first))  18.3 us
    ppermute x9, starting transfers between devices, with_halo(): lax.ppermute(head, axis, [((i + 1) % count, i) for i in range(count)])  13.2 us
    ppermute x9, starting transfers between devices, with_halo(): lax.ppermute(tail, axis, [(i, (i + 1) % count) for i in range(count)])  12.7 us
  transfers between devices with their start and end apart: 18, of which 11 were waited for; matrix products, arithmetic and copies ran while one was open for 5% of the time, Pallas kernels for 0%

commit v1 on v0

v1 whole, which is shorter than its diff:
```python
import functools

import jax
import jax.numpy as jnp
from jax import lax
from jax.experimental import pallas as pl
from jax.experimental.pallas import tpu as pltpu
from jax.sharding import PartitionSpec as P

SWEEPS = 4
REINIT = 2
SUB = 8
CHUNKS = 2

weno_eps = 1e-06
advect_step = 0.15
reinit_step = 0.3


def recip(value):
    return pl.reciprocal(value, approx=True)


def face_pair(d, q6, s4, a, b, c, r_here, r_next):
    ratio_a = b * recip(a)
    ratio_c = b * recip(c)
    gain_a = ratio_a * ratio_a
    gain_c = ratio_c * ratio_c
    part_a = gain_a * r_here
    part_c = gain_c * r_next
    half = 0.5 * (gain_a + gain_c) + 3.0
    mid = d + 0.5 * q6
    minus = (mid + s4) - (part_a + 1.5 * part_c) * recip(half + gain_c)
    negated_plus = (s4 - mid) - (1.5 * part_a + part_c) * recip(half + gain_a)
    return minus, negated_plus


def smoothness(x, y, x_square, y_square):
    cross = x * y
    base = (x_square + y_square) + 0.75 * weno_eps
    outer = base - 2.75 * cross
    return outer + 1.5 * y_square, base - 1.25 * cross, outer + 1.5 * x_square


def along_line(cells):
    count = len(cells) - 6
    d = [cells[i + 1] - cells[i] for i in range(count + 5)]
    e = [d[i + 1] - d[i] for i in range(count + 4)]
    squares = [v * v for v in e]
    triples = [smoothness(e[i], e[i + 1], squares[i], squares[i + 1]) for i in range(count + 3)]
    q6 = [(e[i + 1] - e[i]) * (1.0 / 6.0) for i in range(count + 3)]
    r6 = [q6[i + 1] - q6[i] for i in range(count + 2)]
    faces = []
    for k in range(count + 1):
        s4 = 0.25 * (e[k + 1] + e[k + 2])
        faces.append(
            face_pair(
                d[k + 2], q6[k + 1], s4, triples[k][0], triples[k + 1][1], triples[k + 2][2], r6[k], r6[k + 1]
            )
        )
    return [(faces[i][0], faces[i + 1][1]) for i in range(count)]


def along_lanes(cell):
    length = cell.shape[1]

    def back(v):
        return pltpu.roll(v, 1, 1)

    def ahead(v):
        return pltpu.roll(v, length - 1, 1)

    d = ahead(cell) - cell
    x = d - back(d)
    y = ahead(x)
    a, b, c = smoothness(x, y, x * x, y * y)
    q6 = (y - x) * (1.0 / 6.0)
    r6 = q6 - back(q6)
    minus, negated_plus = face_pair(d, q6, 0.25 * (x + y), back(a), b, ahead(c), r6, ahead(r6))
    return back(minus), negated_plus


def upwind(pair, positive):
    minus, negated_plus = pair
    rising = jnp.maximum(jnp.maximum(minus, negated_plus), 0.0)
    falling = jnp.minimum(jnp.minimum(minus, negated_plus), 0.0)
    chosen = jnp.where(positive, rising, falling)
    return chosen * chosen


def upwind_both(pair):
    minus, negated_plus = pair
    rising = jnp.maximum(jnp.maximum(minus, negated_plus), 0.0)
    falling = jnp.minimum(jnp.minimum(minus, negated_plus), 0.0)
    return rising * rising, falling * falling


def shift_rows(tile, down):
    rows = lax.broadcasted_iota(jnp.int32, tile.shape, 0)
    if down:
        return jnp.where(rows == 0, tile, pltpu.roll(tile, 1, 0))
    return jnp.where(rows == SUB - 1, tile, pltpu.roll(tile, SUB - 1, 0))


def edge_tile(wrapped, nearest_row_tile, low):
    rows = lax.broadcasted_iota(jnp.int32, wrapped.shape, 0)
    if low:
        return jnp.where(rows == 0, nearest_row_tile, pltpu.roll(wrapped, 1, 0))
    return jnp.where(rows == SUB - 1, nearest_row_tile, pltpu.roll(wrapped, SUB - 1, 0))


def local_body(chunks, both, block, *refs):
    u_refs = refs[:chunks]
    if both:
        rise_ref, fall_ref, padded = refs[chunks:]
    else:
        vel_ref, out_ref, padded = refs[chunks:]
    tiles = padded.shape[0] - 6
    per = tiles // chunks
    for index in range(chunks):
        padded[3 + index * per : 3 + (index + 1) * per] = u_refs[index][0]
    first = padded[3]
    final = padded[tiles + 2]
    for step in range(3):
        padded[step] = edge_tile(padded[tiles + step], first, True)
        padded[tiles + 3 + step] = edge_tile(padded[3 + step], final, False)

    def loop(number, carry):
        start = number * block
        cells = [padded[start + i] for i in range(block + 6)]
        pairs = along_line(cells)
        for i in range(block):
            lanes = along_lanes(cells[i + 3])
            if both:
                rise_y, fall_y = upwind_both(pairs[i])
                rise_z, fall_z = upwind_both(lanes)
                rise_ref[0, start + i] = rise_y + rise_z
                fall_ref[0, start + i] = fall_y + fall_z
            else:
                positive = vel_ref[0, start + i] > 0.0
                out_ref[0, start + i] = upwind(pairs[i], positive) + upwind(lanes, positive)
        return carry

    lax.fori_loop(0, tiles // block, loop, 0)


def local_part(pieces, velocity, block=4):
    layers, per, _, lanes = pieces[0].shape
    tiles = per * len(pieces)
    both = velocity is None
    whole = pl.BlockSpec((1, tiles, SUB, lanes), lambda i: (i, 0, 0, 0))
    piece = pl.BlockSpec((1, per, SUB, lanes), lambda i: (i, 0, 0, 0))
    shape = jax.ShapeDtypeStruct((layers, tiles, SUB, lanes), jnp.float32)
    cells = layers * tiles * SUB * lanes
    return pl.pallas_call(
        functools.partial(local_body, len(pieces), both, block),
        grid=(layers,),
        in_specs=[piece] * len(pieces) + ([] if both else [whole]),
        out_specs=(whole, whole) if both else whole,
        out_shape=(shape, shape) if both else shape,
        scratch_shapes=[pltpu.VMEM((tiles + 6, SUB, lanes), jnp.float32)],
        compiler_params=pltpu.CompilerParams(vmem_limit_bytes=24 * 1024 * 1024),
        cost_estimate=pl.CostEstimate(flops=130 * cells, bytes_accessed=12 * cells, transcendentals=8 * cells),
        name="local_part",
    )(*pieces, *(() if both else (velocity,)))


def finish_body(kind, last, *refs):
    u_ref, left_ref, right_ref = refs[:3]
    rest = list(refs[3:])
    layers, tiles = u_ref.shape[0], u_ref.shape[1]
    if kind == "first":
        rise_ref, fall_ref, vel_ref = rest[:3]
        rest = rest[3:]
    else:
        local_ref, vel_ref = rest[:2]
        rest = rest[2:]
        if kind in ("second", "third"):
            base_ref = rest.pop(0)
    out_ref = rest[0]

    def loop(t, carry):
        own = [u_ref[i, t] for i in range(layers)]
        cells = [left_ref[i, t] for i in range(3)] + own + [right_ref[i, t] for i in range(3)]
        pairs = along_line(cells)
        for i in range(layers):
            vel = vel_ref[i, t]
            positive = vel > 0.0
            total = upwind(pairs[i], positive)
            if kind == "first":
                total = total + jnp.where(positive, rise_ref[i, t], fall_ref[i, t])
            else:
                total = total + local_ref[i, t]
            height = jnp.sqrt(total)
            if kind == "first":
                new = own[i] - advect_step * (vel * height)
            elif kind == "second":
                new = 0.75 * base_ref[i, t] + 0.25 * (own[i] - advect_step * (vel * height))
            elif kind == "third":
                new = base_ref[i, t] * (1.0 / 3.0) + (2.0 / 3.0) * (own[i] - advect_step * (vel * height))
            else:
                sign = vel * lax.rsqrt(vel * vel + 1.0)
                new = own[i] - reinit_step * (sign * (height - 1.0))
            out_ref[i, t] = new
            if not last:
                if i < 3:
                    rest[1][i, t] = new
                if i >= layers - 3:
                    rest[2][i - (layers - 3), t] = new
        return carry

    lax.fori_loop(0, tiles, loop, 0)


def finish_part(kind, last, index, u, left, right, others, block=4):
    layers, per, _, lanes = u.shape
    block = min(block, per)
    shift = index * (per // block)
    own = pl.BlockSpec((layers, block, SUB, lanes), lambda i: (0, i, 0, 0))
    side = pl.BlockSpec((3, block, SUB, lanes), lambda i: (0, i, 0, 0))
    moved = pl.BlockSpec((layers, block, SUB, lanes), lambda i: (0, i + shift, 0, 0))
    shape = jax.ShapeDtypeStruct(u.shape, jnp.float32)
    side_shape = jax.ShapeDtypeStruct((3, per, SUB, lanes), jnp.float32)
    specs = [moved if other.shape[1] != per else own for other in others]
    cells = layers * per * SUB * lanes
    return pl.pallas_call(
        functools.partial(finish_body, kind, last),
        grid=(per // block,),
        in_specs=[own, side, side] + specs,
        out_specs=own if last else (own, side, side),
        out_shape=shape if last else (shape, side_shape, side_shape),
        compiler_params=pltpu.CompilerParams(vmem_limit_bytes=24 * 1024 * 1024),
        cost_estimate=pl.CostEstimate(flops=80 * cells, bytes_accessed=32 * cells, transcendentals=6 * cells),
        name="finish_part",
    )(u, left, right, *others)


def sweep_body(low_ref, mid_ref, high_ref, weight_ref, fixed_ref, low_out, mid_out, high_out):
    tiles, lanes = low_ref.shape[1], low_ref.shape[3]
    layers = mid_ref.shape[0] + 2

    def at(i, t):
        if i == 0:
            return low_ref[0, t]
        if i == layers - 1:
            return high_ref[0, t]
        return mid_ref[i - 1, t]

    def one(i, t, cell, before, after):
        total = before + after + pltpu.roll(cell, lanes - 1, 1) + pltpu.roll(cell, 1, 1)
        if i > 0:
            total = total + at(i - 1, t)
        if i < layers - 1:
            total = total + at(i + 1, t)
        weight = weight_ref[i, t]
        new = weight * fixed_ref[i, t] + (1.0 - weight) * (total * (1.0 / 6.0))
        if i == 0:
            low_out[0, t] = new
        elif i == layers - 1:
            high_out[0, t] = new
        else:
            mid_out[i - 1, t] = new

    for i in range(layers):
        first, final = at(i, 0), at(i, tiles - 1)
        one(i, 0, first, edge_tile(final, first, True), at(i, 1))
        one(i, tiles - 1, final, at(i, tiles - 2), edge_tile(first, final, False))

    def loop(t, carry):
        for i in range(layers):
            one(i, t, at(i, t), at(i, t - 1), at(i, t + 1))
        return carry

    lax.fori_loop(1, tiles - 1, loop, 0)


def sweep_part(low, mid, high, weight, fixed):
    cells = weight.size
    shapes = [jax.ShapeDtypeStruct(v.shape, jnp.float32) for v in (low, mid, high)]
    vmem = pl.BlockSpec(memory_space=pltpu.VMEM)
    return pl.pallas_call(
        sweep_body,
        in_specs=[vmem] * 5,
        out_specs=(vmem, vmem, vmem),
        out_shape=tuple(shapes),
        compiler_params=pltpu.CompilerParams(vmem_limit_bytes=24 * 1024 * 1024),
        cost_estimate=pl.CostEstimate(flops=12 * cells, bytes_accessed=16 * cells, transcendentals=0),
        name="sweep_part",
    )(low, mid, high, weight, fixed)


def fold_rows(array):
    layers, rows, lanes = array.shape
    return array.reshape(layers, SUB, rows // SUB, lanes).transpose(0, 2, 1, 3)


def unfold_rows(array):
    layers, tiles, _, lanes = array.shape
    return array.transpose(0, 2, 1, 3).reshape(layers, tiles * SUB, lanes)


def to_next(array):
    count = lax.axis_size("gx")
    return lax.ppermute(array, "gx", [(i, (i + 1) % count) for i in range(count)])


def to_previous(array):
    count = lax.axis_size("gx")
    return lax.ppermute(array, "gx", [((i + 1) % count, i) for i in range(count)])


def per_device(level_set, sensitivity, band):
    layers = level_set.shape[0]
    weight = fold_rows(band).astype(jnp.float32)
    fixed = weight * fold_rows(sensitivity)
    level = fold_rows(level_set)
    per = level.shape[1] // CHUNKS
    pieces = [level[:, i * per : (i + 1) * per] for i in range(CHUNKS)]
    heads = [piece[:3] for piece in pieces]
    tails = [piece[layers - 3 :] for piece in pieces]

    low, mid, high = fixed[:1], fixed[1 : layers - 1], fixed[layers - 1 :]
    low_open = (1.0 - weight[:1]) * (1.0 / 6.0)
    high_open = (1.0 - weight[layers - 1 :]) * (1.0 / 6.0)
    for sweep in range(SWEEPS):
        from_previous = to_next(high)
        from_next = to_previous(low)
        if sweep == 0:
            halos = [(to_next(tails[i]), to_previous(heads[i])) for i in range(CHUNKS)]
        low_part, mid, high_part = sweep_part(low, mid, high, weight, fixed)
        low = low_part + low_open * from_previous
        high = high_part + high_open * from_next
    speed = jnp.concatenate([low, mid, high], axis=0)

    rise, fall = local_part([level], None)
    kinds = ["first", "second", "third"] + ["reinit"] * REINIT
    base = level
    marker = None
    for number, kind in enumerate(kinds):
        last = number == len(kinds) - 1
        if number > 0:
            halos = [(to_next(tails[i]), to_previous(heads[i])) for i in range(CHUNKS)]
            if kind == "reinit" and marker is None:
                marker = pieces
            if kind == "reinit":
                local = local_part(pieces, jnp.concatenate(marker, axis=1) if CHUNKS > 1 else marker[0])
            else:
                local = local_part(pieces, speed)
        results = []
        for i in range(CHUNKS):
            if kind == "first":
                others = (rise, fall, speed)
            elif kind == "reinit":
                others = (local, marker[i])
            else:
                others = (local, speed, level)
            results.append(finish_part(kind, last, i, pieces[i], halos[i][0], halos[i][1], others))
        if last:
            pieces = results
        else:
            pieces = [r[0] for r in results]
            heads = [r[1] for r in results]
            tails = [r[2] for r in results]
    updated = jnp.concatenate(pieces, axis=1) if CHUNKS > 1 else pieces[0]
    return (unfold_rows(speed), unfold_rows(updated))


def solution(mesh):
    spec = P(("cases", "gx"), None, None)
    return jax.shard_map(
        per_device, mesh=mesh, in_specs=(spec, spec, spec), out_specs=(spec, spec), check_vma=False
    )
```

time: 227 us -> 174 us (0.77)
  the two profiles are of different devices: /device:TPU:1 before, /device:TPU:0 now
where the time goes in v1:
time: 174 us
  Pallas kernels  104 us (60%)
  starting transfers between devices  56.1 us (32%)
  waiting for transfers between devices  5.44 us (3%)
  local copies, waits for them, and re-layouts  4.31 us (2%)
  other arithmetic  3.23 us (2%)
    pallas_call x5, Pallas kernels, local_part(): pl.pallas_call(functools.partial(local_body, len(pieces), both, block), g...  71 us
    ppermute x14, starting transfers between devices, to_previous(): lax.ppermute(array, 'gx', [((i + 1) % count, i) for i in range(count)])  47.4 us
    pallas_call x10, Pallas kernels, finish_part(): pl.pallas_call(functools.partial(finish_body, kind, last), grid=(per // b...  21.1 us
    pallas_call x4, Pallas kernels, sweep_part(): pl.pallas_call(sweep_body, in_specs=[vmem] * 5, out_specs=(vmem, vmem, vm...  11.4 us
    ppermute x14, starting transfers between devices, to_next(): lax.ppermute(array, 'gx', [(i, (i + 1) % count) for i in range(count)])  8.69 us
    ppermute x14, waiting for transfers between devices, to_next(): lax.ppermute(array, 'gx', [(i, (i + 1) % count) for i in range(count)])  5.41 us
  transfers between devices with their start and end apart: 28, of which 4 were waited for; matrix products, arithmetic and copies ran while one was open for 2% of the time, Pallas kernels for 58%

profile of v1, /device:TPU:0, one launch (start us, length us, event | category | flops | bytes accessed | tf_op | source)
XLA Modules:
  0.0 173.6 jit_solution(18151535637835124295)
XLA Ops:
  0.6 1.4 convert_element_type.7
  2.0 0.1 copy-done
  2.2 1.2 bitcast_multiply_fusion.fixed_ref
  3.4 0.5 collective-permute-start
  3.9 5.0 %collective-permute-start.1 = (f32[1,32,8,256]{3,2,1,0:T(8,128)S(1)}, f32[1,32,8,256]{3,2,1,0:T(8,128)S(1)}, u32[]{:S(2)}, u32[]{:S(2)}) collective-permute-start(f32[1,32,8,256]{3,2,1,0:T(8,128)S(1)} %get-tuple-element.95.low_ref), channel_id=1, source_target_pairs={{1,0},{2,1},{3,2},{4,3},{5,4},{6,5},{7,6},{8,7},{9,8},{10,9},{11,1... | collective-permute-start | bytes 786440 | tf_op jit(solution)/shard_map/ppermute | solution.py:309
  8.9 0.6 copy.16
  9.6 2.9 %sweep_part.4 = (f32[1,32,8,256]{3,2,1,0:T(8,128)S(1)}, f32[2,32,8,256]{3,2,1,0:T(8,128)S(1)}, f32[1,32,8,256]{3,2,1,0:T(8,128)S(1)}) custom-call(f32[1,32,8,256]{3,2,1,0:T(8,128)S(1)} %get-tuple-element.95.low_ref, f32[2,32,8,256]{3,2,1,0:T(8,128)S(1)} %slice.49.mid_ref, f32[1,32,8,256]{3,2,1,0:T(8,128)S(1)} %get-tuple-element.94.high_ref, ...), custom_call_target="tpu_custom_call" | custom-call | flops 3145728 | bytes 4194304 | tf_op jit(solution)/shard_map/sweep_part/pallas_call | solution.py:281
  12.4 0.6 collective-permute-done
  13.0 0.1 multiply_add_fusion.6
  13.1 2.1 %collective-permute-start.2 = (f32[1,32,8,256]{3,2,1,0:T(8,128)S(1)}, f32[1,32,8,256]{3,2,1,0:T(8,128)S(1)}, u32[]{:S(2)}, u32[]{:S(2)}) collective-permute-start(f32[1,32,8,256]{3,2,1,0:T(8,128)S(1)} %get-tuple-element.92.high_ref), channel_id=1, source_target_pairs={{0,1},{1,2},{2,3},{3,4},{4,5},{5,6},{6,7},{7,8},{8,9},{9,10},{10,1... | collective-permute-start | bytes 786440 | tf_op jit(solution)/shard_map/ppermute | solution.py:304
  15.3 2.4 %collective-permute-start.3 = (f32[1,32,8,256]{3,2,1,0:T(8,128)S(1)}, f32[1,32,8,256]{3,2,1,0:T(8,128)S(1)}, u32[]{:S(2)}, u32[]{:S(2)}) collective-permute-start(f32[1,32,8,256]{3,2,1,0:T(8,128)S(1)} %get-tuple-element.93.low_ref), channel_id=1, source_target_pairs={{1,0},{2,1},{3,2},{4,3},{5,4},{6,5},{7,6},{8,7},{9,8},{10,9},{11,1... | collective-permute-start | bytes 786440 | tf_op jit(solution)/shard_map/ppermute | solution.py:309
  17.7 0.6 copy.15
  18.3 2.9 %sweep_part.5 = (f32[1,32,8,256]{3,2,1,0:T(8,128)S(1)}, f32[2,32,8,256]{3,2,1,0:T(8,128)S(1)}, f32[1,32,8,256]{3,2,1,0:T(8,128)S(1)}) custom-call(f32[1,32,8,256]{3,2,1,0:T(8,128)S(1)} %get-tuple-element.93.low_ref, f32[2,32,8,256]{3,2,1,0:T(8,128)S(1)} %get-tuple-element.41.mid_ref, f32[1,32,8,256]{3,2,1,0:T(8,128)S(1)} %get-tuple-element.92.high_ref, ...), custom_call_target="tpu_custom_call" | custom-call | flops 3145728 | bytes 4194304 | tf_op jit(solution)/shard_map/sweep_part/pallas_call | solution.py:281
  21.1 0.6 collective-permute-done.2
  21.8 0.1 multiply_add_fusion.4
  21.9 2.2 %collective-permute-start.4 = (f32[1,32,8,256]{3,2,1,0:T(8,128)S(1)}, f32[1,32,8,256]{3,2,1,0:T(8,128)S(1)}, u32[]{:S(2)}, u32[]{:S(2)}) collective-permute-start(f32[1,32,8,256]{3,2,1,0:T(8,128)S(1)} %get-tuple-element.90.high_ref), channel_id=1, source_target_pairs={{0,1},{1,2},{2,3},{3,4},{4,5},{5,6},{6,7},{7,8},{8,9},{9,10},{10,1... | collective-permute-start | bytes 786440 | tf_op jit(solution)/shard_map/ppermute | solution.py:304
  24.1 2.3 %collective-permute-start.5 = (f32[1,32,8,256]{3,2,1,0:T(8,128)S(1)}, f32[1,32,8,256]{3,2,1,0:T(8,128)S(1)}, u32[]{:S(2)}, u32[]{:S(2)}) collective-permute-start(f32[1,32,8,256]{3,2,1,0:T(8,128)S(1)} %get-tuple-element.91.low_ref), channel_id=1, source_target_pairs={{1,0},{2,1},{3,2},{4,3},{5,4},{6,5},{7,6},{8,7},{9,8},{10,9},{11,1... | collective-permute-start | bytes 786440 | tf_op jit(solution)/shard_map/ppermute | solution.py:309
  26.4 0.1 fusion.3
  26.5 0.5 collective-permute-start.9
  27.0 0.1 collective-permute-start.13
  27.1 0.4 collective-permute-start.12
  27.6 14.2 %local_part.5 = (f32[4,32,8,256]{3,2,1,0:T(8,128)S(1)}, f32[4,32,8,256]{3,2,1,0:T(8,128)S(1)}) custom-call(f32[4,32,8,256]{3,2,1,0:T(8,128)S(1)} %bitcast.20), custom_call_target="tpu_custom_call" | custom-call | flops 34078720 | bytes 3145728 | tf_op jit(solution)/shard_map/local_part/pallas_call | solution.py:155
  41.8 2.9 %sweep_part.6 = (f32[1,32,8,256]{3,2,1,0:T(8,128)S(1)}, f32[2,32,8,256]{3,2,1,0:T(8,128)S(1)}, f32[1,32,8,256]{3,2,1,0:T(8,128)S(1)}) custom-call(f32[1,32,8,256]{3,2,1,0:T(8,128)S(1)} %get-tuple-element.91.low_ref, f32[2,32,8,256]{3,2,1,0:T(8,128)S(1)} %get-tuple-element.44.mid_ref, f32[1,32,8,256]{3,2,1,0:T(8,128)S(1)} %get-tuple-element.90.high_ref, ...), custom_call_target="tpu_custom_call" | custom-call | flops 3145728 | bytes 4194304 | tf_op jit(solution)/shard_map/sweep_part/pallas_call | solution.py:281
  44.7 0.1 multiply_add_fusion.2
  44.8 1.4 collective-permute-start.6
  46.1 3.1 %collective-permute-start.7 = (f32[1,32,8,256]{3,2,1,0:T(8,128)S(1)}, f32[1,32,8,256]{3,2,1,0:T(8,128)S(1)}, u32[]{:S(2)}, u32[]{:S(2)}) collective-permute-start(f32[1,32,8,256]{3,2,1,0:T(8,128)S(1)} %get-tuple-element.89.low_ref), channel_id=1, source_target_pairs={{1,0},{2,1},{3,2},{4,3},{5,4},{6,5},{7,6},{8,7},{9,8},{10,9},{11,1... | collective-permute-start | bytes 786440 | tf_op jit(solution)/shard_map/ppermute | solution.py:309
  49.3 0.1 fusion.4
  49.4 2.9 %sweep_part.7 = (f32[1,32,8,256]{3,2,1,0:T(8,128)S(1)}, f32[2,32,8,256]{3,2,1,0:T(8,128)S(1)}, f32[1,32,8,256]{3,2,1,0:T(8,128)S(1)}) custom-call(f32[1,32,8,256]{3,2,1,0:T(8,128)S(1)} %get-tuple-element.89.low_ref, f32[2,32,8,256]{3,2,1,0:T(8,128)S(1)} %get-tuple-element.47.mid_ref, f32[1,32,8,256]{3,2,1,0:T(8,128)S(1)} %get-tuple-element.88.high_ref, ...), custom_call_target="tpu_custom_call" | custom-call | flops 3145728 | bytes 4194304 | tf_op jit(solution)/shard_map/sweep_part/pallas_call | solution.py:281
  52.2 1.2 collective-permute-done.6
  53.4 0.1 multiply_add_fusion.1
  53.6 0.2 pad_maximum_fusion
  53.8 2.2 %finish_part.11 = (f32[4,16,8,256]{3,2,1,0:T(8,128)S(1)}, f32[3,16,8,256]{3,2,1,0:T(8,128)S(1)}, f32[3,16,8,256]{3,2,1,0:T(8,128)S(1)}) custom-call(f32[4,16,8,256]{3,2,1,0:T(8,128)S(1)} %get-tuple-element.83.refs_0_, f32[3,16,8,256]{3,2,1,0:T(8,128)S(1)} %collective-permute-done.12.refs_1_, f32[3,16,8,256]{3,2,1,0:T(8,128)S(1)} %collective-permute-done.13.refs_2_, ...), custom_call_target="tpu_custom_call" | custom-call | flops 10485760 | bytes 4194304 | tf_op jit(solution)/shard_map/finish_part/pallas_call | solution.py:226
  55.9 1.4 collective-permute-start.16
  57.3 3.1 %collective-permute-start.17 = (f32[3,16,8,256]{3,2,1,0:T(8,128)S(1)}, f32[3,16,8,256]{3,2,1,0:T(8,128)S(1)}, u32[]{:S(2)}, u32[]{:S(2)}) collective-permute-start(f32[3,16,8,256]{3,2,1,0:T(8,128)S(1)} %get-tuple-element.62), channel_id=1, source_target_pairs={{1,0},{2,1},{3,2},{4,3},{5,4},{6,5},{7,6},{8,7},{9,8},{10,9},{11,1... | collective-permute-start | bytes 1179656 | tf_op jit(solution)/shard_map/ppermute | solution.py:309
  60.5 2.9 %collective-permute-done.8.refs_1_ = f32[3,16,8,256]{3,2,1,0:T(8,128)S(1)} collective-permute-done((f32[3,16,8,256]{3,2,1,0:T(8,128)S(1)}, f32[3,16,8,256]{3,2,1,0:T(8,128)S(1)}, u32[]{:S(2)}, u32[]{:S(2)}) %collective-permute-start.8) | collective-permute-done | bytes 393248 | tf_op jit(solution)/shard_map/ppermute | solution.py:304
  63.4 2.1 %finish_part.10 = (f32[4,16,8,256]{3,2,1,0:T(8,128)S(1)}, f32[3,16,8,256]{3,2,1,0:T(8,128)S(1)}, f32[3,16,8,256]{3,2,1,0:T(8,128)S(1)}) custom-call(f32[4,16,8,256]{3,2,1,0:T(8,128)S(1)} %get-tuple-element.82.refs_0_, f32[3,16,8,256]{3,2,1,0:T(8,128)S(1)} %collective-permute-done.8.refs_1_, f32[3,16,8,256]{3,2,1,0:T(8,128)S(1)} %collective-permute-done.9.refs_2_, ...), custom_call_target="tpu_custom_call" | custom-call | flops 10485760 | bytes 4194304 | tf_op jit(solution)/shard_map/finish_part/pallas_call | solution.py:226
  65.6 0.3 collective-permute-start.10
  65.9 4.2 %collective-permute-start.11 = (f32[3,16,8,256]{3,2,1,0:T(8,128)S(1)}, f32[3,16,8,256]{3,2,1,0:T(8,128)S(1)}, u32[]{:S(2)}, u32[]{:S(2)}) collective-permute-start(f32[3,16,8,256]{3,2,1,0:T(8,128)S(1)} %get-tuple-element.56), channel_id=1, source_target_pairs={{1,0},{2,1},{3,2},{4,3},{5,4},{6,5},{7,6},{8,7},{9,8},{10,9},{11,1... | collective-permute-start | bytes 1179656 | tf_op jit(solution)/shard_map/ppermute | solution.py:309
  70.1 14.2 %local_part.6.refs_3_ = f32[4,32,8,256]{3,2,1,0:T(8,128)S(1)} custom-call(f32[4,16,8,256]{3,2,1,0:T(8,128)S(1)} %get-tuple-element.54.refs_0_, f32[4,16,8,256]{3,2,1,0:T(8,128)S(1)} %get-tuple-element.57.refs_1_.refs_0_, f32[4,32,8,256]{3,2,1,0:T(8,128)S(1)} %get-tuple-element.84.refs_5_.refs_2_.refs_4_), custom_call_target="tpu_custom_call" | custom-call | flops 34078720 | bytes 3145728 | tf_op jit(solution)/shard_map/local_part/pallas_call | solution.py:155
  84.3 2.2 %finish_part.13 = (f32[4,16,8,256]{3,2,1,0:T(8,128)S(1)}, f32[3,16,8,256]{3,2,1,0:T(8,128)S(1)}, f32[3,16,8,256]{3,2,1,0:T(8,128)S(1)}) custom-call(f32[4,16,8,256]{3,2,1,0:T(8,128)S(1)} %get-tuple-element.57.refs_1_.refs_0_, f32[3,16,8,256]{3,2,1,0:T(8,128)S(1)} %collective-permute-done.16.refs_1_, f32[3,16,8,256]{3,2,1,0:T(8,128)S(1)} %collective-permute-done.17.refs_2_, ...), custom_call_target="tpu_custom_call" | custom-call | flops 10485760 | bytes 4194304 | tf_op jit(solution)/shard_map/finish_part/pallas_call | solution.py:226
  86.5 0.1 collective-permute-start.20
  86.5 4.4 %collective-permute-start.21 = (f32[3,16,8,256]{3,2,1,0:T(8,128)S(1)}, f32[3,16,8,256]{3,2,1,0:T(8,128)S(1)}, u32[]{:S(2)}, u32[]{:S(2)}) collective-permute-start(f32[3,16,8,256]{3,2,1,0:T(8,128)S(1)} %get-tuple-element.68), channel_id=1, source_target_pairs={{1,0},{2,1},{3,2},{4,3},{5,4},{6,5},{7,6},{8,7},{9,8},{10,9},{11,1... | collective-permute-start | bytes 1179656 | tf_op jit(solution)/shard_map/ppermute | solution.py:309
  91.0 2.1 %finish_part.12 = (f32[4,16,8,256]{3,2,1,0:T(8,128)S(1)}, f32[3,16,8,256]{3,2,1,0:T(8,128)S(1)}, f32[3,16,8,256]{3,2,1,0:T(8,128)S(1)}) custom-call(f32[4,16,8,256]{3,2,1,0:T(8,128)S(1)} %get-tuple-element.54.refs_0_, f32[3,16,8,256]{3,2,1,0:T(8,128)S(1)} %collective-permute-done.10.refs_1_, f32[3,16,8,256]{3,2,1,0:T(8,128)S(1)} %collective-permute-done.11.refs_2_, ...), custom_call_target="tpu_custom_call" | custom-call | flops 10485760 | bytes 4194304 | tf_op jit(solution)/shard_map/finish_part/pallas_call | solution.py:226
  93.1 0.1 collective-permute-start.14
  93.2 4.4 %collective-permute-start.15 = (f32[3,16,8,256]{3,2,1,0:T(8,128)S(1)}, f32[3,16,8,256]{3,2,1,0:T(8,128)S(1)}, u32[]{:S(2)}, u32[]{:S(2)}) collective-permute-start(f32[3,16,8,256]{3,2,1,0:T(8,128)S(1)} %get-tuple-element.60), channel_id=1, source_target_pairs={{1,0},{2,1},{3,2},{4,3},{5,4},{6,5},{7,6},{8,7},{9,8},{10,9},{11,1... | collective-permute-start | bytes 1179656 | tf_op jit(solution)/shard_map/ppermute | solution.py:309
  97.6 14.2 %local_part.7.refs_3_ = f32[4,32,8,256]{3,2,1,0:T(8,128)S(1)} custom-call(f32[4,16,8,256]{3,2,1,0:T(8,128)S(1)} %get-tuple-element.58.refs_0_, f32[4,16,8,256]{3,2,1,0:T(8,128)S(1)} %get-tuple-element.63.refs_1_.refs_0_, f32[4,32,8,256]{3,2,1,0:T(8,128)S(1)} %get-tuple-element.84.refs_5_.refs_2_.refs_4_), custom_call_target="tpu_custom_call" | custom-call | flops 34078720 | bytes 3145728 | tf_op jit(solution)/shard_map/local_part/pallas_call | solution.py:155
  111.8 2.2 %finish_part.15 = (f32[4,16,8,256]{3,2,1,0:T(8,128)S(1)}, f32[3,16,8,256]{3,2,1,0:T(8,128)S(1)}, f32[3,16,8,256]{3,2,1,0:T(8,128)S(1)}) custom-call(f32[4,16,8,256]{3,2,1,0:T(8,128)S(1)} %get-tuple-element.63.refs_1_.refs_0_, f32[3,16,8,256]{3,2,1,0:T(8,128)S(1)} %collective-permute-done.20.refs_1_, f32[3,16,8,256]{3,2,1,0:T(8,128)S(1)} %collective-permute-done.21.refs_2_, ...), custom_call_target="tpu_custom_call" | custom-call | flops 10485760 | bytes 4194304 | tf_op jit(solution)/shard_map/finish_part/pallas_call | solution.py:226
  114.0 0.1 collective-permute-start.24
  114.1 4.4 %collective-permute-start.25 = (f32[3,16,8,256]{3,2,1,0:T(8,128)S(1)}, f32[3,16,8,256]{3,2,1,0:T(8,128)S(1)}, u32[]{:S(2)}, u32[]{:S(2)}) collective-permute-start(f32[3,16,8,256]{3,2,1,0:T(8,128)S(1)} %get-tuple-element.74), channel_id=1, source_target_pairs={{1,0},{2,1},{3,2},{4,3},{5,4},{6,5},{7,6},{8,7},{9,8},{10,9},{11,1... | collective-permute-start | bytes 1179656 | tf_op jit(solution)/shard_map/ppermute | solution.py:309
  118.5 2.1 %finish_part.14 = (f32[4,16,8,256]{3,2,1,0:T(8,128)S(1)}, f32[3,16,8,256]{3,2,1,0:T(8,128)S(1)}, f32[3,16,8,256]{3,2,1,0:T(8,128)S(1)}) custom-call(f32[4,16,8,256]{3,2,1,0:T(8,128)S(1)} %get-tuple-element.58.refs_0_, f32[3,16,8,256]{3,2,1,0:T(8,128)S(1)} %collective-permute-done.14.refs_1_, f32[3,16,8,256]{3,2,1,0:T(8,128)S(1)} %collective-permute-done.15.refs_2_, ...), custom_call_target="tpu_custom_call" | custom-call | flops 10485760 | bytes 4194304 | tf_op jit(solution)/shard_map/finish_part/pallas_call | solution.py:226
  120.7 0.1 collective-permute-start.18
  120.7 4.4 %collective-permute-start.19 = (f32[3,16,8,256]{3,2,1,0:T(8,128)S(1)}, f32[3,16,8,256]{3,2,1,0:T(8,128)S(1)}, u32[]{:S(2)}, u32[]{:S(2)}) collective-permute-start(f32[3,16,8,256]{3,2,1,0:T(8,128)S(1)} %get-tuple-element.66), channel_id=1, source_target_pairs={{1,0},{2,1},{3,2},{4,3},{5,4},{6,5},{7,6},{8,7},{9,8},{10,9},{11,1... | collective-permute-start | bytes 1179656 | tf_op jit(solution)/shard_map/ppermute | solution.py:309
  125.2 14.2 %local_part.8.refs_3_ = f32[4,32,8,256]{3,2,1,0:T(8,128)S(1)} custom-call(f32[4,16,8,256]{3,2,1,0:T(8,128)S(1)} %get-tuple-element.64.refs_0_.refs_4_, f32[4,16,8,256]{3,2,1,0:T(8,128)S(1)} %get-tuple-element.69.refs_1_.refs_0_.refs_4_, f32[4,32,8,256]{3,2,1,0:T(8,128)S(1)} %constant_dynamic-update-slice_fusion.refs_2_), custom_call_target="tpu_custom_call" | custom-call | flops 34078720 | bytes 3145728 | tf_op jit(solution)/shard_map/local_part/pallas_call | solution.py:155
  139.5 2.1 %finish_part.17 = (f32[4,16,8,256]{3,2,1,0:T(8,128)S(1)}, f32[3,16,8,256]{3,2,1,0:T(8,128)S(1)}, f32[3,16,8,256]{3,2,1,0:T(8,128)S(1)}) custom-call(f32[4,16,8,256]{3,2,1,0:T(8,128)S(1)} %get-tuple-element.69.refs_1_.refs_0_.refs_4_, f32[3,16,8,256]{3,2,1,0:T(8,128)S(1)} %collective-permute-done.24.refs_1_, ...), custom_call_target="tpu_custom_call" | custom-call | flops 10485760 | bytes 4194304 | tf_op jit(solution)/shard_map/finish_part/pallas_call | solution.py:226
  141.5 0.1 collective-permute-start.26
  141.6 4.4 %collective-permute-start.27 = (f32[3,16,8,256]{3,2,1,0:T(8,128)S(1)}, f32[3,16,8,256]{3,2,1,0:T(8,128)S(1)}, u32[]{:S(2)}, u32[]{:S(2)}) collective-permute-start(f32[3,16,8,256]{3,2,1,0:T(8,128)S(1)} %get-tuple-element.77), channel_id=1, source_target_pairs={{1,0},{2,1},{3,2},{4,3},{5,4},{6,5},{7,6},{8,7},{9,8},{10,9},{11,1... | collective-permute-start | bytes 1179656 | tf_op jit(solution)/shard_map/ppermute | solution.py:309
  146.0 2.0 %finish_part.16 = (f32[4,16,8,256]{3,2,1,0:T(8,128)S(1)}, f32[3,16,8,256]{3,2,1,0:T(8,128)S(1)}, f32[3,16,8,256]{3,2,1,0:T(8,128)S(1)}) custom-call(f32[4,16,8,256]{3,2,1,0:T(8,128)S(1)} %get-tuple-element.64.refs_0_.refs_4_, f32[3,16,8,256]{3,2,1,0:T(8,128)S(1)} %collective-permute-done.18.refs_1_, f32[3,16,8,256]{3,2,1,0:T(8,128)S(1)} %collective-permute-done.19.refs_2_, ...), custom_call_target="tpu_custom_call" | custom-call | flops 10485760 | bytes 4194304 | tf_op jit(solution)/shard_map/finish_part/pallas_call | solution.py:226
  148.2 4.4 %collective-permute-start.23 = (f32[3,16,8,256]{3,2,1,0:T(8,128)S(1)}, f32[3,16,8,256]{3,2,1,0:T(8,128)S(1)}, u32[]{:S(2)}, u32[]{:S(2)}) collective-permute-start(f32[3,16,8,256]{3,2,1,0:T(8,128)S(1)} %get-tuple-element.72), channel_id=1, source_target_pairs={{1,0},{2,1},{3,2},{4,3},{5,4},{6,5},{7,6},{8,7},{9,8},{10,9},{11,1... | collective-permute-start | bytes 1179656 | tf_op jit(solution)/shard_map/ppermute | solution.py:309
  152.6 1.3 copy.7
  153.9 14.2 %local_part.9.refs_3_ = f32[4,32,8,256]{3,2,1,0:T(8,128)S(1)} custom-call(f32[4,16,8,256]{3,2,1,0:T(8,128)S(1)} %get-tuple-element.70.refs_0_, f32[4,16,8,256]{3,2,1,0:T(8,128)S(1)} %get-tuple-element.75.refs_1_.refs_0_, f32[4,32,8,256]{3,2,1,0:T(8,128)S(1)} %constant_dynamic-update-slice_fusion.refs_2_), custom_call_target="tpu_custom_call" | custom-call | flops 34078720 | bytes 3145728 | tf_op jit(solution)/shard_map/local_part/pallas_call | solution.py:155
  168.1 2.0 %finish_part.19 = f32[4,16,8,256]{3,2,1,0:T(8,128)S(1)} custom-call(f32[4,16,8,256]{3,2,1,0:T(8,128)S(1)} %get-tuple-element.75.refs_1_.refs_0_, f32[3,16,8,256]{3,2,1,0:T(8,128)S(1)} %collective-permute-done.26.refs_1_, f32[3,16,8,256]{3,2,1,0:T(8,128)S(1)} %collective-permute-done.27.refs_2_, f32[4,32,8,256]{3,2,1,0:T(8,128)S(1)} %local_part.9.refs_3_, ...), custom_call_target="tpu_custom_call" | custom-call | flops 10485760 | bytes 4194304 | tf_op jit(solution)/shard_map/finish_part/pallas_call | solution.py:226
  170.2 2.0 %finish_part.18 = f32[4,16,8,256]{3,2,1,0:T(8,128)S(1)} custom-call(f32[4,16,8,256]{3,2,1,0:T(8,128)S(1)} %get-tuple-element.70.refs_0_, f32[3,16,8,256]{3,2,1,0:T(8,128)S(1)} %collective-permute-done.22.refs_1_, f32[3,16,8,256]{3,2,1,0:T(8,128)S(1)} %collective-permute-done.23.refs_2_, f32[4,32,8,256]{3,2,1,0:T(8,128)S(1)} %local_part.9.refs_3_, ...), custom_call_target="tpu_custom_call" | custom-call | flops 10485760 | bytes 4194304 | tf_op jit(solution)/shard_map/finish_part/pallas_call | solution.py:226
  172.2 0.1 maximum_bitcast_fusion
  172.3 1.3 copy.9
  (33 shorter events, 0.3 us)
Async XLA Ops:
  0.6 1.5 copy-start
  3.4 9.6 %collective-permute-start = (f32[1,32,8,256]{3,2,1,0:T(8,128)S(1)}, f32[1,32,8,256]{3,2,1,0:T(8,128)S(1)}, u32[]{:S(2)}, u32[]{:S(2)}) collective-permute-start(f32[1,32,8,256]{3,2,1,0:T(8,128)S(1)} %get-tuple-element.94.high_ref), channel_id=1, source_target_pairs={{0,1},{1,2},{2,3},{3,4},{4,5},{5,6},{6,7},{7,8},{8,9},{9,10},{10,1... | collective-permute-start | bytes 786440 | tf_op jit(solution)/shard_map/ppermute | solution.py:304
  3.9 9.1 %collective-permute-start.1 = (f32[1,32,8,256]{3,2,1,0:T(8,128)S(1)}, f32[1,32,8,256]{3,2,1,0:T(8,128)S(1)}, u32[]{:S(2)}, u32[]{:S(2)}) collective-permute-start(f32[1,32,8,256]{3,2,1,0:T(8,128)S(1)} %get-tuple-element.95.low_ref), channel_id=1, source_target_pairs={{1,0},{2,1},{3,2},{4,3},{5,4},{6,5},{7,6},{8,7},{9,8},{10,9},{11,1... | collective-permute-start | bytes 786440 | tf_op jit(solution)/shard_map/ppermute | solution.py:309
  13.0 4.7 %copy-start.1 = (f32[4,256,256]{2,1,0:T(8,128)S(1)}, f32[4,256,256]{2,1,0:T(8,128)}, u32[]{:S(2)}) copy-start(f32[4,256,256]{2,1,0:T(8,128)} %param.3) | copy-start | bytes 3145732
  13.1 8.7 %collective-permute-start.2 = (f32[1,32,8,256]{3,2,1,0:T(8,128)S(1)}, f32[1,32,8,256]{3,2,1,0:T(8,128)S(1)}, u32[]{:S(2)}, u32[]{:S(2)}) collective-permute-start(f32[1,32,8,256]{3,2,1,0:T(8,128)S(1)} %get-tuple-element.92.high_ref), channel_id=1, source_target_pairs={{0,1},{1,2},{2,3},{3,4},{4,5},{5,6},{6,7},{7,8},{8,9},{9,10},{10,1... | collective-permute-start | bytes 786440 | tf_op jit(solution)/shard_map/ppermute | solution.py:304
  15.3 6.5 %collective-permute-start.3 = (f32[1,32,8,256]{3,2,1,0:T(8,128)S(1)}, f32[1,32,8,256]{3,2,1,0:T(8,128)S(1)}, u32[]{:S(2)}, u32[]{:S(2)}) collective-permute-start(f32[1,32,8,256]{3,2,1,0:T(8,128)S(1)} %get-tuple-element.93.low_ref), channel_id=1, source_target_pairs={{1,0},{2,1},{3,2},{4,3},{5,4},{6,5},{7,6},{8,7},{9,8},{10,9},{11,1... | collective-permute-start | bytes 786440 | tf_op jit(solution)/shard_map/ppermute | solution.py:309
  21.9 22.8 %collective-permute-start.4 = (f32[1,32,8,256]{3,2,1,0:T(8,128)S(1)}, f32[1,32,8,256]{3,2,1,0:T(8,128)S(1)}, u32[]{:S(2)}, u32[]{:S(2)}) collective-permute-start(f32[1,32,8,256]{3,2,1,0:T(8,128)S(1)} %get-tuple-element.90.high_ref), channel_id=1, source_target_pairs={{0,1},{1,2},{2,3},{3,4},{4,5},{5,6},{6,7},{7,8},{8,9},{9,10},{10,1... | collective-permute-start | bytes 786440 | tf_op jit(solution)/shard_map/ppermute | solution.py:304
  24.1 20.6 %collective-permute-start.5 = (f32[1,32,8,256]{3,2,1,0:T(8,128)S(1)}, f32[1,32,8,256]{3,2,1,0:T(8,128)S(1)}, u32[]{:S(2)}, u32[]{:S(2)}) collective-permute-start(f32[1,32,8,256]{3,2,1,0:T(8,128)S(1)} %get-tuple-element.91.low_ref), channel_id=1, source_target_pairs={{1,0},{2,1},{3,2},{4,3},{5,4},{6,5},{7,6},{8,7},{9,8},{10,9},{11,1... | collective-permute-start | bytes 786440 | tf_op jit(solution)/shard_map/ppermute | solution.py:309
  26.5 33.9 %collective-permute-start.9 = (f32[3,16,8,256]{3,2,1,0:T(8,128)S(1)}, f32[3,16,8,256]{3,2,1,0:T(8,128)S(1)}, u32[]{:S(2)}, u32[]{:S(2)}) collective-permute-start(f32[3,16,8,256]{3,2,1,0:T(8,128)S(1)} %get-tuple-element.78), channel_id=1, source_target_pairs={{1,0},{2,1},{3,2},{4,3},{5,4},{6,5},{7,6},{8,7},{9,8},{10,9},{11,1... | collective-permute-start | bytes 1179656 | tf_op jit(solution)/shard_map/ppermute | solution.py:309
  27.0 26.7 %collective-permute-start.13 = (f32[3,16,8,256]{3,2,1,0:T(8,128)S(1)}, f32[3,16,8,256]{3,2,1,0:T(8,128)S(1)}, u32[]{:S(2)}, u32[]{:S(2)}) collective-permute-start(f32[3,16,8,256]{3,2,1,0:T(8,128)S(1)} %get-tuple-element.79), channel_id=1, source_target_pairs={{1,0},{2,1},{3,2},{4,3},{5,4},{6,5},{7,6},{8,7},{9,8},{10,9},{11,1... | collective-permute-start | bytes 1179656 | tf_op jit(solution)/shard_map/ppermute | solution.py:309
  27.1 26.6 %collective-permute-start.12 = (f32[3,16,8,256]{3,2,1,0:T(8,128)S(1)}, f32[3,16,8,256]{3,2,1,0:T(8,128)S(1)}, u32[]{:S(2)}, u32[]{:S(2)}) collective-permute-start(f32[3,16,8,256]{3,2,1,0:T(8,128)S(1)} %get-tuple-element.80), channel_id=1, source_target_pairs={{0,1},{1,2},{2,3},{3,4},{4,5},{5,6},{6,7},{7,8},{8,9},{9,10},{10,1... | collective-permute-start | bytes 1179656 | tf_op jit(solution)/shard_map/ppermute | solution.py:304
  44.8 8.7 %collective-permute-start.6 = (f32[1,32,8,256]{3,2,1,0:T(8,128)S(1)}, f32[1,32,8,256]{3,2,1,0:T(8,128)S(1)}, u32[]{:S(2)}, u32[]{:S(2)}) collective-permute-start(f32[1,32,8,256]{3,2,1,0:T(8,128)S(1)} %get-tuple-element.88.high_ref), channel_id=1, source_target_pairs={{0,1},{1,2},{2,3},{3,4},{4,5},{5,6},{6,7},{7,8},{8,9},{9,10},{10,1... | collective-permute-start | bytes 786440 | tf_op jit(solution)/shard_map/ppermute | solution.py:304
  46.1 7.3 %collective-permute-start.7 = (f32[1,32,8,256]{3,2,1,0:T(8,128)S(1)}, f32[1,32,8,256]{3,2,1,0:T(8,128)S(1)}, u32[]{:S(2)}, u32[]{:S(2)}) collective-permute-start(f32[1,32,8,256]{3,2,1,0:T(8,128)S(1)} %get-tuple-element.89.low_ref), channel_id=1, source_target_pairs={{1,0},{2,1},{3,2},{4,3},{5,4},{6,5},{7,6},{8,7},{9,8},{10,9},{11,1... | collective-permute-start | bytes 786440 | tf_op jit(solution)/shard_map/ppermute | solution.py:309
  53.4 10.0 %collective-permute-start.8 = (f32[3,16,8,256]{3,2,1,0:T(8,128)S(1)}, f32[3,16,8,256]{3,2,1,0:T(8,128)S(1)}, u32[]{:S(2)}, u32[]{:S(2)}) collective-permute-start(f32[3,16,8,256]{3,2,1,0:T(8,128)S(1)} %get-tuple-element.81), channel_id=1, source_target_pairs={{0,1},{1,2},{2,3},{3,4},{4,5},{5,6},{6,7},{7,8},{8,9},{9,10},{10,1... | collective-permute-start | bytes 1179656 | tf_op jit(solution)/shard_map/ppermute | solution.py:304
  55.9 28.3 %collective-permute-start.16 = (f32[3,16,8,256]{3,2,1,0:T(8,128)S(1)}, f32[3,16,8,256]{3,2,1,0:T(8,128)S(1)}, u32[]{:S(2)}, u32[]{:S(2)}) collective-permute-start(f32[3,16,8,256]{3,2,1,0:T(8,128)S(1)} %get-tuple-element.61), channel_id=1, source_target_pairs={{0,1},{1,2},{2,3},{3,4},{4,5},{5,6},{6,7},{7,8},{8,9},{9,10},{10,1... | collective-permute-start | bytes 1179656 | tf_op jit(solution)/shard_map/ppermute | solution.py:304
  57.3 26.9 %collective-permute-start.17 = (f32[3,16,8,256]{3,2,1,0:T(8,128)S(1)}, f32[3,16,8,256]{3,2,1,0:T(8,128)S(1)}, u32[]{:S(2)}, u32[]{:S(2)}) collective-permute-start(f32[3,16,8,256]{3,2,1,0:T(8,128)S(1)} %get-tuple-element.62), channel_id=1, source_target_pairs={{1,0},{2,1},{3,2},{4,3},{5,4},{6,5},{7,6},{8,7},{9,8},{10,9},{11,1... | collective-permute-start | bytes 1179656 | tf_op jit(solution)/shard_map/ppermute | solution.py:309
  65.6 25.4 %collective-permute-start.10 = (f32[3,16,8,256]{3,2,1,0:T(8,128)S(1)}, f32[3,16,8,256]{3,2,1,0:T(8,128)S(1)}, u32[]{:S(2)}, u32[]{:S(2)}) collective-permute-start(f32[3,16,8,256]{3,2,1,0:T(8,128)S(1)} %get-tuple-element.55), channel_id=1, source_target_pairs={{0,1},{1,2},{2,3},{3,4},{4,5},{5,6},{6,7},{7,8},{8,9},{9,10},{10,1... | collective-permute-start | bytes 1179656 | tf_op jit(solution)/shard_map/ppermute | solution.py:304
  65.9 25.1 %collective-permute-start.11 = (f32[3,16,8,256]{3,2,1,0:T(8,128)S(1)}, f32[3,16,8,256]{3,2,1,0:T(8,128)S(1)}, u32[]{:S(2)}, u32[]{:S(2)}) collective-permute-start(f32[3,16,8,256]{3,2,1,0:T(8,128)S(1)} %get-tuple-element.56), channel_id=1, source_target_pairs={{1,0},{2,1},{3,2},{4,3},{5,4},{6,5},{7,6},{8,7},{9,8},{10,9},{11,1... | collective-permute-start | bytes 1179656 | tf_op jit(solution)/shard_map/ppermute | solution.py:309
  86.5 25.3 %collective-permute-start.20 = (f32[3,16,8,256]{3,2,1,0:T(8,128)S(1)}, f32[3,16,8,256]{3,2,1,0:T(8,128)S(1)}, u32[]{:S(2)}, u32[]{:S(2)}) collective-permute-start(f32[3,16,8,256]{3,2,1,0:T(8,128)S(1)} %get-tuple-element.67), channel_id=1, source_target_pairs={{0,1},{1,2},{2,3},{3,4},{4,5},{5,6},{6,7},{7,8},{8,9},{9,10},{10,1... | collective-permute-start | bytes 1179656 | tf_op jit(solution)/shard_map/ppermute | solution.py:304
  86.5 25.3 %collective-permute-start.21 = (f32[3,16,8,256]{3,2,1,0:T(8,128)S(1)}, f32[3,16,8,256]{3,2,1,0:T(8,128)S(1)}, u32[]{:S(2)}, u32[]{:S(2)}) collective-permute-start(f32[3,16,8,256]{3,2,1,0:T(8,128)S(1)} %get-tuple-element.68), channel_id=1, source_target_pairs={{1,0},{2,1},{3,2},{4,3},{5,4},{6,5},{7,6},{8,7},{9,8},{10,9},{11,1... | collective-permute-start | bytes 1179656 | tf_op jit(solution)/shard_map/ppermute | solution.py:309
  93.1 25.4 %collective-permute-start.14 = (f32[3,16,8,256]{3,2,1,0:T(8,128)S(1)}, f32[3,16,8,256]{3,2,1,0:T(8,128)S(1)}, u32[]{:S(2)}, u32[]{:S(2)}) collective-permute-start(f32[3,16,8,256]{3,2,1,0:T(8,128)S(1)} %get-tuple-element.59), channel_id=1, source_target_pairs={{0,1},{1,2},{2,3},{3,4},{4,5},{5,6},{6,7},{7,8},{8,9},{9,10},{10,1... | collective-permute-start | bytes 1179656 | tf_op jit(solution)/shard_map/ppermute | solution.py:304
  93.2 25.3 %collective-permute-start.15 = (f32[3,16,8,256]{3,2,1,0:T(8,128)S(1)}, f32[3,16,8,256]{3,2,1,0:T(8,128)S(1)}, u32[]{:S(2)}, u32[]{:S(2)}) collective-permute-start(f32[3,16,8,256]{3,2,1,0:T(8,128)S(1)} %get-tuple-element.60), channel_id=1, source_target_pairs={{1,0},{2,1},{3,2},{4,3},{5,4},{6,5},{7,6},{8,7},{9,8},{10,9},{11,1... | collective-permute-start | bytes 1179656 | tf_op jit(solution)/shard_map/ppermute | solution.py:309
  114.0 25.5 %collective-permute-start.24 = (f32[3,16,8,256]{3,2,1,0:T(8,128)S(1)}, f32[3,16,8,256]{3,2,1,0:T(8,128)S(1)}, u32[]{:S(2)}, u32[]{:S(2)}) collective-permute-start(f32[3,16,8,256]{3,2,1,0:T(8,128)S(1)} %get-tuple-element.73), channel_id=1, source_target_pairs={{0,1},{1,2},{2,3},{3,4},{4,5},{5,6},{6,7},{7,8},{8,9},{9,10},{10,1... | collective-permute-start | bytes 1179656 | tf_op jit(solution)/shard_map/ppermute | solution.py:304
  114.1 25.4 %collective-permute-start.25 = (f32[3,16,8,256]{3,2,1,0:T(8,128)S(1)}, f32[3,16,8,256]{3,2,1,0:T(8,128)S(1)}, u32[]{:S(2)}, u32[]{:S(2)}) collective-permute-start(f32[3,16,8,256]{3,2,1,0:T(8,128)S(1)} %get-tuple-element.74), channel_id=1, source_target_pairs={{1,0},{2,1},{3,2},{4,3},{5,4},{6,5},{7,6},{8,7},{9,8},{10,9},{11,1... | collective-permute-start | bytes 1179656 | tf_op jit(solution)/shard_map/ppermute | solution.py:309
  120.7 25.4 %collective-permute-start.18 = (f32[3,16,8,256]{3,2,1,0:T(8,128)S(1)}, f32[3,16,8,256]{3,2,1,0:T(8,128)S(1)}, u32[]{:S(2)}, u32[]{:S(2)}) collective-permute-start(f32[3,16,8,256]{3,2,1,0:T(8,128)S(1)} %get-tuple-element.65), channel_id=1, source_target_pairs={{0,1},{1,2},{2,3},{3,4},{4,5},{5,6},{6,7},{7,8},{8,9},{9,10},{10,1... | collective-permute-start | bytes 1179656 | tf_op jit(solution)/shard_map/ppermute | solution.py:304
  120.7 25.3 %collective-permute-start.19 = (f32[3,16,8,256]{3,2,1,0:T(8,128)S(1)}, f32[3,16,8,256]{3,2,1,0:T(8,128)S(1)}, u32[]{:S(2)}, u32[]{:S(2)}) collective-permute-start(f32[3,16,8,256]{3,2,1,0:T(8,128)S(1)} %get-tuple-element.66), channel_id=1, source_target_pairs={{1,0},{2,1},{3,2},{4,3},{5,4},{6,5},{7,6},{8,7},{9,8},{10,9},{11,1... | collective-permute-start | bytes 1179656 | tf_op jit(solution)/shard_map/ppermute | solution.py:309
  141.5 26.5 %collective-permute-start.26 = (f32[3,16,8,256]{3,2,1,0:T(8,128)S(1)}, f32[3,16,8,256]{3,2,1,0:T(8,128)S(1)}, u32[]{:S(2)}, u32[]{:S(2)}) collective-permute-start(f32[3,16,8,256]{3,2,1,0:T(8,128)S(1)} %get-tuple-element.76), channel_id=1, source_target_pairs={{0,1},{1,2},{2,3},{3,4},{4,5},{5,6},{6,7},{7,8},{8,9},{9,10},{10,1... | collective-permute-start | bytes 1179656 | tf_op jit(solution)/shard_map/ppermute | solution.py:304
  141.6 26.5 %collective-permute-start.27 = (f32[3,16,8,256]{3,2,1,0:T(8,128)S(1)}, f32[3,16,8,256]{3,2,1,0:T(8,128)S(1)}, u32[]{:S(2)}, u32[]{:S(2)}) collective-permute-start(f32[3,16,8,256]{3,2,1,0:T(8,128)S(1)} %get-tuple-element.77), channel_id=1, source_target_pairs={{1,0},{2,1},{3,2},{4,3},{5,4},{6,5},{7,6},{8,7},{9,8},{10,9},{11,1... | collective-permute-start | bytes 1179656 | tf_op jit(solution)/shard_map/ppermute | solution.py:309
  148.1 22.1 %collective-permute-start.22 = (f32[3,16,8,256]{3,2,1,0:T(8,128)S(1)}, f32[3,16,8,256]{3,2,1,0:T(8,128)S(1)}, u32[]{:S(2)}, u32[]{:S(2)}) collective-permute-start(f32[3,16,8,256]{3,2,1,0:T(8,128)S(1)} %get-tuple-element.71), channel_id=1, source_target_pairs={{0,1},{1,2},{2,3},{3,4},{4,5},{5,6},{6,7},{7,8},{8,9},{9,10},{10,1... | collective-permute-start | bytes 1179656 | tf_op jit(solution)/shard_map/ppermute | solution.py:304
  148.2 22.0 %collective-permute-start.23 = (f32[3,16,8,256]{3,2,1,0:T(8,128)S(1)}, f32[3,16,8,256]{3,2,1,0:T(8,128)S(1)}, u32[]{:S(2)}, u32[]{:S(2)}) collective-permute-start(f32[3,16,8,256]{3,2,1,0:T(8,128)S(1)} %get-tuple-element.72), channel_id=1, source_target_pairs={{1,0},{2,1},{3,2},{4,3},{5,4},{6,5},{7,6},{8,7},{9,8},{10,9},{11,1... | collective-permute-start | bytes 1179656 | tf_op jit(solution)/shard_map/ppermute | solution.py:309

commit v2 on v1

--- a/solution.py
+++ b/solution.py
@@ -144,7 +144,7 @@
     lax.fori_loop(0, tiles // block, loop, 0)
 
 
-def local_part(pieces, velocity, block=4):
+def local_part(pieces, velocity, block=16):
     layers, per, _, lanes = pieces[0].shape
     tiles = per * len(pieces)
     both = velocity is None
@@ -271,7 +271,7 @@
             one(i, t, at(i, t), at(i, t - 1), at(i, t + 1))
         return carry
 
-    lax.fori_loop(1, tiles - 1, loop, 0)
+    lax.fori_loop(1, tiles - 1, loop, 0, unroll=5)
 
 
 def sweep_part(low, mid, high, weight, fixed):

time: 174 us -> 134 us (0.77)
  the two profiles are of different devices: /device:TPU:0 before, /device:TPU:1 now
where the time goes in v2:
time: 134 us; the launch traced here: 132 us
  Pallas kernels  53.9 us (40%)
  waiting for transfers between devices  39 us (29%)
  starting transfers between devices  30.1 us (22%)
  local copies, waits for them, and re-layouts  4.86 us (4%)
  other arithmetic  3.23 us (2%)
    pallas_call x5, Pallas kernels, local_part(): pl.pallas_call(functools.partial(local_body, len(pieces), both, block), g...  28.7 us
    pallas_call x10, Pallas kernels, finish_part(): pl.pallas_call(functools.partial(finish_body, kind, last), grid=(per // b...  21 us
    ppermute x14, starting transfers between devices, to_next(): lax.ppermute(array, 'gx', [(i, (i + 1) % count) for i in range(count)])  20.9 us
    ppermute x14, waiting for transfers between devices, to_next(): lax.ppermute(array, 'gx', [(i, (i + 1) % count) for i in range(count)])  20.6 us
    ppermute x14, waiting for transfers between devices, to_previous(): lax.ppermute(array, 'gx', [((i + 1) % count, i) for i in range(count)])  18.4 us
    ppermute x14, starting transfers between devices, to_previous(): lax.ppermute(array, 'gx', [((i + 1) % count, i) for i in range(count)])  9.14 us
    pallas_call x4, Pallas kernels, sweep_part(): pl.pallas_call(sweep_body, in_specs=[vmem] * 5, out_specs=(vmem, vmem, vm...  4.2 us
  transfers between devices with their start and end apart: 28, of which 14 were waited for; matrix products, arithmetic and copies ran while one was open for 2% of the time, Pallas kernels for 39%

profile of v2, /device:TPU:1, one launch (start us, length us, event | category | flops | bytes accessed | tf_op | source)
XLA Modules:
  0.0 132.1 jit_solution(11598506894873355854)
XLA Ops:
  0.6 1.4 %convert_element_type.7 = f32[4,256,256]{2,1,0:T(8,128)S(1)} convert(s32[4,256,256]{2,1,0:T(8,128)} %param.5) | non-fusion elementwise | flops 262144 | bytes 2097152 | tf_op jit(solution)/shard_map/convert_element_type | solution.py:314
  2.0 0.1 copy-done
  2.2 1.2 bitcast_multiply_fusion.fixed_ref
  3.4 2.7 %collective-permute-start = (f32[1,32,8,256]{3,2,1,0:T(8,128)S(1)}, f32[1,32,8,256]{3,2,1,0:T(8,128)S(1)}, u32[]{:S(2)}, u32[]{:S(2)}) collective-permute-start(f32[1,32,8,256]{3,2,1,0:T(8,128)S(1)} %get-tuple-element.94.high_ref), channel_id=1, source_target_pairs={{0,1},{1,2},{2,3},{3,4},{4,5},{5,6},{6,7},{7,8},{8,9},{9,10},{10,1... | collective-permute-start | bytes 786440 | tf_op jit(solution)/shard_map/ppermute | solution.py:304
  6.0 0.6 copy.16
  6.7 1.1 sweep_part.4
  7.8 1.6 %collective-permute-done = f32[1,32,8,256]{3,2,1,0:T(8,128)S(1)} collective-permute-done((f32[1,32,8,256]{3,2,1,0:T(8,128)S(1)}, f32[1,32,8,256]{3,2,1,0:T(8,128)S(1)}, u32[]{:S(2)}, u32[]{:S(2)}) %collective-permute-start) | collective-permute-done | bytes 262176 | tf_op jit(solution)/shard_map/ppermute | solution.py:304
  9.4 5.3 %collective-permute-done.1 = f32[1,32,8,256]{3,2,1,0:T(8,128)S(1)} collective-permute-done((f32[1,32,8,256]{3,2,1,0:T(8,128)S(1)}, f32[1,32,8,256]{3,2,1,0:T(8,128)S(1)}, u32[]{:S(2)}, u32[]{:S(2)}) %collective-permute-start.1) | collective-permute-done | bytes 262176 | tf_op jit(solution)/shard_map/ppermute | solution.py:309
  14.6 0.1 multiply_add_fusion.6
  14.8 0.5 collective-permute-start.3
  15.3 0.6 copy-done.1
  15.9 0.6 copy.15
  16.5 1.1 sweep_part.5
  17.5 3.4 %collective-permute-done.2 = f32[1,32,8,256]{3,2,1,0:T(8,128)S(1)} collective-permute-done((f32[1,32,8,256]{3,2,1,0:T(8,128)S(1)}, f32[1,32,8,256]{3,2,1,0:T(8,128)S(1)}, u32[]{:S(2)}, u32[]{:S(2)}) %collective-permute-start.2) | collective-permute-done | bytes 262176 | tf_op jit(solution)/shard_map/ppermute | solution.py:304
  20.9 2.5 %collective-permute-done.3 = f32[1,32,8,256]{3,2,1,0:T(8,128)S(1)} collective-permute-done((f32[1,32,8,256]{3,2,1,0:T(8,128)S(1)}, f32[1,32,8,256]{3,2,1,0:T(8,128)S(1)}, u32[]{:S(2)}, u32[]{:S(2)}) %collective-permute-start.3) | collective-permute-done | bytes 262176 | tf_op jit(solution)/shard_map/ppermute | solution.py:309
  23.5 0.1 multiply_add_fusion.4
  23.6 0.5 collective-permute-start.5
  24.1 0.1 fusion.3
  24.3 2.4 %collective-permute-start.9 = (f32[3,16,8,256]{3,2,1,0:T(8,128)S(1)}, f32[3,16,8,256]{3,2,1,0:T(8,128)S(1)}, u32[]{:S(2)}, u32[]{:S(2)}) collective-permute-start(f32[3,16,8,256]{3,2,1,0:T(8,128)S(1)} %get-tuple-element.78), channel_id=1, source_target_pairs={{1,0},{2,1},{3,2},{4,3},{5,4},{6,5},{7,6},{8,7},{9,8},{10,9},{11,1... | collective-permute-start | bytes 1179656 | tf_op jit(solution)/shard_map/ppermute | solution.py:309
  26.7 0.4 collective-permute-start.13
  27.1 1.3 collective-permute-start.12
  28.4 6.1 %local_part.5 = (f32[4,32,8,256]{3,2,1,0:T(8,128)S(1)}, f32[4,32,8,256]{3,2,1,0:T(8,128)S(1)}) custom-call(f32[4,32,8,256]{3,2,1,0:T(8,128)S(1)} %bitcast.20), custom_call_target="tpu_custom_call" | custom-call | flops 34078720 | bytes 3145728 | tf_op jit(solution)/shard_map/local_part/pallas_call | solution.py:155
  34.5 1.1 sweep_part.6
  35.6 1.7 %collective-permute-done.4 = f32[1,32,8,256]{3,2,1,0:T(8,128)S(1)} collective-permute-done((f32[1,32,8,256]{3,2,1,0:T(8,128)S(1)}, f32[1,32,8,256]{3,2,1,0:T(8,128)S(1)}, u32[]{:S(2)}, u32[]{:S(2)}) %collective-permute-start.4) | collective-permute-done | bytes 262176 | tf_op jit(solution)/shard_map/ppermute | solution.py:304
  37.4 0.1 multiply_add_fusion.2
  37.5 2.5 %collective-permute-start.6 = (f32[1,32,8,256]{3,2,1,0:T(8,128)S(1)}, f32[1,32,8,256]{3,2,1,0:T(8,128)S(1)}, u32[]{:S(2)}, u32[]{:S(2)}) collective-permute-start(f32[1,32,8,256]{3,2,1,0:T(8,128)S(1)} %get-tuple-element.88.high_ref), channel_id=1, source_target_pairs={{0,1},{1,2},{2,3},{3,4},{4,5},{5,6},{6,7},{7,8},{8,9},{9,10},{10,1... | collective-permute-start | bytes 786440 | tf_op jit(solution)/shard_map/ppermute | solution.py:304
  40.1 1.1 sweep_part.7
  41.1 6.0 %collective-permute-done.6 = f32[1,32,8,256]{3,2,1,0:T(8,128)S(1)} collective-permute-done((f32[1,32,8,256]{3,2,1,0:T(8,128)S(1)}, f32[1,32,8,256]{3,2,1,0:T(8,128)S(1)}, u32[]{:S(2)}, u32[]{:S(2)}) %collective-permute-start.6) | collective-permute-done | bytes 262176 | tf_op jit(solution)/shard_map/ppermute | solution.py:304
  47.2 2.5 %collective-permute-start.8 = (f32[3,16,8,256]{3,2,1,0:T(8,128)S(1)}, f32[3,16,8,256]{3,2,1,0:T(8,128)S(1)}, u32[]{:S(2)}, u32[]{:S(2)}) collective-permute-start(f32[3,16,8,256]{3,2,1,0:T(8,128)S(1)} %get-tuple-element.81), channel_id=1, source_target_pairs={{0,1},{1,2},{2,3},{3,4},{4,5},{5,6},{6,7},{7,8},{8,9},{9,10},{10,1... | collective-permute-start | bytes 1179656 | tf_op jit(solution)/shard_map/ppermute | solution.py:304
  49.7 5.1 %collective-permute-done.7 = f32[1,32,8,256]{3,2,1,0:T(8,128)S(1)} collective-permute-done((f32[1,32,8,256]{3,2,1,0:T(8,128)S(1)}, f32[1,32,8,256]{3,2,1,0:T(8,128)S(1)}, u32[]{:S(2)}, u32[]{:S(2)}) %collective-permute-start.7) | collective-permute-done | bytes 262176 | tf_op jit(solution)/shard_map/ppermute | solution.py:309
  54.9 0.2 pad_maximum_fusion
  55.1 2.2 %finish_part.11 = (f32[4,16,8,256]{3,2,1,0:T(8,128)S(1)}, f32[3,16,8,256]{3,2,1,0:T(8,128)S(1)}, f32[3,16,8,256]{3,2,1,0:T(8,128)S(1)}) custom-call(f32[4,16,8,256]{3,2,1,0:T(8,128)S(1)} %get-tuple-element.83.refs_0_, f32[3,16,8,256]{3,2,1,0:T(8,128)S(1)} %collective-permute-done.12.refs_1_, f32[3,16,8,256]{3,2,1,0:T(8,128)S(1)} %collective-permute-done.13.refs_2_, ...), custom_call_target="tpu_custom_call" | custom-call | flops 10485760 | bytes 4194304 | tf_op jit(solution)/shard_map/finish_part/pallas_call | solution.py:226
  57.3 0.5 collective-permute-start.17
  57.8 2.1 %finish_part.10 = (f32[4,16,8,256]{3,2,1,0:T(8,128)S(1)}, f32[3,16,8,256]{3,2,1,0:T(8,128)S(1)}, f32[3,16,8,256]{3,2,1,0:T(8,128)S(1)}) custom-call(f32[4,16,8,256]{3,2,1,0:T(8,128)S(1)} %get-tuple-element.82.refs_0_, f32[3,16,8,256]{3,2,1,0:T(8,128)S(1)} %collective-permute-done.8.refs_1_, f32[3,16,8,256]{3,2,1,0:T(8,128)S(1)} %collective-permute-done.9.refs_2_, ...), custom_call_target="tpu_custom_call" | custom-call | flops 10485760 | bytes 4194304 | tf_op jit(solution)/shard_map/finish_part/pallas_call | solution.py:226
  60.0 1.4 %collective-permute-start.10 = (f32[3,16,8,256]{3,2,1,0:T(8,128)S(1)}, f32[3,16,8,256]{3,2,1,0:T(8,128)S(1)}, u32[]{:S(2)}, u32[]{:S(2)}) collective-permute-start(f32[3,16,8,256]{3,2,1,0:T(8,128)S(1)} %get-tuple-element.55), channel_id=1, source_target_pairs={{0,1},{1,2},{2,3},{3,4},{4,5},{5,6},{6,7},{7,8},{8,9},{9,10},{10,1... | collective-permute-start | bytes 1179656 | tf_op jit(solution)/shard_map/ppermute | solution.py:304
  61.3 5.6 %local_part.6.refs_3_ = f32[4,32,8,256]{3,2,1,0:T(8,128)S(1)} custom-call(f32[4,16,8,256]{3,2,1,0:T(8,128)S(1)} %get-tuple-element.54.refs_0_, f32[4,16,8,256]{3,2,1,0:T(8,128)S(1)} %get-tuple-element.57.refs_1_.refs_0_, f32[4,32,8,256]{3,2,1,0:T(8,128)S(1)} %get-tuple-element.84.refs_5_.refs_2_.refs_4_), custom_call_target="tpu_custom_call" | custom-call | flops 34078720 | bytes 3145728 | tf_op jit(solution)/shard_map/local_part/pallas_call | solution.py:155
  67.0 1.4 %collective-permute-done.16.refs_1_ = f32[3,16,8,256]{3,2,1,0:T(8,128)S(1)} collective-permute-done((f32[3,16,8,256]{3,2,1,0:T(8,128)S(1)}, f32[3,16,8,256]{3,2,1,0:T(8,128)S(1)}, u32[]{:S(2)}, u32[]{:S(2)}) %collective-permute-start.16) | collective-permute-done | bytes 393248 | tf_op jit(solution)/shard_map/ppermute | solution.py:304
  68.4 2.1 %finish_part.13 = (f32[4,16,8,256]{3,2,1,0:T(8,128)S(1)}, f32[3,16,8,256]{3,2,1,0:T(8,128)S(1)}, f32[3,16,8,256]{3,2,1,0:T(8,128)S(1)}) custom-call(f32[4,16,8,256]{3,2,1,0:T(8,128)S(1)} %get-tuple-element.57.refs_1_.refs_0_, f32[3,16,8,256]{3,2,1,0:T(8,128)S(1)} %collective-permute-done.16.refs_1_, f32[3,16,8,256]{3,2,1,0:T(8,128)S(1)} %collective-permute-done.17.refs_2_, ...), custom_call_target="tpu_custom_call" | custom-call | flops 10485760 | bytes 4194304 | tf_op jit(solution)/shard_map/finish_part/pallas_call | solution.py:226
  70.5 2.5 %collective-permute-start.20 = (f32[3,16,8,256]{3,2,1,0:T(8,128)S(1)}, f32[3,16,8,256]{3,2,1,0:T(8,128)S(1)}, u32[]{:S(2)}, u32[]{:S(2)}) collective-permute-start(f32[3,16,8,256]{3,2,1,0:T(8,128)S(1)} %get-tuple-element.67), channel_id=1, source_target_pairs={{0,1},{1,2},{2,3},{3,4},{4,5},{5,6},{6,7},{7,8},{8,9},{9,10},{10,1... | collective-permute-start | bytes 1179656 | tf_op jit(solution)/shard_map/ppermute | solution.py:304
  73.0 3.7 %collective-permute-done.10.refs_1_ = f32[3,16,8,256]{3,2,1,0:T(8,128)S(1)} collective-permute-done((f32[3,16,8,256]{3,2,1,0:T(8,128)S(1)}, f32[3,16,8,256]{3,2,1,0:T(8,128)S(1)}, u32[]{:S(2)}, u32[]{:S(2)}) %collective-permute-start.10) | collective-permute-done | bytes 393248 | tf_op jit(solution)/shard_map/ppermute | solution.py:304
  76.8 2.1 %finish_part.12 = (f32[4,16,8,256]{3,2,1,0:T(8,128)S(1)}, f32[3,16,8,256]{3,2,1,0:T(8,128)S(1)}, f32[3,16,8,256]{3,2,1,0:T(8,128)S(1)}) custom-call(f32[4,16,8,256]{3,2,1,0:T(8,128)S(1)} %get-tuple-element.54.refs_0_, f32[3,16,8,256]{3,2,1,0:T(8,128)S(1)} %collective-permute-done.10.refs_1_, f32[3,16,8,256]{3,2,1,0:T(8,128)S(1)} %collective-permute-done.11.refs_2_, ...), custom_call_target="tpu_custom_call" | custom-call | flops 10485760 | bytes 4194304 | tf_op jit(solution)/shard_map/finish_part/pallas_call | solution.py:226
  78.9 2.5 %collective-permute-start.14 = (f32[3,16,8,256]{3,2,1,0:T(8,128)S(1)}, f32[3,16,8,256]{3,2,1,0:T(8,128)S(1)}, u32[]{:S(2)}, u32[]{:S(2)}) collective-permute-start(f32[3,16,8,256]{3,2,1,0:T(8,128)S(1)} %get-tuple-element.59), channel_id=1, source_target_pairs={{0,1},{1,2},{2,3},{3,4},{4,5},{5,6},{6,7},{7,8},{8,9},{9,10},{10,1... | collective-permute-start | bytes 1179656 | tf_op jit(solution)/shard_map/ppermute | solution.py:304
  81.5 5.6 %local_part.7.refs_3_ = f32[4,32,8,256]{3,2,1,0:T(8,128)S(1)} custom-call(f32[4,16,8,256]{3,2,1,0:T(8,128)S(1)} %get-tuple-element.58.refs_0_, f32[4,16,8,256]{3,2,1,0:T(8,128)S(1)} %get-tuple-element.63.refs_1_.refs_0_, f32[4,32,8,256]{3,2,1,0:T(8,128)S(1)} %get-tuple-element.84.refs_5_.refs_2_.refs_4_), custom_call_target="tpu_custom_call" | custom-call | flops 34078720 | bytes 3145728 | tf_op jit(solution)/shard_map/local_part/pallas_call | solution.py:155
  87.1 1.6 %collective-permute-done.21.refs_2_ = f32[3,16,8,256]{3,2,1,0:T(8,128)S(1)} collective-permute-done((f32[3,16,8,256]{3,2,1,0:T(8,128)S(1)}, f32[3,16,8,256]{3,2,1,0:T(8,128)S(1)}, u32[]{:S(2)}, u32[]{:S(2)}) %collective-permute-start.21) | collective-permute-done | bytes 393248 | tf_op jit(solution)/shard_map/ppermute | solution.py:309
  88.7 2.1 %finish_part.15 = (f32[4,16,8,256]{3,2,1,0:T(8,128)S(1)}, f32[3,16,8,256]{3,2,1,0:T(8,128)S(1)}, f32[3,16,8,256]{3,2,1,0:T(8,128)S(1)}) custom-call(f32[4,16,8,256]{3,2,1,0:T(8,128)S(1)} %get-tuple-element.63.refs_1_.refs_0_, f32[3,16,8,256]{3,2,1,0:T(8,128)S(1)} %collective-permute-done.20.refs_1_, f32[3,16,8,256]{3,2,1,0:T(8,128)S(1)} %collective-permute-done.21.refs_2_, ...), custom_call_target="tpu_custom_call" | custom-call | flops 10485760 | bytes 4194304 | tf_op jit(solution)/shard_map/finish_part/pallas_call | solution.py:226
  90.8 0.3 collective-permute-start.24
  91.1 0.3 collective-permute-start.25
  91.4 1.5 %collective-permute-done.15.refs_2_ = f32[3,16,8,256]{3,2,1,0:T(8,128)S(1)} collective-permute-done((f32[3,16,8,256]{3,2,1,0:T(8,128)S(1)}, f32[3,16,8,256]{3,2,1,0:T(8,128)S(1)}, u32[]{:S(2)}, u32[]{:S(2)}) %collective-permute-start.15) | collective-permute-done | bytes 393248 | tf_op jit(solution)/shard_map/ppermute | solution.py:309
  92.9 2.1 %finish_part.14 = (f32[4,16,8,256]{3,2,1,0:T(8,128)S(1)}, f32[3,16,8,256]{3,2,1,0:T(8,128)S(1)}, f32[3,16,8,256]{3,2,1,0:T(8,128)S(1)}) custom-call(f32[4,16,8,256]{3,2,1,0:T(8,128)S(1)} %get-tuple-element.58.refs_0_, f32[3,16,8,256]{3,2,1,0:T(8,128)S(1)} %collective-permute-done.14.refs_1_, f32[3,16,8,256]{3,2,1,0:T(8,128)S(1)} %collective-permute-done.15.refs_2_, ...), custom_call_target="tpu_custom_call" | custom-call | flops 10485760 | bytes 4194304 | tf_op jit(solution)/shard_map/finish_part/pallas_call | solution.py:226
  95.1 3.0 %collective-permute-start.19 = (f32[3,16,8,256]{3,2,1,0:T(8,128)S(1)}, f32[3,16,8,256]{3,2,1,0:T(8,128)S(1)}, u32[]{:S(2)}, u32[]{:S(2)}) collective-permute-start(f32[3,16,8,256]{3,2,1,0:T(8,128)S(1)} %get-tuple-element.66), channel_id=1, source_target_pairs={{1,0},{2,1},{3,2},{4,3},{5,4},{6,5},{7,6},{8,7},{9,8},{10,9},{11,1... | collective-permute-start | bytes 1179656 | tf_op jit(solution)/shard_map/ppermute | solution.py:309
  98.1 5.6 %local_part.8.refs_3_ = f32[4,32,8,256]{3,2,1,0:T(8,128)S(1)} custom-call(f32[4,16,8,256]{3,2,1,0:T(8,128)S(1)} %get-tuple-element.64.refs_0_.refs_4_, f32[4,16,8,256]{3,2,1,0:T(8,128)S(1)} %get-tuple-element.69.refs_1_.refs_0_.refs_4_, f32[4,32,8,256]{3,2,1,0:T(8,128)S(1)} %constant_dynamic-update-slice_fusion.refs_2_), custom_call_target="tpu_custom_call" | custom-call | flops 34078720 | bytes 3145728 | tf_op jit(solution)/shard_map/local_part/pallas_call | solution.py:155
  103.8 0.4 collective-permute-done.24.refs_1_
  104.2 2.0 %finish_part.17 = (f32[4,16,8,256]{3,2,1,0:T(8,128)S(1)}, f32[3,16,8,256]{3,2,1,0:T(8,128)S(1)}, f32[3,16,8,256]{3,2,1,0:T(8,128)S(1)}) custom-call(f32[4,16,8,256]{3,2,1,0:T(8,128)S(1)} %get-tuple-element.69.refs_1_.refs_0_.refs_4_, f32[3,16,8,256]{3,2,1,0:T(8,128)S(1)} %collective-permute-done.24.refs_1_, ...), custom_call_target="tpu_custom_call" | custom-call | flops 10485760 | bytes 4194304 | tf_op jit(solution)/shard_map/finish_part/pallas_call | solution.py:226
  106.3 2.5 %collective-permute-start.26 = (f32[3,16,8,256]{3,2,1,0:T(8,128)S(1)}, f32[3,16,8,256]{3,2,1,0:T(8,128)S(1)}, u32[]{:S(2)}, u32[]{:S(2)}) collective-permute-start(f32[3,16,8,256]{3,2,1,0:T(8,128)S(1)} %get-tuple-element.76), channel_id=1, source_target_pairs={{0,1},{1,2},{2,3},{3,4},{4,5},{5,6},{6,7},{7,8},{8,9},{9,10},{10,1... | collective-permute-start | bytes 1179656 | tf_op jit(solution)/shard_map/ppermute | solution.py:304
  108.8 1.6 %collective-permute-start.27 = (f32[3,16,8,256]{3,2,1,0:T(8,128)S(1)}, f32[3,16,8,256]{3,2,1,0:T(8,128)S(1)}, u32[]{:S(2)}, u32[]{:S(2)}) collective-permute-start(f32[3,16,8,256]{3,2,1,0:T(8,128)S(1)} %get-tuple-element.77), channel_id=1, source_target_pairs={{1,0},{2,1},{3,2},{4,3},{5,4},{6,5},{7,6},{8,7},{9,8},{10,9},{11,1... | collective-permute-start | bytes 1179656 | tf_op jit(solution)/shard_map/ppermute | solution.py:309
  110.4 2.3 %collective-permute-done.18.refs_1_ = f32[3,16,8,256]{3,2,1,0:T(8,128)S(1)} collective-permute-done((f32[3,16,8,256]{3,2,1,0:T(8,128)S(1)}, f32[3,16,8,256]{3,2,1,0:T(8,128)S(1)}, u32[]{:S(2)}, u32[]{:S(2)}) %collective-permute-start.18) | collective-permute-done | bytes 393248 | tf_op jit(solution)/shard_map/ppermute | solution.py:304
  112.6 2.0 %finish_part.16 = (f32[4,16,8,256]{3,2,1,0:T(8,128)S(1)}, f32[3,16,8,256]{3,2,1,0:T(8,128)S(1)}, f32[3,16,8,256]{3,2,1,0:T(8,128)S(1)}) custom-call(f32[4,16,8,256]{3,2,1,0:T(8,128)S(1)} %get-tuple-element.64.refs_0_.refs_4_, f32[3,16,8,256]{3,2,1,0:T(8,128)S(1)} %collective-permute-done.18.refs_1_, f32[3,16,8,256]{3,2,1,0:T(8,128)S(1)} %collective-permute-done.19.refs_2_, ...), custom_call_target="tpu_custom_call" | custom-call | flops 10485760 | bytes 4194304 | tf_op jit(solution)/shard_map/finish_part/pallas_call | solution.py:226
  114.7 2.5 %collective-permute-start.22 = (f32[3,16,8,256]{3,2,1,0:T(8,128)S(1)}, f32[3,16,8,256]{3,2,1,0:T(8,128)S(1)}, u32[]{:S(2)}, u32[]{:S(2)}) collective-permute-start(f32[3,16,8,256]{3,2,1,0:T(8,128)S(1)} %get-tuple-element.71), channel_id=1, source_target_pairs={{0,1},{1,2},{2,3},{3,4},{4,5},{5,6},{6,7},{7,8},{8,9},{9,10},{10,1... | collective-permute-start | bytes 1179656 | tf_op jit(solution)/shard_map/ppermute | solution.py:304
  117.2 1.3 copy.7
  118.5 5.6 %local_part.9.refs_3_ = f32[4,32,8,256]{3,2,1,0:T(8,128)S(1)} custom-call(f32[4,16,8,256]{3,2,1,0:T(8,128)S(1)} %get-tuple-element.70.refs_0_, f32[4,16,8,256]{3,2,1,0:T(8,128)S(1)} %get-tuple-element.75.refs_1_.refs_0_, f32[4,32,8,256]{3,2,1,0:T(8,128)S(1)} %constant_dynamic-update-slice_fusion.refs_2_), custom_call_target="tpu_custom_call" | custom-call | flops 34078720 | bytes 3145728 | tf_op jit(solution)/shard_map/local_part/pallas_call | solution.py:155
  124.2 2.0 %finish_part.19 = f32[4,16,8,256]{3,2,1,0:T(8,128)S(1)} custom-call(f32[4,16,8,256]{3,2,1,0:T(8,128)S(1)} %get-tuple-element.75.refs_1_.refs_0_, f32[3,16,8,256]{3,2,1,0:T(8,128)S(1)} %collective-permute-done.26.refs_1_, f32[3,16,8,256]{3,2,1,0:T(8,128)S(1)} %collective-permute-done.27.refs_2_, f32[4,32,8,256]{3,2,1,0:T(8,128)S(1)} %local_part.9.refs_3_, ...), custom_call_target="tpu_custom_call" | custom-call | flops 10485760 | bytes 4194304 | tf_op jit(solution)/shard_map/finish_part/pallas_call | solution.py:226
  126.2 2.4 %collective-permute-done.23.refs_2_ = f32[3,16,8,256]{3,2,1,0:T(8,128)S(1)} collective-permute-done((f32[3,16,8,256]{3,2,1,0:T(8,128)S(1)}, f32[3,16,8,256]{3,2,1,0:T(8,128)S(1)}, u32[]{:S(2)}, u32[]{:S(2)}) %collective-permute-start.23) | collective-permute-done | bytes 393248 | tf_op jit(solution)/shard_map/ppermute | solution.py:309
  128.6 2.0 %finish_part.18 = f32[4,16,8,256]{3,2,1,0:T(8,128)S(1)} custom-call(f32[4,16,8,256]{3,2,1,0:T(8,128)S(1)} %get-tuple-element.70.refs_0_, f32[3,16,8,256]{3,2,1,0:T(8,128)S(1)} %collective-permute-done.22.refs_1_, f32[3,16,8,256]{3,2,1,0:T(8,128)S(1)} %collective-permute-done.23.refs_2_, f32[4,32,8,256]{3,2,1,0:T(8,128)S(1)} %local_part.9.refs_3_, ...), custom_call_target="tpu_custom_call" | custom-call | flops 10485760 | bytes 4194304 | tf_op jit(solution)/shard_map/finish_part/pallas_call | solution.py:226
  130.8 1.3 copy.9
  (33 shorter events, 0.7 us)
Async XLA Ops:
  0.6 1.5 %copy-start = (f32[4,256,256]{2,1,0:T(8,128)S(1)}, f32[4,256,256]{2,1,0:T(8,128)}, u32[]{:S(2)}) copy-start(f32[4,256,256]{2,1,0:T(8,128)} %param.4) | copy-start | bytes 3145732
  3.4 6.0 %collective-permute-start = (f32[1,32,8,256]{3,2,1,0:T(8,128)S(1)}, f32[1,32,8,256]{3,2,1,0:T(8,128)S(1)}, u32[]{:S(2)}, u32[]{:S(2)}) collective-permute-start(f32[1,32,8,256]{3,2,1,0:T(8,128)S(1)} %get-tuple-element.94.high_ref), channel_id=1, source_target_pairs={{0,1},{1,2},{2,3},{3,4},{4,5},{5,6},{6,7},{7,8},{8,9},{9,10},{10,1... | collective-permute-start | bytes 786440 | tf_op jit(solution)/shard_map/ppermute | solution.py:304
  6.0 8.6 %collective-permute-start.1 = (f32[1,32,8,256]{3,2,1,0:T(8,128)S(1)}, f32[1,32,8,256]{3,2,1,0:T(8,128)S(1)}, u32[]{:S(2)}, u32[]{:S(2)}) collective-permute-start(f32[1,32,8,256]{3,2,1,0:T(8,128)S(1)} %get-tuple-element.95.low_ref), channel_id=1, source_target_pairs={{1,0},{2,1},{3,2},{4,3},{5,4},{6,5},{7,6},{8,7},{9,8},{10,9},{11,1... | collective-permute-start | bytes 786440 | tf_op jit(solution)/shard_map/ppermute | solution.py:309
  14.6 1.2 copy-start.1
  14.8 6.2 %collective-permute-start.2 = (f32[1,32,8,256]{3,2,1,0:T(8,128)S(1)}, f32[1,32,8,256]{3,2,1,0:T(8,128)S(1)}, u32[]{:S(2)}, u32[]{:S(2)}) collective-permute-start(f32[1,32,8,256]{3,2,1,0:T(8,128)S(1)} %get-tuple-element.92.high_ref), channel_id=1, source_target_pairs={{0,1},{1,2},{2,3},{3,4},{4,5},{5,6},{6,7},{7,8},{8,9},{9,10},{10,1... | collective-permute-start | bytes 786440 | tf_op jit(solution)/shard_map/ppermute | solution.py:304
  14.8 8.7 %collective-permute-start.3 = (f32[1,32,8,256]{3,2,1,0:T(8,128)S(1)}, f32[1,32,8,256]{3,2,1,0:T(8,128)S(1)}, u32[]{:S(2)}, u32[]{:S(2)}) collective-permute-start(f32[1,32,8,256]{3,2,1,0:T(8,128)S(1)} %get-tuple-element.93.low_ref), channel_id=1, source_target_pairs={{1,0},{2,1},{3,2},{4,3},{5,4},{6,5},{7,6},{8,7},{9,8},{10,9},{11,1... | collective-permute-start | bytes 786440 | tf_op jit(solution)/shard_map/ppermute | solution.py:309
  23.6 13.8 %collective-permute-start.4 = (f32[1,32,8,256]{3,2,1,0:T(8,128)S(1)}, f32[1,32,8,256]{3,2,1,0:T(8,128)S(1)}, u32[]{:S(2)}, u32[]{:S(2)}) collective-permute-start(f32[1,32,8,256]{3,2,1,0:T(8,128)S(1)} %get-tuple-element.90.high_ref), channel_id=1, source_target_pairs={{0,1},{1,2},{2,3},{3,4},{4,5},{5,6},{6,7},{7,8},{8,9},{9,10},{10,1... | collective-permute-start | bytes 786440 | tf_op jit(solution)/shard_map/ppermute | solution.py:304
  23.6 13.7 %collective-permute-start.5 = (f32[1,32,8,256]{3,2,1,0:T(8,128)S(1)}, f32[1,32,8,256]{3,2,1,0:T(8,128)S(1)}, u32[]{:S(2)}, u32[]{:S(2)}) collective-permute-start(f32[1,32,8,256]{3,2,1,0:T(8,128)S(1)} %get-tuple-element.91.low_ref), channel_id=1, source_target_pairs={{1,0},{2,1},{3,2},{4,3},{5,4},{6,5},{7,6},{8,7},{9,8},{10,9},{11,1... | collective-permute-start | bytes 786440 | tf_op jit(solution)/shard_map/ppermute | solution.py:309
  24.3 33.5 %collective-permute-start.9 = (f32[3,16,8,256]{3,2,1,0:T(8,128)S(1)}, f32[3,16,8,256]{3,2,1,0:T(8,128)S(1)}, u32[]{:S(2)}, u32[]{:S(2)}) collective-permute-start(f32[3,16,8,256]{3,2,1,0:T(8,128)S(1)} %get-tuple-element.78), channel_id=1, source_target_pairs={{1,0},{2,1},{3,2},{4,3},{5,4},{6,5},{7,6},{8,7},{9,8},{10,9},{11,1... | collective-permute-start | bytes 1179656 | tf_op jit(solution)/shard_map/ppermute | solution.py:309
  26.7 28.4 %collective-permute-start.13 = (f32[3,16,8,256]{3,2,1,0:T(8,128)S(1)}, f32[3,16,8,256]{3,2,1,0:T(8,128)S(1)}, u32[]{:S(2)}, u32[]{:S(2)}) collective-permute-start(f32[3,16,8,256]{3,2,1,0:T(8,128)S(1)} %get-tuple-element.79), channel_id=1, source_target_pairs={{1,0},{2,1},{3,2},{4,3},{5,4},{6,5},{7,6},{8,7},{9,8},{10,9},{11,1... | collective-permute-start | bytes 1179656 | tf_op jit(solution)/shard_map/ppermute | solution.py:309
  27.1 28.0 %collective-permute-start.12 = (f32[3,16,8,256]{3,2,1,0:T(8,128)S(1)}, f32[3,16,8,256]{3,2,1,0:T(8,128)S(1)}, u32[]{:S(2)}, u32[]{:S(2)}) collective-permute-start(f32[3,16,8,256]{3,2,1,0:T(8,128)S(1)} %get-tuple-element.80), channel_id=1, source_target_pairs={{0,1},{1,2},{2,3},{3,4},{4,5},{5,6},{6,7},{7,8},{8,9},{9,10},{10,1... | collective-permute-start | bytes 1179656 | tf_op jit(solution)/shard_map/ppermute | solution.py:304
  37.5 9.7 %collective-permute-start.6 = (f32[1,32,8,256]{3,2,1,0:T(8,128)S(1)}, f32[1,32,8,256]{3,2,1,0:T(8,128)S(1)}, u32[]{:S(2)}, u32[]{:S(2)}) collective-permute-start(f32[1,32,8,256]{3,2,1,0:T(8,128)S(1)} %get-tuple-element.88.high_ref), channel_id=1, source_target_pairs={{0,1},{1,2},{2,3},{3,4},{4,5},{5,6},{6,7},{7,8},{8,9},{9,10},{10,1... | collective-permute-start | bytes 786440 | tf_op jit(solution)/shard_map/ppermute | solution.py:304
  40.0 14.8 %collective-permute-start.7 = (f32[1,32,8,256]{3,2,1,0:T(8,128)S(1)}, f32[1,32,8,256]{3,2,1,0:T(8,128)S(1)}, u32[]{:S(2)}, u32[]{:S(2)}) collective-permute-start(f32[1,32,8,256]{3,2,1,0:T(8,128)S(1)} %get-tuple-element.89.low_ref), channel_id=1, source_target_pairs={{1,0},{2,1},{3,2},{4,3},{5,4},{6,5},{7,6},{8,7},{9,8},{10,9},{11,1... | collective-permute-start | bytes 786440 | tf_op jit(solution)/shard_map/ppermute | solution.py:309
  47.2 10.6 %collective-permute-start.8 = (f32[3,16,8,256]{3,2,1,0:T(8,128)S(1)}, f32[3,16,8,256]{3,2,1,0:T(8,128)S(1)}, u32[]{:S(2)}, u32[]{:S(2)}) collective-permute-start(f32[3,16,8,256]{3,2,1,0:T(8,128)S(1)} %get-tuple-element.81), channel_id=1, source_target_pairs={{0,1},{1,2},{2,3},{3,4},{4,5},{5,6},{6,7},{7,8},{8,9},{9,10},{10,1... | collective-permute-start | bytes 1179656 | tf_op jit(solution)/shard_map/ppermute | solution.py:304
  57.3 11.1 %collective-permute-start.16 = (f32[3,16,8,256]{3,2,1,0:T(8,128)S(1)}, f32[3,16,8,256]{3,2,1,0:T(8,128)S(1)}, u32[]{:S(2)}, u32[]{:S(2)}) collective-permute-start(f32[3,16,8,256]{3,2,1,0:T(8,128)S(1)} %get-tuple-element.61), channel_id=1, source_target_pairs={{0,1},{1,2},{2,3},{3,4},{4,5},{5,6},{6,7},{7,8},{8,9},{9,10},{10,1... | collective-permute-start | bytes 1179656 | tf_op jit(solution)/shard_map/ppermute | solution.py:304
  57.3 11.0 %collective-permute-start.17 = (f32[3,16,8,256]{3,2,1,0:T(8,128)S(1)}, f32[3,16,8,256]{3,2,1,0:T(8,128)S(1)}, u32[]{:S(2)}, u32[]{:S(2)}) collective-permute-start(f32[3,16,8,256]{3,2,1,0:T(8,128)S(1)} %get-tuple-element.62), channel_id=1, source_target_pairs={{1,0},{2,1},{3,2},{4,3},{5,4},{6,5},{7,6},{8,7},{9,8},{10,9},{11,1... | collective-permute-start | bytes 1179656 | tf_op jit(solution)/shard_map/ppermute | solution.py:309
  60.0 16.8 %collective-permute-start.10 = (f32[3,16,8,256]{3,2,1,0:T(8,128)S(1)}, f32[3,16,8,256]{3,2,1,0:T(8,128)S(1)}, u32[]{:S(2)}, u32[]{:S(2)}) collective-permute-start(f32[3,16,8,256]{3,2,1,0:T(8,128)S(1)} %get-tuple-element.55), channel_id=1, source_target_pairs={{0,1},{1,2},{2,3},{3,4},{4,5},{5,6},{6,7},{7,8},{8,9},{9,10},{10,1... | collective-permute-start | bytes 1179656 | tf_op jit(solution)/shard_map/ppermute | solution.py:304
  61.3 15.5 %collective-permute-start.11 = (f32[3,16,8,256]{3,2,1,0:T(8,128)S(1)}, f32[3,16,8,256]{3,2,1,0:T(8,128)S(1)}, u32[]{:S(2)}, u32[]{:S(2)}) collective-permute-start(f32[3,16,8,256]{3,2,1,0:T(8,128)S(1)} %get-tuple-element.56), channel_id=1, source_target_pairs={{1,0},{2,1},{3,2},{4,3},{5,4},{6,5},{7,6},{8,7},{9,8},{10,9},{11,1... | collective-permute-start | bytes 1179656 | tf_op jit(solution)/shard_map/ppermute | solution.py:309
  70.5 16.6 %collective-permute-start.20 = (f32[3,16,8,256]{3,2,1,0:T(8,128)S(1)}, f32[3,16,8,256]{3,2,1,0:T(8,128)S(1)}, u32[]{:S(2)}, u32[]{:S(2)}) collective-permute-start(f32[3,16,8,256]{3,2,1,0:T(8,128)S(1)} %get-tuple-element.67), channel_id=1, source_target_pairs={{0,1},{1,2},{2,3},{3,4},{4,5},{5,6},{6,7},{7,8},{8,9},{9,10},{10,1... | collective-permute-start | bytes 1179656 | tf_op jit(solution)/shard_map/ppermute | solution.py:304
  73.0 15.6 %collective-permute-start.21 = (f32[3,16,8,256]{3,2,1,0:T(8,128)S(1)}, f32[3,16,8,256]{3,2,1,0:T(8,128)S(1)}, u32[]{:S(2)}, u32[]{:S(2)}) collective-permute-start(f32[3,16,8,256]{3,2,1,0:T(8,128)S(1)} %get-tuple-element.68), channel_id=1, source_target_pairs={{1,0},{2,1},{3,2},{4,3},{5,4},{6,5},{7,6},{8,7},{9,8},{10,9},{11,1... | collective-permute-start | bytes 1179656 | tf_op jit(solution)/shard_map/ppermute | solution.py:309
  78.9 12.5 %collective-permute-start.14 = (f32[3,16,8,256]{3,2,1,0:T(8,128)S(1)}, f32[3,16,8,256]{3,2,1,0:T(8,128)S(1)}, u32[]{:S(2)}, u32[]{:S(2)}) collective-permute-start(f32[3,16,8,256]{3,2,1,0:T(8,128)S(1)} %get-tuple-element.59), channel_id=1, source_target_pairs={{0,1},{1,2},{2,3},{3,4},{4,5},{5,6},{6,7},{7,8},{8,9},{9,10},{10,1... | collective-permute-start | bytes 1179656 | tf_op jit(solution)/shard_map/ppermute | solution.py:304
  81.5 11.4 %collective-permute-start.15 = (f32[3,16,8,256]{3,2,1,0:T(8,128)S(1)}, f32[3,16,8,256]{3,2,1,0:T(8,128)S(1)}, u32[]{:S(2)}, u32[]{:S(2)}) collective-permute-start(f32[3,16,8,256]{3,2,1,0:T(8,128)S(1)} %get-tuple-element.60), channel_id=1, source_target_pairs={{1,0},{2,1},{3,2},{4,3},{5,4},{6,5},{7,6},{8,7},{9,8},{10,9},{11,1... | collective-permute-start | bytes 1179656 | tf_op jit(solution)/shard_map/ppermute | solution.py:309
  90.8 13.4 %collective-permute-start.24 = (f32[3,16,8,256]{3,2,1,0:T(8,128)S(1)}, f32[3,16,8,256]{3,2,1,0:T(8,128)S(1)}, u32[]{:S(2)}, u32[]{:S(2)}) collective-permute-start(f32[3,16,8,256]{3,2,1,0:T(8,128)S(1)} %get-tuple-element.73), channel_id=1, source_target_pairs={{0,1},{1,2},{2,3},{3,4},{4,5},{5,6},{6,7},{7,8},{8,9},{9,10},{10,1... | collective-permute-start | bytes 1179656 | tf_op jit(solution)/shard_map/ppermute | solution.py:304
  91.1 13.1 %collective-permute-start.25 = (f32[3,16,8,256]{3,2,1,0:T(8,128)S(1)}, f32[3,16,8,256]{3,2,1,0:T(8,128)S(1)}, u32[]{:S(2)}, u32[]{:S(2)}) collective-permute-start(f32[3,16,8,256]{3,2,1,0:T(8,128)S(1)} %get-tuple-element.74), channel_id=1, source_target_pairs={{1,0},{2,1},{3,2},{4,3},{5,4},{6,5},{7,6},{8,7},{9,8},{10,9},{11,1... | collective-permute-start | bytes 1179656 | tf_op jit(solution)/shard_map/ppermute | solution.py:309
  95.0 17.6 %collective-permute-start.18 = (f32[3,16,8,256]{3,2,1,0:T(8,128)S(1)}, f32[3,16,8,256]{3,2,1,0:T(8,128)S(1)}, u32[]{:S(2)}, u32[]{:S(2)}) collective-permute-start(f32[3,16,8,256]{3,2,1,0:T(8,128)S(1)} %get-tuple-element.65), channel_id=1, source_target_pairs={{0,1},{1,2},{2,3},{3,4},{4,5},{5,6},{6,7},{7,8},{8,9},{9,10},{10,1... | collective-permute-start | bytes 1179656 | tf_op jit(solution)/shard_map/ppermute | solution.py:304
  95.1 17.5 %collective-permute-start.19 = (f32[3,16,8,256]{3,2,1,0:T(8,128)S(1)}, f32[3,16,8,256]{3,2,1,0:T(8,128)S(1)}, u32[]{:S(2)}, u32[]{:S(2)}) collective-permute-start(f32[3,16,8,256]{3,2,1,0:T(8,128)S(1)} %get-tuple-element.66), channel_id=1, source_target_pairs={{1,0},{2,1},{3,2},{4,3},{5,4},{6,5},{7,6},{8,7},{9,8},{10,9},{11,1... | collective-permute-start | bytes 1179656 | tf_op jit(solution)/shard_map/ppermute | solution.py:309
  106.3 17.9 %collective-permute-start.26 = (f32[3,16,8,256]{3,2,1,0:T(8,128)S(1)}, f32[3,16,8,256]{3,2,1,0:T(8,128)S(1)}, u32[]{:S(2)}, u32[]{:S(2)}) collective-permute-start(f32[3,16,8,256]{3,2,1,0:T(8,128)S(1)} %get-tuple-element.76), channel_id=1, source_target_pairs={{0,1},{1,2},{2,3},{3,4},{4,5},{5,6},{6,7},{7,8},{8,9},{9,10},{10,1... | collective-permute-start | bytes 1179656 | tf_op jit(solution)/shard_map/ppermute | solution.py:304
  108.8 15.4 %collective-permute-start.27 = (f32[3,16,8,256]{3,2,1,0:T(8,128)S(1)}, f32[3,16,8,256]{3,2,1,0:T(8,128)S(1)}, u32[]{:S(2)}, u32[]{:S(2)}) collective-permute-start(f32[3,16,8,256]{3,2,1,0:T(8,128)S(1)} %get-tuple-element.77), channel_id=1, source_target_pairs={{1,0},{2,1},{3,2},{4,3},{5,4},{6,5},{7,6},{8,7},{9,8},{10,9},{11,1... | collective-permute-start | bytes 1179656 | tf_op jit(solution)/shard_map/ppermute | solution.py:309
  114.7 11.5 %collective-permute-start.22 = (f32[3,16,8,256]{3,2,1,0:T(8,128)S(1)}, f32[3,16,8,256]{3,2,1,0:T(8,128)S(1)}, u32[]{:S(2)}, u32[]{:S(2)}) collective-permute-start(f32[3,16,8,256]{3,2,1,0:T(8,128)S(1)} %get-tuple-element.71), channel_id=1, source_target_pairs={{0,1},{1,2},{2,3},{3,4},{4,5},{5,6},{6,7},{7,8},{8,9},{9,10},{10,1... | collective-permute-start | bytes 1179656 | tf_op jit(solution)/shard_map/ppermute | solution.py:304
  117.2 11.4 %collective-permute-start.23 = (f32[3,16,8,256]{3,2,1,0:T(8,128)S(1)}, f32[3,16,8,256]{3,2,1,0:T(8,128)S(1)}, u32[]{:S(2)}, u32[]{:S(2)}) collective-permute-start(f32[3,16,8,256]{3,2,1,0:T(8,128)S(1)} %get-tuple-element.72), channel_id=1, source_target_pairs={{1,0},{2,1},{3,2},{4,3},{5,4},{6,5},{7,6},{8,7},{9,8},{10,9},{11,1... | collective-permute-start | bytes 1179656 | tf_op jit(solution)/shard_map/ppermute | solution.py:309

commit v3 on v2

--- a/solution.py
+++ b/solution.py
@@ -10,7 +10,7 @@
 SWEEPS = 4
 REINIT = 2
 SUB = 8
-CHUNKS = 2
+SPLIT = (0, 4, 8)
 
 weno_eps = 1e-06
 advect_step = 0.15
@@ -116,9 +116,10 @@
     else:
         vel_ref, out_ref, padded = refs[chunks:]
     tiles = padded.shape[0] - 6
-    per = tiles // chunks
-    for index in range(chunks):
-        padded[3 + index * per : 3 + (index + 1) * per] = u_refs[index][0]
+    start = 3
+    for ref in u_refs:
+        padded[start : start + ref.shape[1]] = ref[0]
+        start += ref.shape[1]
     first = padded[3]
     final = padded[tiles + 2]
     for step in range(3):
@@ -145,17 +146,16 @@
 
 
 def local_part(pieces, velocity, block=16):
-    layers, per, _, lanes = pieces[0].shape
-    tiles = per * len(pieces)
+    layers, _, _, lanes = pieces[0].shape
+    tiles = sum(piece.shape[1] for piece in pieces)
     both = velocity is None
     whole = pl.BlockSpec((1, tiles, SUB, lanes), lambda i: (i, 0, 0, 0))
-    piece = pl.BlockSpec((1, per, SUB, lanes), lambda i: (i, 0, 0, 0))
     shape = jax.ShapeDtypeStruct((layers, tiles, SUB, lanes), jnp.float32)
     cells = layers * tiles * SUB * lanes
     return pl.pallas_call(
         functools.partial(local_body, len(pieces), both, block),
         grid=(layers,),
-        in_specs=[piece] * len(pieces) + ([] if both else [whole]),
+        in_specs=[pl.BlockSpec((1,) + p.shape[1:], lambda i: (i, 0, 0, 0)) for p in pieces] + ([] if both else [whole]),
         out_specs=(whole, whole) if both else whole,
         out_shape=(shape, shape) if both else shape,
         scratch_shapes=[pltpu.VMEM((tiles + 6, SUB, lanes), jnp.float32)],
@@ -166,8 +166,9 @@
 
 
 def finish_body(kind, last, *refs):
-    u_ref, left_ref, right_ref = refs[:3]
-    rest = list(refs[3:])
+    parity_ref, u_ref, far_ref, near_ref = refs[:4]
+    rest = list(refs[4:])
+    even = parity_ref[0] == 0
     layers, tiles = u_ref.shape[0], u_ref.shape[1]
     if kind == "first":
         rise_ref, fall_ref, vel_ref = rest[:3]
@@ -181,7 +182,10 @@
 
     def loop(t, carry):
         own = [u_ref[i, t] for i in range(layers)]
-        cells = [left_ref[i, t] for i in range(3)] + own + [right_ref[i, t] for i in range(3)]
+        far = [far_ref[i, t] for i in range(3)]
+        near = [near_ref[i, t] for i in range(3)]
+        cells = [jnp.where(even, a, b) for a, b in zip(far, near)] + own + [jnp.where(even, b, a) for a, b in zip(far, near)]
+        made = []
         pairs = along_line(cells)
         for i in range(layers):
             vel = vel_ref[i, t]
@@ -202,20 +206,20 @@
                 sign = vel * lax.rsqrt(vel * vel + 1.0)
                 new = own[i] - reinit_step * (sign * (height - 1.0))
             out_ref[i, t] = new
-            if not last:
-                if i < 3:
-                    rest[1][i, t] = new
-                if i >= layers - 3:
-                    rest[2][i - (layers - 3), t] = new
+            made.append(new)
+        if not last:
+            for i in range(3):
+                rest[1][i, t] = jnp.where(even, made[i], made[layers - 3 + i])
+                rest[2][i, t] = jnp.where(even, made[layers - 3 + i], made[i])
         return carry
 
     lax.fori_loop(0, tiles, loop, 0)
 
 
-def finish_part(kind, last, index, u, left, right, others, block=4):
+def finish_part(kind, last, start, parity, u, far, near, others, block=4):
     layers, per, _, lanes = u.shape
     block = min(block, per)
-    shift = index * (per // block)
+    shift = start // block
     own = pl.BlockSpec((layers, block, SUB, lanes), lambda i: (0, i, 0, 0))
     side = pl.BlockSpec((3, block, SUB, lanes), lambda i: (0, i, 0, 0))
     moved = pl.BlockSpec((layers, block, SUB, lanes), lambda i: (0, i + shift, 0, 0))
@@ -226,67 +230,64 @@
     return pl.pallas_call(
         functools.partial(finish_body, kind, last),
         grid=(per // block,),
-        in_specs=[own, side, side] + specs,
+        in_specs=[pl.BlockSpec(memory_space=pltpu.SMEM), own, side, side] + specs,
         out_specs=own if last else (own, side, side),
         out_shape=shape if last else (shape, side_shape, side_shape),
         compiler_params=pltpu.CompilerParams(vmem_limit_bytes=24 * 1024 * 1024),
         cost_estimate=pl.CostEstimate(flops=80 * cells, bytes_accessed=32 * cells, transcendentals=6 * cells),
         name="finish_part",
-    )(u, left, right, *others)
-
-
-def sweep_body(low_ref, mid_ref, high_ref, weight_ref, fixed_ref, low_out, mid_out, high_out):
-    tiles, lanes = low_ref.shape[1], low_ref.shape[3]
-    layers = mid_ref.shape[0] + 2
-
-    def at(i, t):
-        if i == 0:
-            return low_ref[0, t]
-        if i == layers - 1:
-            return high_ref[0, t]
-        return mid_ref[i - 1, t]
-
-    def one(i, t, cell, before, after):
-        total = before + after + pltpu.roll(cell, lanes - 1, 1) + pltpu.roll(cell, 1, 1)
-        if i > 0:
-            total = total + at(i - 1, t)
-        if i < layers - 1:
-            total = total + at(i + 1, t)
-        weight = weight_ref[i, t]
-        new = weight * fixed_ref[i, t] + (1.0 - weight) * (total * (1.0 / 6.0))
-        if i == 0:
-            low_out[0, t] = new
-        elif i == layers - 1:
-            high_out[0, t] = new
-        else:
-            mid_out[i - 1, t] = new
-
+    )(parity, u, far, near, *others)
+
+
+def sweep_body(parity_ref, far_ref, mid_ref, near_ref, weight_ref, fixed_ref, far_out, mid_out, near_out, padded):
+    layers, tiles, lanes = weight_ref.shape[0], weight_ref.shape[1], weight_ref.shape[3]
+    even = parity_ref[0] == 0
+    padded[jnp.where(even, 0, layers - 1), 1 : tiles + 1] = far_ref[0]
+    padded[jnp.where(even, layers - 1, 0), 1 : tiles + 1] = near_ref[0]
+    for i in range(1, layers - 1):
+        padded[i, 1 : tiles + 1] = mid_ref[i - 1]
     for i in range(layers):
-        first, final = at(i, 0), at(i, tiles - 1)
-        one(i, 0, first, edge_tile(final, first, True), at(i, 1))
-        one(i, tiles - 1, final, at(i, tiles - 2), edge_tile(first, final, False))
+        first, final = padded[i, 1], padded[i, tiles]
+        padded[i, 0] = edge_tile(final, first, True)
+        padded[i, tiles + 1] = edge_tile(first, final, False)
 
     def loop(t, carry):
+        cells = [padded[i, t + 1] for i in range(layers)]
+        ends = []
         for i in range(layers):
-            one(i, t, at(i, t), at(i, t - 1), at(i, t + 1))
+            total = padded[i, t] + padded[i, t + 2]
+            total = total + pltpu.roll(cells[i], lanes - 1, 1) + pltpu.roll(cells[i], 1, 1)
+            if i > 0:
+                total = total + cells[i - 1]
+            if i < layers - 1:
+                total = total + cells[i + 1]
+            weight = weight_ref[i, t]
+            new = weight * fixed_ref[i, t] + (1.0 - weight) * (total * (1.0 / 6.0))
+            if 0 < i < layers - 1:
+                mid_out[i - 1, t] = new
+            else:
+                ends.append(new)
+        far_out[0, t] = jnp.where(even, ends[0], ends[1])
+        near_out[0, t] = jnp.where(even, ends[1], ends[0])
         return carry
 
-    lax.fori_loop(1, tiles - 1, loop, 0, unroll=5)
-
-
-def sweep_part(low, mid, high, weight, fixed):
+    lax.fori_loop(0, tiles, loop, 0, unroll=4)
+
+
+def sweep_part(parity, far, mid, near, weight, fixed):
     cells = weight.size
-    shapes = [jax.ShapeDtypeStruct(v.shape, jnp.float32) for v in (low, mid, high)]
+    layers, tiles, _, lanes = weight.shape
     vmem = pl.BlockSpec(memory_space=pltpu.VMEM)
     return pl.pallas_call(
         sweep_body,
-        in_specs=[vmem] * 5,
+        in_specs=[pl.BlockSpec(memory_space=pltpu.SMEM)] + [vmem] * 5,
         out_specs=(vmem, vmem, vmem),
-        out_shape=tuple(shapes),
+        out_shape=tuple(jax.ShapeDtypeStruct(v.shape, jnp.float32) for v in (far, mid, near)),
+        scratch_shapes=[pltpu.VMEM((layers, tiles + 2, SUB, lanes), jnp.float32)],
         compiler_params=pltpu.CompilerParams(vmem_limit_bytes=24 * 1024 * 1024),
         cost_estimate=pl.CostEstimate(flops=12 * cells, bytes_accessed=16 * cells, transcendentals=0),
         name="sweep_part",
-    )(low, mid, high, weight, fixed)
+    )(parity, far, mid, near, weight, fixed)
 
 
 def fold_rows(array):
@@ -299,14 +300,15 @@
     return array.transpose(0, 2, 1, 3).reshape(layers, tiles * SUB, lanes)
 
 
-def to_next(array):
+def swap_far(array):
     count = lax.axis_size("gx")
-    return lax.ppermute(array, "gx", [(i, (i + 1) % count) for i in range(count)])
-
-
-def to_previous(array):
+    odd = range(1, count, 2)
+    return lax.ppermute(array, "gx", [(i, (i + 1) % count) for i in odd] + [((i + 1) % count, i) for i in odd])
+
+
+def swap_near(array):
     count = lax.axis_size("gx")
-    return lax.ppermute(array, "gx", [((i + 1) % count, i) for i in range(count)])
+    return lax.ppermute(array, "gx", [(i, i + 1 - 2 * (i % 2)) for i in range(count)])
 
 
 def per_device(level_set, sensitivity, band):
@@ -314,54 +316,65 @@
     weight = fold_rows(band).astype(jnp.float32)
     fixed = weight * fold_rows(sensitivity)
     level = fold_rows(level_set)
-    per = level.shape[1] // CHUNKS
-    pieces = [level[:, i * per : (i + 1) * per] for i in range(CHUNKS)]
-    heads = [piece[:3] for piece in pieces]
-    tails = [piece[layers - 3 :] for piece in pieces]
-
-    low, mid, high = fixed[:1], fixed[1 : layers - 1], fixed[layers - 1 :]
-    low_open = (1.0 - weight[:1]) * (1.0 / 6.0)
-    high_open = (1.0 - weight[layers - 1 :]) * (1.0 / 6.0)
+    bounds = [level.shape[1] * part // 8 for part in SPLIT]
+
+    def cut(array):
+        return [array[:, start:stop] for start, stop in zip(bounds, bounds[1:])]
+
+    pieces = cut(level)
+    parity = lax.rem(lax.axis_index("gx"), 2)
+    even = parity == 0
+    parity = parity.astype(jnp.int32).reshape(1)
+
+    def order(first, second):
+        return jnp.where(even, first, second), jnp.where(even, second, first)
+
+    sides = list(zip(*[cut(side) for side in order(level[:3], level[layers - 3 :])]))
+
+    edges = [slice(0, 1), slice(layers - 1, layers)]
+    far, near = order(*[fold_rows(band[e].astype(jnp.float32) * sensitivity[e]) for e in edges])
+    far_open, near_open = order(*[(1.0 - fold_rows(band[e]).astype(jnp.float32)) * (1.0 / 6.0) for e in edges])
+    mid = fixed[1 : layers - 1]
+    halos = [(swap_far(side[0]), swap_near(side[1])) for side in sides]
+    rise, fall = local_part([level], None)
     for sweep in range(SWEEPS):
-        from_previous = to_next(high)
-        from_next = to_previous(low)
-        if sweep == 0:
-            halos = [(to_next(tails[i]), to_previous(heads[i])) for i in range(CHUNKS)]
-        low_part, mid, high_part = sweep_part(low, mid, high, weight, fixed)
-        low = low_part + low_open * from_previous
-        high = high_part + high_open * from_next
+        from_far, from_near = swap_far(far), swap_near(near)
+        far_part, mid, near_part = sweep_part(parity, far, mid, near, weight, fixed)
+        if sweep == 1:
+            mid, rise, fall = lax.optimization_barrier((mid, rise, fall))
+        far = far_part + far_open * from_far
+        near = near_part + near_open * from_near
+    low, high = order(far, near)
     speed = jnp.concatenate([low, mid, high], axis=0)
 
-    rise, fall = local_part([level], None)
     kinds = ["first", "second", "third"] + ["reinit"] * REINIT
     base = level
     marker = None
     for number, kind in enumerate(kinds):
         last = number == len(kinds) - 1
         if number > 0:
-            halos = [(to_next(tails[i]), to_previous(heads[i])) for i in range(CHUNKS)]
+            halos = [(swap_far(far), swap_near(near)) for far, near in sides]
             if kind == "reinit" and marker is None:
                 marker = pieces
             if kind == "reinit":
-                local = local_part(pieces, jnp.concatenate(marker, axis=1) if CHUNKS > 1 else marker[0])
+                local = local_part(pieces, jnp.concatenate(marker, axis=1))
             else:
                 local = local_part(pieces, speed)
         results = []
-        for i in range(CHUNKS):
+        for i in range(len(pieces)):
             if kind == "first":
                 others = (rise, fall, speed)
             elif kind == "reinit":
                 others = (local, marker[i])
             else:
                 others = (local, speed, level)
-            results.append(finish_part(kind, last, i, pieces[i], halos[i][0], halos[i][1], others))
+            results.append(finish_part(kind, last, bounds[i], parity, pieces[i], halos[i][0], halos[i][1], others))
         if last:
             pieces = results
         else:
             pieces = [r[0] for r in results]
-            heads = [r[1] for r in results]
-            tails = [r[2] for r in results]
-    updated = jnp.concatenate(pieces, axis=1) if CHUNKS > 1 else pieces[0]
+            sides = [r[1:] for r in results]
+    updated = jnp.concatenate(pieces, axis=1)
     return (unfold_rows(speed), unfold_rows(updated))
 
 

time: 134 us -> 128 us (0.955); the launches traced: 132 us -> 128 us
  waiting for transfers between devices: 39 us -> 30.9 us
  starting transfers between devices: 30.1 us -> 31.7 us
    ppermute x28, waiting for transfers between devices: 39 us -> 30.9 us  [the longest x14 30.8 us: swap_far(): lax.ppermute(array, 'gx', [(i, (i + 1) % count) for i in odd] + [((i + 1)...]
    select_n x0 -> x3, other arithmetic: none -> 1.78 us  [order(): return (jnp.where(even, first, second), jnp.where(even, second, first))]
    ppermute x28, starting transfers between devices: 30.1 us -> 31.7 us  [the longest x14 16.5 us: swap_near(): lax.ppermute(array, 'gx', [(i, i + 1 - 2 * (i % 2)) for i in range(count)])]
  transfers between devices with their start and end apart: 28 -> 28, of which waited for: 14 -> 9; matrix products, arithmetic and copies ran while one was open for 2% -> 5% of each run, Pallas kernels for 39% -> 41%
where the time goes in v3:
time: 128 us
  Pallas kernels  54.8 us (43%)
  starting transfers between devices  31.7 us (25%)
  waiting for transfers between devices  30.9 us (24%)
  local copies, waits for them, and re-layouts  5.06 us (4%)
  other arithmetic  4.36 us (3%)
    ppermute x14, waiting for transfers between devices, swap_far(): lax.ppermute(array, 'gx', [(i, (i + 1) % count) for i in odd] + [((i + 1)...  30.8 us
    pallas_call x5, Pallas kernels, local_part(): pl.pallas_call(functools.partial(local_body, len(pieces), both, block), g...  28.7 us
    pallas_call x10, Pallas kernels, finish_part(): pl.pallas_call(functools.partial(finish_body, kind, last), grid=(per // b...  20.9 us
    ppermute x14, starting transfers between devices, swap_near(): lax.ppermute(array, 'gx', [(i, i + 1 - 2 * (i % 2)) for i in range(count)])  16.5 us
    ppermute x14, starting transfers between devices, swap_far(): lax.ppermute(array, 'gx', [(i, (i + 1) % count) for i in odd] + [((i + 1)...  15.2 us
    pallas_call x4, Pallas kernels, sweep_part(): pl.pallas_call(sweep_body, in_specs=[pl.BlockSpec(memory_space=pltpu.SMEM...  5.15 us
    transpose x2, local copies, waits for them, and re-layouts, unfold_rows(): return array.transpose(0, 2, 1, 3).reshape(layers, tiles * SUB, lanes)  2.59 us
  transfers between devices with their start and end apart: 28, of which 9 were waited for; matrix products, arithmetic and copies ran while one was open for 5% of the time, Pallas kernels for 41%

profile of v3, /device:TPU:1, one launch (start us, length us, event | category | flops | bytes accessed | tf_op | source)
XLA Modules:
  0.0 127.8 jit_solution(13030369211898935703)
XLA Ops:
  0.6 1.3 %fusion.9 = (f32[1,256,256]{2,1,0:T(8,128)S(1)}, f32[1,256,256]{2,1,0:T(8,128)S(1)}, f32[1,256,256]{2,1,0:T(8,128)S(1)}, f32[1,256,256]{2,1,0:T(8,128)S(1)}) fusion(s32[4,256,256]{2,1,0:T(8,128)} %param.5, pred[]{:T(512)S(6)} %eq.3, f32[4,256,256]{2,1,0:T(8,128)} %param.4), kind=kLoop, calls=%fused_computation.30 | loop fusion | flops 786432 | bytes 2097153 | tf_op jit(solution)/shard_map/jit(_where)/select_n | solution.py:330
  1.9 0.3 copy_bitcast_fusion.2
  2.3 2.7 %collective-permute-start = (f32[1,32,8,256]{3,2,1,0:T(8,128)S(1)}, f32[1,32,8,256]{3,2,1,0:T(8,128)S(1)}, u32[]{:S(2)}, u32[]{:S(2)}) collective-permute-start(f32[1,32,8,256]{3,2,1,0:T(8,128)S(1)} %get-tuple-element.103.far_ref), channel_id=1, source_target_pairs={{1,2},{3,4},{5,6},{7,8},{9,10},{11,12},{13,14},{15,0},{2,1},{4,3},... | collective-permute-start | bytes 786440 | tf_op jit(solution)/shard_map/ppermute | solution.py:306
  4.9 2.9 %collective-permute-start.1 = (f32[1,32,8,256]{3,2,1,0:T(8,128)S(1)}, f32[1,32,8,256]{3,2,1,0:T(8,128)S(1)}, u32[]{:S(2)}, u32[]{:S(2)}) collective-permute-start(f32[1,32,8,256]{3,2,1,0:T(8,128)S(1)} %get-tuple-element.102.near_ref), channel_id=1, source_target_pairs={{0,1},{1,0},{2,3},{3,2},{4,5},{5,4},{6,7},{7,6},{8,9},{9,8},{10,11... | collective-permute-start | bytes 786440 | tf_op jit(solution)/shard_map/ppermute | solution.py:311
  7.9 0.6 copy.37
  8.5 0.6 copy-done
  9.1 1.2 bitcast_multiply_fusion.fixed_ref
  10.3 0.1 slice_select_fusion
  10.4 0.6 copy.38
  11.1 1.4 %sweep_part.4 = (f32[1,32,8,256]{3,2,1,0:T(8,128)S(1)}, f32[2,32,8,256]{3,2,1,0:T(8,128)S(1)}, f32[1,32,8,256]{3,2,1,0:T(8,128)S(1)}) custom-call(s32[1]{0:T(128)} %bitcast.parity_ref.refs_0_, f32[1,32,8,256]{3,2,1,0:T(8,128)S(1)} %get-tuple-element.103.far_ref, f32[2,32,8,256]{3,2,1,0:T(8,128)S(1)} %slice.54.mid_ref, ...), custom_call_target="tpu_custom_call" | custom-call | flops 3145728 | bytes 4194304 | tf_op jit(solution)/shard_map/sweep_part/pallas_call | solution.py:281
  12.6 0.2 fusion.4.far_ref
  12.7 1.0 collective-permute-start.2
  13.8 0.2 fusion.near_ref
  14.0 2.9 %collective-permute-start.3 = (f32[1,32,8,256]{3,2,1,0:T(8,128)S(1)}, f32[1,32,8,256]{3,2,1,0:T(8,128)S(1)}, u32[]{:S(2)}, u32[]{:S(2)}) collective-permute-start(f32[1,32,8,256]{3,2,1,0:T(8,128)S(1)} %fusion.near_ref), channel_id=1, source_target_pairs={{0,1},{1,0},{2,3},{3,2},{4,5},{5,4},{6,7},{7,6},{8,9},{9,8},{10,11... | collective-permute-start | bytes 786440 | tf_op jit(solution)/shard_map/ppermute | solution.py:311
  17.0 1.2 sweep_part.5
  18.3 8.6 %collective-permute-done.2 = f32[1,32,8,256]{3,2,1,0:T(8,128)S(1)} collective-permute-done((f32[1,32,8,256]{3,2,1,0:T(8,128)S(1)}, f32[1,32,8,256]{3,2,1,0:T(8,128)S(1)}, u32[]{:S(2)}, u32[]{:S(2)}) %collective-permute-start.2) | collective-permute-done | bytes 262176 | tf_op jit(solution)/shard_map/ppermute | solution.py:306
  26.9 0.2 fusion.5.far_ref
  27.1 2.5 %collective-permute-start.4 = (f32[1,32,8,256]{3,2,1,0:T(8,128)S(1)}, f32[1,32,8,256]{3,2,1,0:T(8,128)S(1)}, u32[]{:S(2)}, u32[]{:S(2)}) collective-permute-start(f32[1,32,8,256]{3,2,1,0:T(8,128)S(1)} %fusion.5.far_ref), channel_id=1, source_target_pairs={{1,2},{3,4},{5,6},{7,8},{9,10},{11,12},{13,14},{15,0},{2,1},{4,3},... | collective-permute-start | bytes 786440 | tf_op jit(solution)/shard_map/ppermute | solution.py:306
  29.7 0.2 fusion.1.near_ref
  30.0 0.6 collective-permute-start.13
  30.6 6.1 %local_part.5 = (f32[4,32,8,256]{3,2,1,0:T(8,128)S(1)}, f32[4,32,8,256]{3,2,1,0:T(8,128)S(1)}) custom-call(f32[4,32,8,256]{3,2,1,0:T(8,128)S(1)} %bitcast.63), custom_call_target="tpu_custom_call" | custom-call | flops 34078720 | bytes 3145728 | tf_op jit(solution)/shard_map/local_part/pallas_call | solution.py:155
  36.7 1.2 sweep_part.6
  38.0 2.2 %collective-permute-done.4 = f32[1,32,8,256]{3,2,1,0:T(8,128)S(1)} collective-permute-done((f32[1,32,8,256]{3,2,1,0:T(8,128)S(1)}, f32[1,32,8,256]{3,2,1,0:T(8,128)S(1)}, u32[]{:S(2)}, u32[]{:S(2)}) %collective-permute-start.4) | collective-permute-done | bytes 262176 | tf_op jit(solution)/shard_map/ppermute | solution.py:306
  40.1 0.2 fusion.6.far_ref
  40.3 0.6 collective-permute-start.6
  40.9 0.2 fusion.2.near_ref
  41.1 1.9 %collective-permute-start.7 = (f32[1,32,8,256]{3,2,1,0:T(8,128)S(1)}, f32[1,32,8,256]{3,2,1,0:T(8,128)S(1)}, u32[]{:S(2)}, u32[]{:S(2)}) collective-permute-start(f32[1,32,8,256]{3,2,1,0:T(8,128)S(1)} %fusion.2.near_ref), channel_id=1, source_target_pairs={{0,1},{1,0},{2,3},{3,2},{4,5},{5,4},{6,7},{7,6},{8,9},{9,8},{10,11... | collective-permute-start | bytes 786440 | tf_op jit(solution)/shard_map/ppermute | solution.py:311
  43.1 1.2 sweep_part.7
  44.3 5.5 %collective-permute-done.6 = f32[1,32,8,256]{3,2,1,0:T(8,128)S(1)} collective-permute-done((f32[1,32,8,256]{3,2,1,0:T(8,128)S(1)}, f32[1,32,8,256]{3,2,1,0:T(8,128)S(1)}, u32[]{:S(2)}, u32[]{:S(2)}) %collective-permute-start.6) | collective-permute-done | bytes 262176 | tf_op jit(solution)/shard_map/ppermute | solution.py:306
  49.8 0.4 broadcast_select_fusion.3
  50.2 0.2 pad_maximum_fusion
  50.4 2.1 %finish_part.11 = (f32[4,16,8,256]{3,2,1,0:T(8,128)S(1)}, f32[3,16,8,256]{3,2,1,0:T(8,128)S(1)}, f32[3,16,8,256]{3,2,1,0:T(8,128)S(1)}) custom-call(s32[1]{0:T(128)} %bitcast.parity_ref.refs_0_, f32[4,16,8,256]{3,2,1,0:T(8,128)S(1)} %get-tuple-element.89.refs_1_, f32[3,16,8,256]{3,2,1,0:T(8,128)S(1)} %collective-permute-done.12.refs_2_, ...), custom_call_target="tpu_custom_call" | custom-call | flops 10485760 | bytes 4194304 | tf_op jit(solution)/shard_map/finish_part/pallas_call | solution.py:230
  52.5 0.7 collective-permute-start.16
  53.3 2.7 %collective-permute-start.17 = (f32[3,16,8,256]{3,2,1,0:T(8,128)S(1)}, f32[3,16,8,256]{3,2,1,0:T(8,128)S(1)}, u32[]{:S(2)}, u32[]{:S(2)}) collective-permute-start(f32[3,16,8,256]{3,2,1,0:T(8,128)S(1)} %get-tuple-element.68), channel_id=1, source_target_pairs={{0,1},{1,0},{2,3},{3,2},{4,5},{5,4},{6,7},{7,6},{8,9},{9,8},{10,11... | collective-permute-start | bytes 1179656 | tf_op jit(solution)/shard_map/ppermute | solution.py:311
  55.9 2.1 %finish_part.10 = (f32[4,16,8,256]{3,2,1,0:T(8,128)S(1)}, f32[3,16,8,256]{3,2,1,0:T(8,128)S(1)}, f32[3,16,8,256]{3,2,1,0:T(8,128)S(1)}) custom-call(s32[1]{0:T(128)} %bitcast.parity_ref.refs_0_, f32[4,16,8,256]{3,2,1,0:T(8,128)S(1)} %get-tuple-element.88.refs_1_, f32[3,16,8,256]{3,2,1,0:T(8,128)S(1)} %collective-permute-done.8.refs_2_, ...), custom_call_target="tpu_custom_call" | custom-call | flops 10485760 | bytes 4194304 | tf_op jit(solution)/shard_map/finish_part/pallas_call | solution.py:230
  58.1 1.6 %collective-permute-start.11 = (f32[3,16,8,256]{3,2,1,0:T(8,128)S(1)}, f32[3,16,8,256]{3,2,1,0:T(8,128)S(1)}, u32[]{:S(2)}, u32[]{:S(2)}) collective-permute-start(f32[3,16,8,256]{3,2,1,0:T(8,128)S(1)} %get-tuple-element.62), channel_id=1, source_target_pairs={{0,1},{1,0},{2,3},{3,2},{4,5},{5,4},{6,7},{7,6},{8,9},{9,8},{10,11... | collective-permute-start | bytes 1179656 | tf_op jit(solution)/shard_map/ppermute | solution.py:311
  59.7 5.6 %local_part.6.refs_4_ = f32[4,32,8,256]{3,2,1,0:T(8,128)S(1)} custom-call(f32[4,16,8,256]{3,2,1,0:T(8,128)S(1)} %get-tuple-element.60.refs_0_.refs_1_, f32[4,16,8,256]{3,2,1,0:T(8,128)S(1)} %get-tuple-element.63.refs_1_, f32[4,32,8,256]{3,2,1,0:T(8,128)S(1)} %get-tuple-element.90.refs_6_.refs_2_.refs_5_), custom_call_target="tpu_custom_call" | custom-call | flops 34078720 | bytes 3145728 | tf_op jit(solution)/shard_map/local_part/pallas_call | solution.py:155
  65.4 2.8 %collective-permute-done.16.refs_2_ = f32[3,16,8,256]{3,2,1,0:T(8,128)S(1)} collective-permute-done((f32[3,16,8,256]{3,2,1,0:T(8,128)S(1)}, f32[3,16,8,256]{3,2,1,0:T(8,128)S(1)}, u32[]{:S(2)}, u32[]{:S(2)}) %collective-permute-start.16) | collective-permute-done | bytes 393248 | tf_op jit(solution)/shard_map/ppermute | solution.py:306
  68.2 2.2 %finish_part.13 = (f32[4,16,8,256]{3,2,1,0:T(8,128)S(1)}, f32[3,16,8,256]{3,2,1,0:T(8,128)S(1)}, f32[3,16,8,256]{3,2,1,0:T(8,128)S(1)}) custom-call(s32[1]{0:T(128)} %bitcast.parity_ref.refs_0_, f32[4,16,8,256]{3,2,1,0:T(8,128)S(1)} %get-tuple-element.63.refs_1_, f32[3,16,8,256]{3,2,1,0:T(8,128)S(1)} %collective-permute-done.16.refs_2_, ...), custom_call_target="tpu_custom_call" | custom-call | flops 10485760 | bytes 4194304 | tf_op jit(solution)/shard_map/finish_part/pallas_call | solution.py:230
  70.4 0.7 collective-permute-start.20
  71.1 3.7 %collective-permute-done.10.refs_2_ = f32[3,16,8,256]{3,2,1,0:T(8,128)S(1)} collective-permute-done((f32[3,16,8,256]{3,2,1,0:T(8,128)S(1)}, f32[3,16,8,256]{3,2,1,0:T(8,128)S(1)}, u32[]{:S(2)}, u32[]{:S(2)}) %collective-permute-start.10) | collective-permute-done | bytes 393248 | tf_op jit(solution)/shard_map/ppermute | solution.py:306
  74.8 2.1 %finish_part.12 = (f32[4,16,8,256]{3,2,1,0:T(8,128)S(1)}, f32[3,16,8,256]{3,2,1,0:T(8,128)S(1)}, f32[3,16,8,256]{3,2,1,0:T(8,128)S(1)}) custom-call(s32[1]{0:T(128)} %bitcast.parity_ref.refs_0_, f32[4,16,8,256]{3,2,1,0:T(8,128)S(1)} %get-tuple-element.60.refs_0_.refs_1_, f32[3,16,8,256]{3,2,1,0:T(8,128)S(1)} %collective-permute-done.10.refs_2_, ...), custom_call_target="tpu_custom_call" | custom-call | flops 10485760 | bytes 4194304 | tf_op jit(solution)/shard_map/finish_part/pallas_call | solution.py:230
  77.0 2.5 %collective-permute-start.14 = (f32[3,16,8,256]{3,2,1,0:T(8,128)S(1)}, f32[3,16,8,256]{3,2,1,0:T(8,128)S(1)}, u32[]{:S(2)}, u32[]{:S(2)}) collective-permute-start(f32[3,16,8,256]{3,2,1,0:T(8,128)S(1)} %get-tuple-element.65), channel_id=1, source_target_pairs={{1,2},{3,4},{5,6},{7,8},{9,10},{11,12},{13,14},{15,0},{2,1},{4,3},... | collective-permute-start | bytes 1179656 | tf_op jit(solution)/shard_map/ppermute | solution.py:306
  79.5 5.6 %local_part.7.refs_4_ = f32[4,32,8,256]{3,2,1,0:T(8,128)S(1)} custom-call(f32[4,16,8,256]{3,2,1,0:T(8,128)S(1)} %get-tuple-element.64.refs_0_.refs_1_, f32[4,16,8,256]{3,2,1,0:T(8,128)S(1)} %get-tuple-element.69.refs_1_, f32[4,32,8,256]{3,2,1,0:T(8,128)S(1)} %get-tuple-element.90.refs_6_.refs_2_.refs_5_), custom_call_target="tpu_custom_call" | custom-call | flops 34078720 | bytes 3145728 | tf_op jit(solution)/shard_map/local_part/pallas_call | solution.py:155
  85.2 0.1 collective-permute-done.20.refs_2_
  85.3 2.2 %finish_part.15 = (f32[4,16,8,256]{3,2,1,0:T(8,128)S(1)}, f32[3,16,8,256]{3,2,1,0:T(8,128)S(1)}, f32[3,16,8,256]{3,2,1,0:T(8,128)S(1)}) custom-call(s32[1]{0:T(128)} %bitcast.parity_ref.refs_0_, f32[4,16,8,256]{3,2,1,0:T(8,128)S(1)} %get-tuple-element.69.refs_1_, f32[3,16,8,256]{3,2,1,0:T(8,128)S(1)} %collective-permute-done.20.refs_2_, ...), custom_call_target="tpu_custom_call" | custom-call | flops 10485760 | bytes 4194304 | tf_op jit(solution)/shard_map/finish_part/pallas_call | solution.py:230
  87.5 0.5 collective-permute-start.24
  88.0 2.2 %collective-permute-start.25 = (f32[3,16,8,256]{3,2,1,0:T(8,128)S(1)}, f32[3,16,8,256]{3,2,1,0:T(8,128)S(1)}, u32[]{:S(2)}, u32[]{:S(2)}) collective-permute-start(f32[3,16,8,256]{3,2,1,0:T(8,128)S(1)} %get-tuple-element.80), channel_id=1, source_target_pairs={{0,1},{1,0},{2,3},{3,2},{4,5},{5,4},{6,7},{7,6},{8,9},{9,8},{10,11... | collective-permute-start | bytes 1179656 | tf_op jit(solution)/shard_map/ppermute | solution.py:311
  90.1 2.1 %finish_part.14 = (f32[4,16,8,256]{3,2,1,0:T(8,128)S(1)}, f32[3,16,8,256]{3,2,1,0:T(8,128)S(1)}, f32[3,16,8,256]{3,2,1,0:T(8,128)S(1)}) custom-call(s32[1]{0:T(128)} %bitcast.parity_ref.refs_0_, f32[4,16,8,256]{3,2,1,0:T(8,128)S(1)} %get-tuple-element.64.refs_0_.refs_1_, f32[3,16,8,256]{3,2,1,0:T(8,128)S(1)} %collective-permute-done.14.refs_2_, ...), custom_call_target="tpu_custom_call" | custom-call | flops 10485760 | bytes 4194304 | tf_op jit(solution)/shard_map/finish_part/pallas_call | solution.py:230
  92.3 0.7 collective-permute-start.18
  92.9 1.7 %collective-permute-start.19 = (f32[3,16,8,256]{3,2,1,0:T(8,128)S(1)}, f32[3,16,8,256]{3,2,1,0:T(8,128)S(1)}, u32[]{:S(2)}, u32[]{:S(2)}) collective-permute-start(f32[3,16,8,256]{3,2,1,0:T(8,128)S(1)} %get-tuple-element.72), channel_id=1, source_target_pairs={{0,1},{1,0},{2,3},{3,2},{4,5},{5,4},{6,7},{7,6},{8,9},{9,8},{10,11... | collective-permute-start | bytes 1179656 | tf_op jit(solution)/shard_map/ppermute | solution.py:311
  94.7 5.7 %local_part.8.refs_4_ = f32[4,32,8,256]{3,2,1,0:T(8,128)S(1)} custom-call(f32[4,16,8,256]{3,2,1,0:T(8,128)S(1)} %get-tuple-element.70.refs_0_.refs_1_.refs_5_, f32[4,16,8,256]{3,2,1,0:T(8,128)S(1)} %get-tuple-element.75.refs_1_.refs_5_, f32[4,32,8,256]{3,2,1,0:T(8,128)S(1)} %constant_dynamic-update-slice_fusion.refs_2_), custom_call_target="tpu_custom_call" | custom-call | flops 34078720 | bytes 3145728 | tf_op jit(solution)/shard_map/local_part/pallas_call | solution.py:155
  100.4 2.8 %collective-permute-done.24.refs_2_ = f32[3,16,8,256]{3,2,1,0:T(8,128)S(1)} collective-permute-done((f32[3,16,8,256]{3,2,1,0:T(8,128)S(1)}, f32[3,16,8,256]{3,2,1,0:T(8,128)S(1)}, u32[]{:S(2)}, u32[]{:S(2)}) %collective-permute-start.24) | collective-permute-done | bytes 393248 | tf_op jit(solution)/shard_map/ppermute | solution.py:306
  103.2 2.1 %finish_part.17 = (f32[4,16,8,256]{3,2,1,0:T(8,128)S(1)}, f32[3,16,8,256]{3,2,1,0:T(8,128)S(1)}, f32[3,16,8,256]{3,2,1,0:T(8,128)S(1)}) custom-call(s32[1]{0:T(128)} %bitcast.parity_ref.refs_0_, f32[4,16,8,256]{3,2,1,0:T(8,128)S(1)} %get-tuple-element.75.refs_1_.refs_5_, f32[3,16,8,256]{3,2,1,0:T(8,128)S(1)} %collective-permute-done.24.refs_2_, ...), custom_call_target="tpu_custom_call" | custom-call | flops 10485760 | bytes 4194304 | tf_op jit(solution)/shard_map/finish_part/pallas_call | solution.py:230
  105.3 0.5 collective-permute-start.26
  105.8 3.8 %collective-permute-done.18.refs_2_ = f32[3,16,8,256]{3,2,1,0:T(8,128)S(1)} collective-permute-done((f32[3,16,8,256]{3,2,1,0:T(8,128)S(1)}, f32[3,16,8,256]{3,2,1,0:T(8,128)S(1)}, u32[]{:S(2)}, u32[]{:S(2)}) %collective-permute-start.18) | collective-permute-done | bytes 393248 | tf_op jit(solution)/shard_map/ppermute | solution.py:306
  109.6 2.1 %finish_part.16 = (f32[4,16,8,256]{3,2,1,0:T(8,128)S(1)}, f32[3,16,8,256]{3,2,1,0:T(8,128)S(1)}, f32[3,16,8,256]{3,2,1,0:T(8,128)S(1)}) custom-call(s32[1]{0:T(128)} %bitcast.parity_ref.refs_0_, f32[4,16,8,256]{3,2,1,0:T(8,128)S(1)} %get-tuple-element.70.refs_0_.refs_1_.refs_5_, f32[3,16,8,256]{3,2,1,0:T(8,128)S(1)} %collective-permute-done.18.refs_2_, ...), custom_call_target="tpu_custom_call" | custom-call | flops 10485760 | bytes 4194304 | tf_op jit(solution)/shard_map/finish_part/pallas_call | solution.py:230
  111.6 2.5 %collective-permute-start.22 = (f32[3,16,8,256]{3,2,1,0:T(8,128)S(1)}, f32[3,16,8,256]{3,2,1,0:T(8,128)S(1)}, u32[]{:S(2)}, u32[]{:S(2)}) collective-permute-start(f32[3,16,8,256]{3,2,1,0:T(8,128)S(1)} %get-tuple-element.77), channel_id=1, source_target_pairs={{1,2},{3,4},{5,6},{7,8},{9,10},{11,12},{13,14},{15,0},{2,1},{4,3},... | collective-permute-start | bytes 1179656 | tf_op jit(solution)/shard_map/ppermute | solution.py:306
  114.2 1.3 %copy.12 = f32[4,8,32,256]{3,2,1,0:T(8,128)} copy(f32[4,8,32,256]{3,1,2,0:T(8,128)S(1)} %get-tuple-element.91) | data formatting | bytes 2097152 | tf_op jit(solution)/shard_map/transpose | solution.py:300
  115.5 5.6 %local_part.9.refs_4_ = f32[4,32,8,256]{3,2,1,0:T(8,128)S(1)} custom-call(f32[4,16,8,256]{3,2,1,0:T(8,128)S(1)} %get-tuple-element.76.refs_0_.refs_1_, f32[4,16,8,256]{3,2,1,0:T(8,128)S(1)} %get-tuple-element.81.refs_1_, f32[4,32,8,256]{3,2,1,0:T(8,128)S(1)} %constant_dynamic-update-slice_fusion.refs_2_), custom_call_target="tpu_custom_call" | custom-call | flops 34078720 | bytes 3145728 | tf_op jit(solution)/shard_map/local_part/pallas_call | solution.py:155
  121.1 2.0 %finish_part.19 = f32[4,16,8,256]{3,2,1,0:T(8,128)S(1)} custom-call(s32[1]{0:T(128)} %bitcast.parity_ref.refs_0_, f32[4,16,8,256]{3,2,1,0:T(8,128)S(1)} %get-tuple-element.81.refs_1_, f32[3,16,8,256]{3,2,1,0:T(8,128)S(1)} %collective-permute-done.26.refs_2_, f32[3,16,8,256]{3,2,1,0:T(8,128)S(1)} %collective-permute-done.27.refs_3_, ...), custom_call_target="tpu_custom_call" | custom-call | flops 10485760 | bytes 4194304 | tf_op jit(solution)/shard_map/finish_part/pallas_call | solution.py:230
  123.1 1.3 %collective-permute-done.22.refs_2_ = f32[3,16,8,256]{3,2,1,0:T(8,128)S(1)} collective-permute-done((f32[3,16,8,256]{3,2,1,0:T(8,128)S(1)}, f32[3,16,8,256]{3,2,1,0:T(8,128)S(1)}, u32[]{:S(2)}, u32[]{:S(2)}) %collective-permute-start.22) | collective-permute-done | bytes 393248 | tf_op jit(solution)/shard_map/ppermute | solution.py:306
  124.4 2.0 %finish_part.18 = f32[4,16,8,256]{3,2,1,0:T(8,128)S(1)} custom-call(s32[1]{0:T(128)} %bitcast.parity_ref.refs_0_, f32[4,16,8,256]{3,2,1,0:T(8,128)S(1)} %get-tuple-element.76.refs_0_.refs_1_, f32[3,16,8,256]{3,2,1,0:T(8,128)S(1)} %collective-permute-done.22.refs_2_, f32[3,16,8,256]{3,2,1,0:T(8,128)S(1)} %collective-permute-done.23.refs_3_, ...), custom_call_target="tpu_custom_call" | custom-call | flops 10485760 | bytes 4194304 | tf_op jit(solution)/shard_map/finish_part/pallas_call | solution.py:230
  126.5 1.3 %copy.13 = f32[4,8,32,256]{3,2,1,0:T(8,128)} copy(f32[4,8,32,256]{3,1,2,0:T(8,128)S(1)} %maximum_bitcast_fusion) | data formatting | bytes 2097152 | tf_op jit(solution)/shard_map/transpose | solution.py:300
  (41 shorter events, 0.8 us)
Async XLA Ops:
  1.9 5.9 %copy-start.1 = (s32[4,256,256]{2,1,0:T(8,128)S(1)}, s32[4,256,256]{2,1,0:T(8,128)}, u32[]{:S(2)}) copy-start(s32[4,256,256]{2,1,0:T(8,128)} %param.5) | copy-start | bytes 3145732
  2.3 10.3 %collective-permute-start = (f32[1,32,8,256]{3,2,1,0:T(8,128)S(1)}, f32[1,32,8,256]{3,2,1,0:T(8,128)S(1)}, u32[]{:S(2)}, u32[]{:S(2)}) collective-permute-start(f32[1,32,8,256]{3,2,1,0:T(8,128)S(1)} %get-tuple-element.103.far_ref), channel_id=1, source_target_pairs={{1,2},{3,4},{5,6},{7,8},{9,10},{11,12},{13,14},{15,0},{2,1},{4,3},... | collective-permute-start | bytes 786440 | tf_op jit(solution)/shard_map/ppermute | solution.py:306
  4.9 3.0 %copy-start.2 = (f32[4,256,256]{2,1,0:T(8,128)S(1)}, f32[4,256,256]{2,1,0:T(8,128)}, u32[]{:S(2)}) copy-start(f32[4,256,256]{2,1,0:T(8,128)} %param.3) | copy-start | bytes 3145732
  4.9 8.9 %collective-permute-start.1 = (f32[1,32,8,256]{3,2,1,0:T(8,128)S(1)}, f32[1,32,8,256]{3,2,1,0:T(8,128)S(1)}, u32[]{:S(2)}, u32[]{:S(2)}) collective-permute-start(f32[1,32,8,256]{3,2,1,0:T(8,128)S(1)} %get-tuple-element.102.near_ref), channel_id=1, source_target_pairs={{0,1},{1,0},{2,3},{3,2},{4,5},{5,4},{6,7},{7,6},{8,9},{9,8},{10,11... | collective-permute-start | bytes 786440 | tf_op jit(solution)/shard_map/ppermute | solution.py:311
  7.9 1.2 copy-start
  12.7 14.2 %collective-permute-start.2 = (f32[1,32,8,256]{3,2,1,0:T(8,128)S(1)}, f32[1,32,8,256]{3,2,1,0:T(8,128)S(1)}, u32[]{:S(2)}, u32[]{:S(2)}) collective-permute-start(f32[1,32,8,256]{3,2,1,0:T(8,128)S(1)} %fusion.4.far_ref), channel_id=1, source_target_pairs={{1,2},{3,4},{5,6},{7,8},{9,10},{11,12},{13,14},{15,0},{2,1},{4,3},... | collective-permute-start | bytes 786440 | tf_op jit(solution)/shard_map/ppermute | solution.py:306
  14.0 15.7 %collective-permute-start.3 = (f32[1,32,8,256]{3,2,1,0:T(8,128)S(1)}, f32[1,32,8,256]{3,2,1,0:T(8,128)S(1)}, u32[]{:S(2)}, u32[]{:S(2)}) collective-permute-start(f32[1,32,8,256]{3,2,1,0:T(8,128)S(1)} %fusion.near_ref), channel_id=1, source_target_pairs={{0,1},{1,0},{2,3},{3,2},{4,5},{5,4},{6,7},{7,6},{8,9},{9,8},{10,11... | collective-permute-start | bytes 786440 | tf_op jit(solution)/shard_map/ppermute | solution.py:311
  17.0 33.4 %collective-permute-start.12 = (f32[3,16,8,256]{3,2,1,0:T(8,128)S(1)}, f32[3,16,8,256]{3,2,1,0:T(8,128)S(1)}, u32[]{:S(2)}, u32[]{:S(2)}) collective-permute-start(f32[3,16,8,256]{3,2,1,0:T(8,128)S(1)} %get-tuple-element.101), channel_id=1, source_target_pairs={{1,2},{3,4},{5,6},{7,8},{9,10},{11,12},{13,14},{15,0},{2,1},{4,3},... | collective-permute-start | bytes 1179656 | tf_op jit(solution)/shard_map/ppermute | solution.py:306
  27.1 13.0 %collective-permute-start.4 = (f32[1,32,8,256]{3,2,1,0:T(8,128)S(1)}, f32[1,32,8,256]{3,2,1,0:T(8,128)S(1)}, u32[]{:S(2)}, u32[]{:S(2)}) collective-permute-start(f32[1,32,8,256]{3,2,1,0:T(8,128)S(1)} %fusion.5.far_ref), channel_id=1, source_target_pairs={{1,2},{3,4},{5,6},{7,8},{9,10},{11,12},{13,14},{15,0},{2,1},{4,3},... | collective-permute-start | bytes 786440 | tf_op jit(solution)/shard_map/ppermute | solution.py:306
  29.8 11.1 %collective-permute-start.5 = (f32[1,32,8,256]{3,2,1,0:T(8,128)S(1)}, f32[1,32,8,256]{3,2,1,0:T(8,128)S(1)}, u32[]{:S(2)}, u32[]{:S(2)}) collective-permute-start(f32[1,32,8,256]{3,2,1,0:T(8,128)S(1)} %fusion.1.near_ref), channel_id=1, source_target_pairs={{0,1},{1,0},{2,3},{3,2},{4,5},{5,4},{6,7},{7,6},{8,9},{9,8},{10,11... | collective-permute-start | bytes 786440 | tf_op jit(solution)/shard_map/ppermute | solution.py:311
  30.0 20.4 %collective-permute-start.13 = (f32[3,16,8,256]{3,2,1,0:T(8,128)S(1)}, f32[3,16,8,256]{3,2,1,0:T(8,128)S(1)}, u32[]{:S(2)}, u32[]{:S(2)}) collective-permute-start(f32[3,16,8,256]{3,2,1,0:T(8,128)S(1)} %get-tuple-element.99), channel_id=1, source_target_pairs={{0,1},{1,0},{2,3},{3,2},{4,5},{5,4},{6,7},{7,6},{8,9},{9,8},{10,11... | collective-permute-start | bytes 1179656 | tf_op jit(solution)/shard_map/ppermute | solution.py:311
  30.6 25.4 %collective-permute-start.8 = (f32[3,16,8,256]{3,2,1,0:T(8,128)S(1)}, f32[3,16,8,256]{3,2,1,0:T(8,128)S(1)}, u32[]{:S(2)}, u32[]{:S(2)}) collective-permute-start(f32[3,16,8,256]{3,2,1,0:T(8,128)S(1)} %get-tuple-element.100), channel_id=1, source_target_pairs={{1,2},{3,4},{5,6},{7,8},{9,10},{11,12},{13,14},{15,0},{2,1},{4,3},... | collective-permute-start | bytes 1179656 | tf_op jit(solution)/shard_map/ppermute | solution.py:306
  40.3 9.5 %collective-permute-start.6 = (f32[1,32,8,256]{3,2,1,0:T(8,128)S(1)}, f32[1,32,8,256]{3,2,1,0:T(8,128)S(1)}, u32[]{:S(2)}, u32[]{:S(2)}) collective-permute-start(f32[1,32,8,256]{3,2,1,0:T(8,128)S(1)} %fusion.6.far_ref), channel_id=1, source_target_pairs={{1,2},{3,4},{5,6},{7,8},{9,10},{11,12},{13,14},{15,0},{2,1},{4,3},... | collective-permute-start | bytes 786440 | tf_op jit(solution)/shard_map/ppermute | solution.py:306
  41.1 8.7 %collective-permute-start.7 = (f32[1,32,8,256]{3,2,1,0:T(8,128)S(1)}, f32[1,32,8,256]{3,2,1,0:T(8,128)S(1)}, u32[]{:S(2)}, u32[]{:S(2)}) collective-permute-start(f32[1,32,8,256]{3,2,1,0:T(8,128)S(1)} %fusion.2.near_ref), channel_id=1, source_target_pairs={{0,1},{1,0},{2,3},{3,2},{4,5},{5,4},{6,7},{7,6},{8,9},{9,8},{10,11... | collective-permute-start | bytes 786440 | tf_op jit(solution)/shard_map/ppermute | solution.py:311
  49.8 6.1 %collective-permute-start.9 = (f32[3,16,8,256]{3,2,1,0:T(8,128)S(1)}, f32[3,16,8,256]{3,2,1,0:T(8,128)S(1)}, u32[]{:S(2)}, u32[]{:S(2)}) collective-permute-start(f32[3,16,8,256]{3,2,1,0:T(8,128)S(1)} %get-tuple-element.98), channel_id=1, source_target_pairs={{0,1},{1,0},{2,3},{3,2},{4,5},{5,4},{6,7},{7,6},{8,9},{9,8},{10,11... | collective-permute-start | bytes 1179656 | tf_op jit(solution)/shard_map/ppermute | solution.py:311
  52.5 15.7 %collective-permute-start.16 = (f32[3,16,8,256]{3,2,1,0:T(8,128)S(1)}, f32[3,16,8,256]{3,2,1,0:T(8,128)S(1)}, u32[]{:S(2)}, u32[]{:S(2)}) collective-permute-start(f32[3,16,8,256]{3,2,1,0:T(8,128)S(1)} %get-tuple-element.67), channel_id=1, source_target_pairs={{1,2},{3,4},{5,6},{7,8},{9,10},{11,12},{13,14},{15,0},{2,1},{4,3},... | collective-permute-start | bytes 1179656 | tf_op jit(solution)/shard_map/ppermute | solution.py:306
  53.3 15.0 %collective-permute-start.17 = (f32[3,16,8,256]{3,2,1,0:T(8,128)S(1)}, f32[3,16,8,256]{3,2,1,0:T(8,128)S(1)}, u32[]{:S(2)}, u32[]{:S(2)}) collective-permute-start(f32[3,16,8,256]{3,2,1,0:T(8,128)S(1)} %get-tuple-element.68), channel_id=1, source_target_pairs={{0,1},{1,0},{2,3},{3,2},{4,5},{5,4},{6,7},{7,6},{8,9},{9,8},{10,11... | collective-permute-start | bytes 1179656 | tf_op jit(solution)/shard_map/ppermute | solution.py:311
  58.0 16.8 %collective-permute-start.10 = (f32[3,16,8,256]{3,2,1,0:T(8,128)S(1)}, f32[3,16,8,256]{3,2,1,0:T(8,128)S(1)}, u32[]{:S(2)}, u32[]{:S(2)}) collective-permute-start(f32[3,16,8,256]{3,2,1,0:T(8,128)S(1)} %get-tuple-element.61), channel_id=1, source_target_pairs={{1,2},{3,4},{5,6},{7,8},{9,10},{11,12},{13,14},{15,0},{2,1},{4,3},... | collective-permute-start | bytes 1179656 | tf_op jit(solution)/shard_map/ppermute | solution.py:306
  58.1 16.7 %collective-permute-start.11 = (f32[3,16,8,256]{3,2,1,0:T(8,128)S(1)}, f32[3,16,8,256]{3,2,1,0:T(8,128)S(1)}, u32[]{:S(2)}, u32[]{:S(2)}) collective-permute-start(f32[3,16,8,256]{3,2,1,0:T(8,128)S(1)} %get-tuple-element.62), channel_id=1, source_target_pairs={{0,1},{1,0},{2,3},{3,2},{4,5},{5,4},{6,7},{7,6},{8,9},{9,8},{10,11... | collective-permute-start | bytes 1179656 | tf_op jit(solution)/shard_map/ppermute | solution.py:311
  70.4 14.9 %collective-permute-start.20 = (f32[3,16,8,256]{3,2,1,0:T(8,128)S(1)}, f32[3,16,8,256]{3,2,1,0:T(8,128)S(1)}, u32[]{:S(2)}, u32[]{:S(2)}) collective-permute-start(f32[3,16,8,256]{3,2,1,0:T(8,128)S(1)} %get-tuple-element.73), channel_id=1, source_target_pairs={{1,2},{3,4},{5,6},{7,8},{9,10},{11,12},{13,14},{15,0},{2,1},{4,3},... | collective-permute-start | bytes 1179656 | tf_op jit(solution)/shard_map/ppermute | solution.py:306
  71.1 14.2 %collective-permute-start.21 = (f32[3,16,8,256]{3,2,1,0:T(8,128)S(1)}, f32[3,16,8,256]{3,2,1,0:T(8,128)S(1)}, u32[]{:S(2)}, u32[]{:S(2)}) collective-permute-start(f32[3,16,8,256]{3,2,1,0:T(8,128)S(1)} %get-tuple-element.74), channel_id=1, source_target_pairs={{0,1},{1,0},{2,3},{3,2},{4,5},{5,4},{6,7},{7,6},{8,9},{9,8},{10,11... | collective-permute-start | bytes 1179656 | tf_op jit(solution)/shard_map/ppermute | solution.py:311
  77.0 13.2 %collective-permute-start.14 = (f32[3,16,8,256]{3,2,1,0:T(8,128)S(1)}, f32[3,16,8,256]{3,2,1,0:T(8,128)S(1)}, u32[]{:S(2)}, u32[]{:S(2)}) collective-permute-start(f32[3,16,8,256]{3,2,1,0:T(8,128)S(1)} %get-tuple-element.65), channel_id=1, source_target_pairs={{1,2},{3,4},{5,6},{7,8},{9,10},{11,12},{13,14},{15,0},{2,1},{4,3},... | collective-permute-start | bytes 1179656 | tf_op jit(solution)/shard_map/ppermute | solution.py:306
  79.5 10.6 %collective-permute-start.15 = (f32[3,16,8,256]{3,2,1,0:T(8,128)S(1)}, f32[3,16,8,256]{3,2,1,0:T(8,128)S(1)}, u32[]{:S(2)}, u32[]{:S(2)}) collective-permute-start(f32[3,16,8,256]{3,2,1,0:T(8,128)S(1)} %get-tuple-element.66), channel_id=1, source_target_pairs={{0,1},{1,0},{2,3},{3,2},{4,5},{5,4},{6,7},{7,6},{8,9},{9,8},{10,11... | collective-permute-start | bytes 1179656 | tf_op jit(solution)/shard_map/ppermute | solution.py:311
  87.5 15.7 %collective-permute-start.24 = (f32[3,16,8,256]{3,2,1,0:T(8,128)S(1)}, f32[3,16,8,256]{3,2,1,0:T(8,128)S(1)}, u32[]{:S(2)}, u32[]{:S(2)}) collective-permute-start(f32[3,16,8,256]{3,2,1,0:T(8,128)S(1)} %get-tuple-element.79), channel_id=1, source_target_pairs={{1,2},{3,4},{5,6},{7,8},{9,10},{11,12},{13,14},{15,0},{2,1},{4,3},... | collective-permute-start | bytes 1179656 | tf_op jit(solution)/shard_map/ppermute | solution.py:306
  88.0 15.2 %collective-permute-start.25 = (f32[3,16,8,256]{3,2,1,0:T(8,128)S(1)}, f32[3,16,8,256]{3,2,1,0:T(8,128)S(1)}, u32[]{:S(2)}, u32[]{:S(2)}) collective-permute-start(f32[3,16,8,256]{3,2,1,0:T(8,128)S(1)} %get-tuple-element.80), channel_id=1, source_target_pairs={{0,1},{1,0},{2,3},{3,2},{4,5},{5,4},{6,7},{7,6},{8,9},{9,8},{10,11... | collective-permute-start | bytes 1179656 | tf_op jit(solution)/shard_map/ppermute | solution.py:311
  92.3 17.3 %collective-permute-start.18 = (f32[3,16,8,256]{3,2,1,0:T(8,128)S(1)}, f32[3,16,8,256]{3,2,1,0:T(8,128)S(1)}, u32[]{:S(2)}, u32[]{:S(2)}) collective-permute-start(f32[3,16,8,256]{3,2,1,0:T(8,128)S(1)} %get-tuple-element.71), channel_id=1, source_target_pairs={{1,2},{3,4},{5,6},{7,8},{9,10},{11,12},{13,14},{15,0},{2,1},{4,3},... | collective-permute-start | bytes 1179656 | tf_op jit(solution)/shard_map/ppermute | solution.py:306
  92.9 16.6 %collective-permute-start.19 = (f32[3,16,8,256]{3,2,1,0:T(8,128)S(1)}, f32[3,16,8,256]{3,2,1,0:T(8,128)S(1)}, u32[]{:S(2)}, u32[]{:S(2)}) collective-permute-start(f32[3,16,8,256]{3,2,1,0:T(8,128)S(1)} %get-tuple-element.72), channel_id=1, source_target_pairs={{0,1},{1,0},{2,3},{3,2},{4,5},{5,4},{6,7},{7,6},{8,9},{9,8},{10,11... | collective-permute-start | bytes 1179656 | tf_op jit(solution)/shard_map/ppermute | solution.py:311
  105.3 15.9 %collective-permute-start.26 = (f32[3,16,8,256]{3,2,1,0:T(8,128)S(1)}, f32[3,16,8,256]{3,2,1,0:T(8,128)S(1)}, u32[]{:S(2)}, u32[]{:S(2)}) collective-permute-start(f32[3,16,8,256]{3,2,1,0:T(8,128)S(1)} %get-tuple-element.82), channel_id=1, source_target_pairs={{1,2},{3,4},{5,6},{7,8},{9,10},{11,12},{13,14},{15,0},{2,1},{4,3},... | collective-permute-start | bytes 1179656 | tf_op jit(solution)/shard_map/ppermute | solution.py:306
  105.8 15.4 %collective-permute-start.27 = (f32[3,16,8,256]{3,2,1,0:T(8,128)S(1)}, f32[3,16,8,256]{3,2,1,0:T(8,128)S(1)}, u32[]{:S(2)}, u32[]{:S(2)}) collective-permute-start(f32[3,16,8,256]{3,2,1,0:T(8,128)S(1)} %get-tuple-element.83), channel_id=1, source_target_pairs={{0,1},{1,0},{2,3},{3,2},{4,5},{5,4},{6,7},{7,6},{8,9},{9,8},{10,11... | collective-permute-start | bytes 1179656 | tf_op jit(solution)/shard_map/ppermute | solution.py:311
  111.6 12.8 %collective-permute-start.22 = (f32[3,16,8,256]{3,2,1,0:T(8,128)S(1)}, f32[3,16,8,256]{3,2,1,0:T(8,128)S(1)}, u32[]{:S(2)}, u32[]{:S(2)}) collective-permute-start(f32[3,16,8,256]{3,2,1,0:T(8,128)S(1)} %get-tuple-element.77), channel_id=1, source_target_pairs={{1,2},{3,4},{5,6},{7,8},{9,10},{11,12},{13,14},{15,0},{2,1},{4,3},... | collective-permute-start | bytes 1179656 | tf_op jit(solution)/shard_map/ppermute | solution.py:306
  114.2 10.3 %collective-permute-start.23 = (f32[3,16,8,256]{3,2,1,0:T(8,128)S(1)}, f32[3,16,8,256]{3,2,1,0:T(8,128)S(1)}, u32[]{:S(2)}, u32[]{:S(2)}) collective-permute-start(f32[3,16,8,256]{3,2,1,0:T(8,128)S(1)} %get-tuple-element.78), channel_id=1, source_target_pairs={{0,1},{1,0},{2,3},{3,2},{4,5},{5,4},{6,7},{7,6},{8,9},{9,8},{10,11... | collective-permute-start | bytes 1179656 | tf_op jit(solution)/shard_map/ppermute | solution.py:311

commit v4 on v3

--- a/solution.py
+++ b/solution.py
@@ -213,7 +213,7 @@
                 rest[2][i, t] = jnp.where(even, made[layers - 3 + i], made[i])
         return carry
 
-    lax.fori_loop(0, tiles, loop, 0)
+    lax.fori_loop(0, tiles, loop, 0, unroll=4)
 
 
 def finish_part(kind, last, start, parity, u, far, near, others, block=4):
@@ -340,7 +340,7 @@
     for sweep in range(SWEEPS):
         from_far, from_near = swap_far(far), swap_near(near)
         far_part, mid, near_part = sweep_part(parity, far, mid, near, weight, fixed)
-        if sweep == 1:
+        if sweep == 0:
             mid, rise, fall = lax.optimization_barrier((mid, rise, fall))
         far = far_part + far_open * from_far
         near = near_part + near_open * from_near

time: 128 us -> 127 us (level)
  waiting for transfers between devices: 30.9 us -> 33.2 us
  Pallas kernels: 54.8 us -> 52.5 us
    pallas_call x10, Pallas kernels: 20.9 us -> 18.6 us  [finish_part(): pl.pallas_call(functools.partial(finish_body, kind, last), grid=(per // b...]
    ppermute x14, waiting for transfers between devices: 30.8 us -> 33.1 us  [swap_far(): lax.ppermute(array, 'gx', [(i, (i + 1) % count) for i in odd] + [((i + 1)...]
  transfers between devices with their start and end apart: 28 -> 28, of which waited for: 9 -> 8; matrix products, arithmetic and copies ran while one was open for 5% -> 5% of each run, Pallas kernels for 41% -> 40%
where the time goes in v4:
time: 127 us
  Pallas kernels  52.5 us (41%)
  waiting for transfers between devices  33.2 us (26%)
  starting transfers between devices  30.5 us (24%)
  local copies, waits for them, and re-layouts  5.06 us (4%)
  other arithmetic  4.36 us (3%)
    ppermute x14, waiting for transfers between devices, swap_far(): lax.ppermute(array, 'gx', [(i, (i + 1) % count) for i in odd] + [((i + 1)...  33.1 us
    pallas_call x5, Pallas kernels, local_part(): pl.pallas_call(functools.partial(local_body, len(pieces), both, block), g...  28.7 us
    pallas_call x10, Pallas kernels, finish_part(): pl.pallas_call(functools.partial(finish_body, kind, last), grid=(per // b...  18.6 us
    ppermute x14, starting transfers between devices, swap_near(): lax.ppermute(array, 'gx', [(i, i + 1 - 2 * (i % 2)) for i in range(count)])  15.9 us
    ppermute x14, starting transfers between devices, swap_far(): lax.ppermute(array, 'gx', [(i, (i + 1) % count) for i in odd] + [((i + 1)...  14.7 us
    pallas_call x4, Pallas kernels, sweep_part(): pl.pallas_call(sweep_body, in_specs=[pl.BlockSpec(memory_space=pltpu.SMEM...  5.15 us
    transpose x2, local copies, waits for them, and re-layouts, unfold_rows(): return array.transpose(0, 2, 1, 3).reshape(layers, tiles * SUB, lanes)  2.59 us
  transfers between devices with their start and end apart: 28, of which 8 were waited for; matrix products, arithmetic and copies ran while one was open for 5% of the time, Pallas kernels for 40%

profile of v4, /device:TPU:1, one launch (start us, length us, event | category | flops | bytes accessed | tf_op | source)
XLA Modules:
  0.0 126.7 jit_solution(13842131568661379317)
XLA Ops:
  0.6 1.3 %fusion.9 = (f32[1,256,256]{2,1,0:T(8,128)S(1)}, f32[1,256,256]{2,1,0:T(8,128)S(1)}, f32[1,256,256]{2,1,0:T(8,128)S(1)}, f32[1,256,256]{2,1,0:T(8,128)S(1)}) fusion(s32[4,256,256]{2,1,0:T(8,128)} %param.5, pred[]{:T(512)S(6)} %eq.3, f32[4,256,256]{2,1,0:T(8,128)} %param.4), kind=kLoop, calls=%fused_computation.30 | loop fusion | flops 786432 | bytes 2097153 | tf_op jit(solution)/shard_map/jit(_where)/select_n | solution.py:330
  1.9 0.3 copy_bitcast_fusion.2
  2.3 2.7 %collective-permute-start = (f32[1,32,8,256]{3,2,1,0:T(8,128)S(1)}, f32[1,32,8,256]{3,2,1,0:T(8,128)S(1)}, u32[]{:S(2)}, u32[]{:S(2)}) collective-permute-start(f32[1,32,8,256]{3,2,1,0:T(8,128)S(1)} %get-tuple-element.103.far_ref), channel_id=1, source_target_pairs={{1,2},{3,4},{5,6},{7,8},{9,10},{11,12},{13,14},{15,0},{2,1},{4,3},... | collective-permute-start | bytes 786440 | tf_op jit(solution)/shard_map/ppermute | solution.py:306
  4.9 2.9 %collective-permute-start.1 = (f32[1,32,8,256]{3,2,1,0:T(8,128)S(1)}, f32[1,32,8,256]{3,2,1,0:T(8,128)S(1)}, u32[]{:S(2)}, u32[]{:S(2)}) collective-permute-start(f32[1,32,8,256]{3,2,1,0:T(8,128)S(1)} %get-tuple-element.102.near_ref), channel_id=1, source_target_pairs={{0,1},{1,0},{2,3},{3,2},{4,5},{5,4},{6,7},{7,6},{8,9},{9,8},{10,11... | collective-permute-start | bytes 786440 | tf_op jit(solution)/shard_map/ppermute | solution.py:311
  7.8 0.1 convert_element_type.21
  7.9 0.6 copy.37
  8.5 0.6 copy-done
  9.1 1.2 bitcast_multiply_fusion.fixed_ref
  10.3 0.1 slice_select_fusion
  10.4 0.6 copy.38
  11.1 1.4 %sweep_part.4 = (f32[1,32,8,256]{3,2,1,0:T(8,128)S(1)}, f32[2,32,8,256]{3,2,1,0:T(8,128)S(1)}, f32[1,32,8,256]{3,2,1,0:T(8,128)S(1)}) custom-call(s32[1]{0:T(128)} %bitcast.parity_ref.refs_0_, f32[1,32,8,256]{3,2,1,0:T(8,128)S(1)} %get-tuple-element.103.far_ref, f32[2,32,8,256]{3,2,1,0:T(8,128)S(1)} %slice.54.mid_ref, ...), custom_call_target="tpu_custom_call" | custom-call | flops 3145728 | bytes 4194304 | tf_op jit(solution)/shard_map/sweep_part/pallas_call | solution.py:281
  12.6 0.2 fusion.4.far_ref
  12.7 1.0 collective-permute-start.2
  13.8 0.2 fusion.near_ref
  14.0 2.9 %collective-permute-start.3 = (f32[1,32,8,256]{3,2,1,0:T(8,128)S(1)}, f32[1,32,8,256]{3,2,1,0:T(8,128)S(1)}, u32[]{:S(2)}, u32[]{:S(2)}) collective-permute-start(f32[1,32,8,256]{3,2,1,0:T(8,128)S(1)} %fusion.near_ref), channel_id=1, source_target_pairs={{0,1},{1,0},{2,3},{3,2},{4,5},{5,4},{6,7},{7,6},{8,9},{9,8},{10,11... | collective-permute-start | bytes 786440 | tf_op jit(solution)/shard_map/ppermute | solution.py:311
  17.0 6.2 %local_part.5 = (f32[4,32,8,256]{3,2,1,0:T(8,128)S(1)}, f32[4,32,8,256]{3,2,1,0:T(8,128)S(1)}) custom-call(f32[4,32,8,256]{3,2,1,0:T(8,128)S(1)} %bitcast.63), custom_call_target="tpu_custom_call" | custom-call | flops 34078720 | bytes 3145728 | tf_op jit(solution)/shard_map/local_part/pallas_call | solution.py:155
  23.2 1.2 sweep_part.5
  24.5 0.2 fusion.5.far_ref
  24.6 2.2 %collective-permute-start.4 = (f32[1,32,8,256]{3,2,1,0:T(8,128)S(1)}, f32[1,32,8,256]{3,2,1,0:T(8,128)S(1)}, u32[]{:S(2)}, u32[]{:S(2)}) collective-permute-start(f32[1,32,8,256]{3,2,1,0:T(8,128)S(1)} %fusion.5.far_ref), channel_id=1, source_target_pairs={{1,2},{3,4},{5,6},{7,8},{9,10},{11,12},{13,14},{15,0},{2,1},{4,3},... | collective-permute-start | bytes 786440 | tf_op jit(solution)/shard_map/ppermute | solution.py:306
  26.8 0.2 fusion.1.near_ref
  27.0 2.4 %collective-permute-start.5 = (f32[1,32,8,256]{3,2,1,0:T(8,128)S(1)}, f32[1,32,8,256]{3,2,1,0:T(8,128)S(1)}, u32[]{:S(2)}, u32[]{:S(2)}) collective-permute-start(f32[1,32,8,256]{3,2,1,0:T(8,128)S(1)} %fusion.1.near_ref), channel_id=1, source_target_pairs={{0,1},{1,0},{2,3},{3,2},{4,5},{5,4},{6,7},{7,6},{8,9},{9,8},{10,11... | collective-permute-start | bytes 786440 | tf_op jit(solution)/shard_map/ppermute | solution.py:311
  29.6 1.2 sweep_part.6
  30.9 10.1 %collective-permute-done.4 = f32[1,32,8,256]{3,2,1,0:T(8,128)S(1)} collective-permute-done((f32[1,32,8,256]{3,2,1,0:T(8,128)S(1)}, f32[1,32,8,256]{3,2,1,0:T(8,128)S(1)}, u32[]{:S(2)}, u32[]{:S(2)}) %collective-permute-start.4) | collective-permute-done | bytes 262176 | tf_op jit(solution)/shard_map/ppermute | solution.py:306
  41.0 0.2 fusion.6.far_ref
  41.2 2.5 %collective-permute-start.6 = (f32[1,32,8,256]{3,2,1,0:T(8,128)S(1)}, f32[1,32,8,256]{3,2,1,0:T(8,128)S(1)}, u32[]{:S(2)}, u32[]{:S(2)}) collective-permute-start(f32[1,32,8,256]{3,2,1,0:T(8,128)S(1)} %fusion.6.far_ref), channel_id=1, source_target_pairs={{1,2},{3,4},{5,6},{7,8},{9,10},{11,12},{13,14},{15,0},{2,1},{4,3},... | collective-permute-start | bytes 786440 | tf_op jit(solution)/shard_map/ppermute | solution.py:306
  43.7 0.2 fusion.2.near_ref
  44.0 1.2 sweep_part.7
  45.3 4.5 %collective-permute-done.6 = f32[1,32,8,256]{3,2,1,0:T(8,128)S(1)} collective-permute-done((f32[1,32,8,256]{3,2,1,0:T(8,128)S(1)}, f32[1,32,8,256]{3,2,1,0:T(8,128)S(1)}, u32[]{:S(2)}, u32[]{:S(2)}) %collective-permute-start.6) | collective-permute-done | bytes 262176 | tf_op jit(solution)/shard_map/ppermute | solution.py:306
  49.8 0.4 broadcast_select_fusion.3
  50.2 0.2 pad_maximum_fusion
  50.4 1.9 %finish_part.11 = (f32[4,16,8,256]{3,2,1,0:T(8,128)S(1)}, f32[3,16,8,256]{3,2,1,0:T(8,128)S(1)}, f32[3,16,8,256]{3,2,1,0:T(8,128)S(1)}) custom-call(s32[1]{0:T(128)} %bitcast.parity_ref.refs_0_, f32[4,16,8,256]{3,2,1,0:T(8,128)S(1)} %get-tuple-element.89.refs_1_, f32[3,16,8,256]{3,2,1,0:T(8,128)S(1)} %collective-permute-done.12.refs_2_, ...), custom_call_target="tpu_custom_call" | custom-call | flops 10485760 | bytes 4194304 | tf_op jit(solution)/shard_map/finish_part/pallas_call | solution.py:230
  52.3 0.7 collective-permute-start.16
  53.0 2.7 %collective-permute-start.17 = (f32[3,16,8,256]{3,2,1,0:T(8,128)S(1)}, f32[3,16,8,256]{3,2,1,0:T(8,128)S(1)}, u32[]{:S(2)}, u32[]{:S(2)}) collective-permute-start(f32[3,16,8,256]{3,2,1,0:T(8,128)S(1)} %get-tuple-element.68), channel_id=1, source_target_pairs={{0,1},{1,0},{2,3},{3,2},{4,5},{5,4},{6,7},{7,6},{8,9},{9,8},{10,11... | collective-permute-start | bytes 1179656 | tf_op jit(solution)/shard_map/ppermute | solution.py:311
  55.7 1.9 %finish_part.10 = (f32[4,16,8,256]{3,2,1,0:T(8,128)S(1)}, f32[3,16,8,256]{3,2,1,0:T(8,128)S(1)}, f32[3,16,8,256]{3,2,1,0:T(8,128)S(1)}) custom-call(s32[1]{0:T(128)} %bitcast.parity_ref.refs_0_, f32[4,16,8,256]{3,2,1,0:T(8,128)S(1)} %get-tuple-element.88.refs_1_, f32[3,16,8,256]{3,2,1,0:T(8,128)S(1)} %collective-permute-done.8.refs_2_, ...), custom_call_target="tpu_custom_call" | custom-call | flops 10485760 | bytes 4194304 | tf_op jit(solution)/shard_map/finish_part/pallas_call | solution.py:230
  57.6 1.6 %collective-permute-start.11 = (f32[3,16,8,256]{3,2,1,0:T(8,128)S(1)}, f32[3,16,8,256]{3,2,1,0:T(8,128)S(1)}, u32[]{:S(2)}, u32[]{:S(2)}) collective-permute-start(f32[3,16,8,256]{3,2,1,0:T(8,128)S(1)} %get-tuple-element.62), channel_id=1, source_target_pairs={{0,1},{1,0},{2,3},{3,2},{4,5},{5,4},{6,7},{7,6},{8,9},{9,8},{10,11... | collective-permute-start | bytes 1179656 | tf_op jit(solution)/shard_map/ppermute | solution.py:311
  59.2 5.6 %local_part.6.refs_4_ = f32[4,32,8,256]{3,2,1,0:T(8,128)S(1)} custom-call(f32[4,16,8,256]{3,2,1,0:T(8,128)S(1)} %get-tuple-element.60.refs_0_.refs_1_, f32[4,16,8,256]{3,2,1,0:T(8,128)S(1)} %get-tuple-element.63.refs_1_, f32[4,32,8,256]{3,2,1,0:T(8,128)S(1)} %get-tuple-element.90.refs_6_.refs_2_.refs_5_), custom_call_target="tpu_custom_call" | custom-call | flops 34078720 | bytes 3145728 | tf_op jit(solution)/shard_map/local_part/pallas_call | solution.py:155
  64.9 3.1 %collective-permute-done.16.refs_2_ = f32[3,16,8,256]{3,2,1,0:T(8,128)S(1)} collective-permute-done((f32[3,16,8,256]{3,2,1,0:T(8,128)S(1)}, f32[3,16,8,256]{3,2,1,0:T(8,128)S(1)}, u32[]{:S(2)}, u32[]{:S(2)}) %collective-permute-start.16) | collective-permute-done | bytes 393248 | tf_op jit(solution)/shard_map/ppermute | solution.py:306
  68.0 1.9 %finish_part.13 = (f32[4,16,8,256]{3,2,1,0:T(8,128)S(1)}, f32[3,16,8,256]{3,2,1,0:T(8,128)S(1)}, f32[3,16,8,256]{3,2,1,0:T(8,128)S(1)}) custom-call(s32[1]{0:T(128)} %bitcast.parity_ref.refs_0_, f32[4,16,8,256]{3,2,1,0:T(8,128)S(1)} %get-tuple-element.63.refs_1_, f32[3,16,8,256]{3,2,1,0:T(8,128)S(1)} %collective-permute-done.16.refs_2_, ...), custom_call_target="tpu_custom_call" | custom-call | flops 10485760 | bytes 4194304 | tf_op jit(solution)/shard_map/finish_part/pallas_call | solution.py:230
  69.9 0.7 collective-permute-start.20
  70.6 5.8 %collective-permute-done.10.refs_2_ = f32[3,16,8,256]{3,2,1,0:T(8,128)S(1)} collective-permute-done((f32[3,16,8,256]{3,2,1,0:T(8,128)S(1)}, f32[3,16,8,256]{3,2,1,0:T(8,128)S(1)}, u32[]{:S(2)}, u32[]{:S(2)}) %collective-permute-start.10) | collective-permute-done | bytes 393248 | tf_op jit(solution)/shard_map/ppermute | solution.py:306
  76.4 1.9 %finish_part.12 = (f32[4,16,8,256]{3,2,1,0:T(8,128)S(1)}, f32[3,16,8,256]{3,2,1,0:T(8,128)S(1)}, f32[3,16,8,256]{3,2,1,0:T(8,128)S(1)}) custom-call(s32[1]{0:T(128)} %bitcast.parity_ref.refs_0_, f32[4,16,8,256]{3,2,1,0:T(8,128)S(1)} %get-tuple-element.60.refs_0_.refs_1_, f32[3,16,8,256]{3,2,1,0:T(8,128)S(1)} %collective-permute-done.10.refs_2_, ...), custom_call_target="tpu_custom_call" | custom-call | flops 10485760 | bytes 4194304 | tf_op jit(solution)/shard_map/finish_part/pallas_call | solution.py:230
  78.3 0.7 collective-permute-start.14
  79.0 5.6 %local_part.7.refs_4_ = f32[4,32,8,256]{3,2,1,0:T(8,128)S(1)} custom-call(f32[4,16,8,256]{3,2,1,0:T(8,128)S(1)} %get-tuple-element.64.refs_0_.refs_1_, f32[4,16,8,256]{3,2,1,0:T(8,128)S(1)} %get-tuple-element.69.refs_1_, f32[4,32,8,256]{3,2,1,0:T(8,128)S(1)} %get-tuple-element.90.refs_6_.refs_2_.refs_5_), custom_call_target="tpu_custom_call" | custom-call | flops 34078720 | bytes 3145728 | tf_op jit(solution)/shard_map/local_part/pallas_call | solution.py:155
  84.7 0.1 collective-permute-done.20.refs_2_
  84.8 1.9 %finish_part.15 = (f32[4,16,8,256]{3,2,1,0:T(8,128)S(1)}, f32[3,16,8,256]{3,2,1,0:T(8,128)S(1)}, f32[3,16,8,256]{3,2,1,0:T(8,128)S(1)}) custom-call(s32[1]{0:T(128)} %bitcast.parity_ref.refs_0_, f32[4,16,8,256]{3,2,1,0:T(8,128)S(1)} %get-tuple-element.69.refs_1_, f32[3,16,8,256]{3,2,1,0:T(8,128)S(1)} %collective-permute-done.20.refs_2_, ...), custom_call_target="tpu_custom_call" | custom-call | flops 10485760 | bytes 4194304 | tf_op jit(solution)/shard_map/finish_part/pallas_call | solution.py:230
  86.7 1.1 collective-permute-start.24
  87.8 1.6 %collective-permute-start.25 = (f32[3,16,8,256]{3,2,1,0:T(8,128)S(1)}, f32[3,16,8,256]{3,2,1,0:T(8,128)S(1)}, u32[]{:S(2)}, u32[]{:S(2)}) collective-permute-start(f32[3,16,8,256]{3,2,1,0:T(8,128)S(1)} %get-tuple-element.80), channel_id=1, source_target_pairs={{0,1},{1,0},{2,3},{3,2},{4,5},{5,4},{6,7},{7,6},{8,9},{9,8},{10,11... | collective-permute-start | bytes 1179656 | tf_op jit(solution)/shard_map/ppermute | solution.py:311
  89.4 1.9 %finish_part.14 = (f32[4,16,8,256]{3,2,1,0:T(8,128)S(1)}, f32[3,16,8,256]{3,2,1,0:T(8,128)S(1)}, f32[3,16,8,256]{3,2,1,0:T(8,128)S(1)}) custom-call(s32[1]{0:T(128)} %bitcast.parity_ref.refs_0_, f32[4,16,8,256]{3,2,1,0:T(8,128)S(1)} %get-tuple-element.64.refs_0_.refs_1_, f32[3,16,8,256]{3,2,1,0:T(8,128)S(1)} %collective-permute-done.14.refs_2_, ...), custom_call_target="tpu_custom_call" | custom-call | flops 10485760 | bytes 4194304 | tf_op jit(solution)/shard_map/finish_part/pallas_call | solution.py:230
  91.3 0.7 collective-permute-start.18
  91.9 1.7 %collective-permute-start.19 = (f32[3,16,8,256]{3,2,1,0:T(8,128)S(1)}, f32[3,16,8,256]{3,2,1,0:T(8,128)S(1)}, u32[]{:S(2)}, u32[]{:S(2)}) collective-permute-start(f32[3,16,8,256]{3,2,1,0:T(8,128)S(1)} %get-tuple-element.72), channel_id=1, source_target_pairs={{0,1},{1,0},{2,3},{3,2},{4,5},{5,4},{6,7},{7,6},{8,9},{9,8},{10,11... | collective-permute-start | bytes 1179656 | tf_op jit(solution)/shard_map/ppermute | solution.py:311
  93.7 5.7 %local_part.8.refs_4_ = f32[4,32,8,256]{3,2,1,0:T(8,128)S(1)} custom-call(f32[4,16,8,256]{3,2,1,0:T(8,128)S(1)} %get-tuple-element.70.refs_0_.refs_1_.refs_5_, f32[4,16,8,256]{3,2,1,0:T(8,128)S(1)} %get-tuple-element.75.refs_1_.refs_5_, f32[4,32,8,256]{3,2,1,0:T(8,128)S(1)} %constant_dynamic-update-slice_fusion.refs_2_), custom_call_target="tpu_custom_call" | custom-call | flops 34078720 | bytes 3145728 | tf_op jit(solution)/shard_map/local_part/pallas_call | solution.py:155
  99.4 3.0 %collective-permute-done.24.refs_2_ = f32[3,16,8,256]{3,2,1,0:T(8,128)S(1)} collective-permute-done((f32[3,16,8,256]{3,2,1,0:T(8,128)S(1)}, f32[3,16,8,256]{3,2,1,0:T(8,128)S(1)}, u32[]{:S(2)}, u32[]{:S(2)}) %collective-permute-start.24) | collective-permute-done | bytes 393248 | tf_op jit(solution)/shard_map/ppermute | solution.py:306
  102.4 1.9 %finish_part.17 = (f32[4,16,8,256]{3,2,1,0:T(8,128)S(1)}, f32[3,16,8,256]{3,2,1,0:T(8,128)S(1)}, f32[3,16,8,256]{3,2,1,0:T(8,128)S(1)}) custom-call(s32[1]{0:T(128)} %bitcast.parity_ref.refs_0_, f32[4,16,8,256]{3,2,1,0:T(8,128)S(1)} %get-tuple-element.75.refs_1_.refs_5_, f32[3,16,8,256]{3,2,1,0:T(8,128)S(1)} %collective-permute-done.24.refs_2_, ...), custom_call_target="tpu_custom_call" | custom-call | flops 10485760 | bytes 4194304 | tf_op jit(solution)/shard_map/finish_part/pallas_call | solution.py:230
  104.3 1.1 collective-permute-start.26
  105.4 5.5 %collective-permute-done.18.refs_2_ = f32[3,16,8,256]{3,2,1,0:T(8,128)S(1)} collective-permute-done((f32[3,16,8,256]{3,2,1,0:T(8,128)S(1)}, f32[3,16,8,256]{3,2,1,0:T(8,128)S(1)}, u32[]{:S(2)}, u32[]{:S(2)}) %collective-permute-start.18) | collective-permute-done | bytes 393248 | tf_op jit(solution)/shard_map/ppermute | solution.py:306
  110.9 1.9 %finish_part.16 = (f32[4,16,8,256]{3,2,1,0:T(8,128)S(1)}, f32[3,16,8,256]{3,2,1,0:T(8,128)S(1)}, f32[3,16,8,256]{3,2,1,0:T(8,128)S(1)}) custom-call(s32[1]{0:T(128)} %bitcast.parity_ref.refs_0_, f32[4,16,8,256]{3,2,1,0:T(8,128)S(1)} %get-tuple-element.70.refs_0_.refs_1_.refs_5_, f32[3,16,8,256]{3,2,1,0:T(8,128)S(1)} %collective-permute-done.18.refs_2_, ...), custom_call_target="tpu_custom_call" | custom-call | flops 10485760 | bytes 4194304 | tf_op jit(solution)/shard_map/finish_part/pallas_call | solution.py:230
  112.8 1.0 collective-permute-start.22
  113.8 1.3 %copy.12 = f32[4,8,32,256]{3,2,1,0:T(8,128)} copy(f32[4,8,32,256]{3,1,2,0:T(8,128)S(1)} %get-tuple-element.91) | data formatting | bytes 2097152 | tf_op jit(solution)/shard_map/transpose | solution.py:300
  115.1 5.6 %local_part.9.refs_4_ = f32[4,32,8,256]{3,2,1,0:T(8,128)S(1)} custom-call(f32[4,16,8,256]{3,2,1,0:T(8,128)S(1)} %get-tuple-element.76.refs_0_.refs_1_, f32[4,16,8,256]{3,2,1,0:T(8,128)S(1)} %get-tuple-element.81.refs_1_, f32[4,32,8,256]{3,2,1,0:T(8,128)S(1)} %constant_dynamic-update-slice_fusion.refs_2_), custom_call_target="tpu_custom_call" | custom-call | flops 34078720 | bytes 3145728 | tf_op jit(solution)/shard_map/local_part/pallas_call | solution.py:155
  120.8 1.8 %finish_part.19 = f32[4,16,8,256]{3,2,1,0:T(8,128)S(1)} custom-call(s32[1]{0:T(128)} %bitcast.parity_ref.refs_0_, f32[4,16,8,256]{3,2,1,0:T(8,128)S(1)} %get-tuple-element.81.refs_1_, f32[3,16,8,256]{3,2,1,0:T(8,128)S(1)} %collective-permute-done.26.refs_2_, f32[3,16,8,256]{3,2,1,0:T(8,128)S(1)} %collective-permute-done.27.refs_3_, ...), custom_call_target="tpu_custom_call" | custom-call | flops 10485760 | bytes 4194304 | tf_op jit(solution)/shard_map/finish_part/pallas_call | solution.py:230
  122.6 0.9 collective-permute-done.22.refs_2_
  123.5 1.8 %finish_part.18 = f32[4,16,8,256]{3,2,1,0:T(8,128)S(1)} custom-call(s32[1]{0:T(128)} %bitcast.parity_ref.refs_0_, f32[4,16,8,256]{3,2,1,0:T(8,128)S(1)} %get-tuple-element.76.refs_0_.refs_1_, f32[3,16,8,256]{3,2,1,0:T(8,128)S(1)} %collective-permute-done.22.refs_2_, f32[3,16,8,256]{3,2,1,0:T(8,128)S(1)} %collective-permute-done.23.refs_3_, ...), custom_call_target="tpu_custom_call" | custom-call | flops 10485760 | bytes 4194304 | tf_op jit(solution)/shard_map/finish_part/pallas_call | solution.py:230
  125.3 0.1 maximum_bitcast_fusion
  125.4 1.3 %copy.13 = f32[4,8,32,256]{3,2,1,0:T(8,128)} copy(f32[4,8,32,256]{3,1,2,0:T(8,128)S(1)} %maximum_bitcast_fusion) | data formatting | bytes 2097152 | tf_op jit(solution)/shard_map/transpose | solution.py:300
  (41 shorter events, 0.8 us)
Async XLA Ops:
  1.9 5.9 %copy-start.1 = (s32[4,256,256]{2,1,0:T(8,128)S(1)}, s32[4,256,256]{2,1,0:T(8,128)}, u32[]{:S(2)}) copy-start(s32[4,256,256]{2,1,0:T(8,128)} %param.5) | copy-start | bytes 3145732
  2.3 10.3 %collective-permute-start = (f32[1,32,8,256]{3,2,1,0:T(8,128)S(1)}, f32[1,32,8,256]{3,2,1,0:T(8,128)S(1)}, u32[]{:S(2)}, u32[]{:S(2)}) collective-permute-start(f32[1,32,8,256]{3,2,1,0:T(8,128)S(1)} %get-tuple-element.103.far_ref), channel_id=1, source_target_pairs={{1,2},{3,4},{5,6},{7,8},{9,10},{11,12},{13,14},{15,0},{2,1},{4,3},... | collective-permute-start | bytes 786440 | tf_op jit(solution)/shard_map/ppermute | solution.py:306
  4.9 3.0 %copy-start.2 = (f32[4,256,256]{2,1,0:T(8,128)S(1)}, f32[4,256,256]{2,1,0:T(8,128)}, u32[]{:S(2)}) copy-start(f32[4,256,256]{2,1,0:T(8,128)} %param.3) | copy-start | bytes 3145732
  4.9 8.9 %collective-permute-start.1 = (f32[1,32,8,256]{3,2,1,0:T(8,128)S(1)}, f32[1,32,8,256]{3,2,1,0:T(8,128)S(1)}, u32[]{:S(2)}, u32[]{:S(2)}) collective-permute-start(f32[1,32,8,256]{3,2,1,0:T(8,128)S(1)} %get-tuple-element.102.near_ref), channel_id=1, source_target_pairs={{0,1},{1,0},{2,3},{3,2},{4,5},{5,4},{6,7},{7,6},{8,9},{9,8},{10,11... | collective-permute-start | bytes 786440 | tf_op jit(solution)/shard_map/ppermute | solution.py:311
  7.9 1.2 copy-start
  12.7 11.7 %collective-permute-start.2 = (f32[1,32,8,256]{3,2,1,0:T(8,128)S(1)}, f32[1,32,8,256]{3,2,1,0:T(8,128)S(1)}, u32[]{:S(2)}, u32[]{:S(2)}) collective-permute-start(f32[1,32,8,256]{3,2,1,0:T(8,128)S(1)} %fusion.4.far_ref), channel_id=1, source_target_pairs={{1,2},{3,4},{5,6},{7,8},{9,10},{11,12},{13,14},{15,0},{2,1},{4,3},... | collective-permute-start | bytes 786440 | tf_op jit(solution)/shard_map/ppermute | solution.py:306
  14.0 12.9 %collective-permute-start.3 = (f32[1,32,8,256]{3,2,1,0:T(8,128)S(1)}, f32[1,32,8,256]{3,2,1,0:T(8,128)S(1)}, u32[]{:S(2)}, u32[]{:S(2)}) collective-permute-start(f32[1,32,8,256]{3,2,1,0:T(8,128)S(1)} %fusion.near_ref), channel_id=1, source_target_pairs={{0,1},{1,0},{2,3},{3,2},{4,5},{5,4},{6,7},{7,6},{8,9},{9,8},{10,11... | collective-permute-start | bytes 786440 | tf_op jit(solution)/shard_map/ppermute | solution.py:311
  17.0 33.4 %collective-permute-start.12 = (f32[3,16,8,256]{3,2,1,0:T(8,128)S(1)}, f32[3,16,8,256]{3,2,1,0:T(8,128)S(1)}, u32[]{:S(2)}, u32[]{:S(2)}) collective-permute-start(f32[3,16,8,256]{3,2,1,0:T(8,128)S(1)} %get-tuple-element.101), channel_id=1, source_target_pairs={{1,2},{3,4},{5,6},{7,8},{9,10},{11,12},{13,14},{15,0},{2,1},{4,3},... | collective-permute-start | bytes 1179656 | tf_op jit(solution)/shard_map/ppermute | solution.py:306
  24.6 16.3 %collective-permute-start.4 = (f32[1,32,8,256]{3,2,1,0:T(8,128)S(1)}, f32[1,32,8,256]{3,2,1,0:T(8,128)S(1)}, u32[]{:S(2)}, u32[]{:S(2)}) collective-permute-start(f32[1,32,8,256]{3,2,1,0:T(8,128)S(1)} %fusion.5.far_ref), channel_id=1, source_target_pairs={{1,2},{3,4},{5,6},{7,8},{9,10},{11,12},{13,14},{15,0},{2,1},{4,3},... | collective-permute-start | bytes 786440 | tf_op jit(solution)/shard_map/ppermute | solution.py:306
  27.0 16.7 %collective-permute-start.5 = (f32[1,32,8,256]{3,2,1,0:T(8,128)S(1)}, f32[1,32,8,256]{3,2,1,0:T(8,128)S(1)}, u32[]{:S(2)}, u32[]{:S(2)}) collective-permute-start(f32[1,32,8,256]{3,2,1,0:T(8,128)S(1)} %fusion.1.near_ref), channel_id=1, source_target_pairs={{0,1},{1,0},{2,3},{3,2},{4,5},{5,4},{6,7},{7,6},{8,9},{9,8},{10,11... | collective-permute-start | bytes 786440 | tf_op jit(solution)/shard_map/ppermute | solution.py:311
  29.5 20.9 %collective-permute-start.13 = (f32[3,16,8,256]{3,2,1,0:T(8,128)S(1)}, f32[3,16,8,256]{3,2,1,0:T(8,128)S(1)}, u32[]{:S(2)}, u32[]{:S(2)}) collective-permute-start(f32[3,16,8,256]{3,2,1,0:T(8,128)S(1)} %get-tuple-element.99), channel_id=1, source_target_pairs={{0,1},{1,0},{2,3},{3,2},{4,5},{5,4},{6,7},{7,6},{8,9},{9,8},{10,11... | collective-permute-start | bytes 1179656 | tf_op jit(solution)/shard_map/ppermute | solution.py:311
  29.6 26.1 %collective-permute-start.8 = (f32[3,16,8,256]{3,2,1,0:T(8,128)S(1)}, f32[3,16,8,256]{3,2,1,0:T(8,128)S(1)}, u32[]{:S(2)}, u32[]{:S(2)}) collective-permute-start(f32[3,16,8,256]{3,2,1,0:T(8,128)S(1)} %get-tuple-element.100), channel_id=1, source_target_pairs={{1,2},{3,4},{5,6},{7,8},{9,10},{11,12},{13,14},{15,0},{2,1},{4,3},... | collective-permute-start | bytes 1179656 | tf_op jit(solution)/shard_map/ppermute | solution.py:306
  41.2 8.7 %collective-permute-start.6 = (f32[1,32,8,256]{3,2,1,0:T(8,128)S(1)}, f32[1,32,8,256]{3,2,1,0:T(8,128)S(1)}, u32[]{:S(2)}, u32[]{:S(2)}) collective-permute-start(f32[1,32,8,256]{3,2,1,0:T(8,128)S(1)} %fusion.6.far_ref), channel_id=1, source_target_pairs={{1,2},{3,4},{5,6},{7,8},{9,10},{11,12},{13,14},{15,0},{2,1},{4,3},... | collective-permute-start | bytes 786440 | tf_op jit(solution)/shard_map/ppermute | solution.py:306
  43.9 5.9 %collective-permute-start.7 = (f32[1,32,8,256]{3,2,1,0:T(8,128)S(1)}, f32[1,32,8,256]{3,2,1,0:T(8,128)S(1)}, u32[]{:S(2)}, u32[]{:S(2)}) collective-permute-start(f32[1,32,8,256]{3,2,1,0:T(8,128)S(1)} %fusion.2.near_ref), channel_id=1, source_target_pairs={{0,1},{1,0},{2,3},{3,2},{4,5},{5,4},{6,7},{7,6},{8,9},{9,8},{10,11... | collective-permute-start | bytes 786440 | tf_op jit(solution)/shard_map/ppermute | solution.py:311
  49.8 5.9 %collective-permute-start.9 = (f32[3,16,8,256]{3,2,1,0:T(8,128)S(1)}, f32[3,16,8,256]{3,2,1,0:T(8,128)S(1)}, u32[]{:S(2)}, u32[]{:S(2)}) collective-permute-start(f32[3,16,8,256]{3,2,1,0:T(8,128)S(1)} %get-tuple-element.98), channel_id=1, source_target_pairs={{0,1},{1,0},{2,3},{3,2},{4,5},{5,4},{6,7},{7,6},{8,9},{9,8},{10,11... | collective-permute-start | bytes 1179656 | tf_op jit(solution)/shard_map/ppermute | solution.py:311
  52.3 15.7 %collective-permute-start.16 = (f32[3,16,8,256]{3,2,1,0:T(8,128)S(1)}, f32[3,16,8,256]{3,2,1,0:T(8,128)S(1)}, u32[]{:S(2)}, u32[]{:S(2)}) collective-permute-start(f32[3,16,8,256]{3,2,1,0:T(8,128)S(1)} %get-tuple-element.67), channel_id=1, source_target_pairs={{1,2},{3,4},{5,6},{7,8},{9,10},{11,12},{13,14},{15,0},{2,1},{4,3},... | collective-permute-start | bytes 1179656 | tf_op jit(solution)/shard_map/ppermute | solution.py:306
  53.0 15.0 %collective-permute-start.17 = (f32[3,16,8,256]{3,2,1,0:T(8,128)S(1)}, f32[3,16,8,256]{3,2,1,0:T(8,128)S(1)}, u32[]{:S(2)}, u32[]{:S(2)}) collective-permute-start(f32[3,16,8,256]{3,2,1,0:T(8,128)S(1)} %get-tuple-element.68), channel_id=1, source_target_pairs={{0,1},{1,0},{2,3},{3,2},{4,5},{5,4},{6,7},{7,6},{8,9},{9,8},{10,11... | collective-permute-start | bytes 1179656 | tf_op jit(solution)/shard_map/ppermute | solution.py:311
  57.5 18.9 %collective-permute-start.10 = (f32[3,16,8,256]{3,2,1,0:T(8,128)S(1)}, f32[3,16,8,256]{3,2,1,0:T(8,128)S(1)}, u32[]{:S(2)}, u32[]{:S(2)}) collective-permute-start(f32[3,16,8,256]{3,2,1,0:T(8,128)S(1)} %get-tuple-element.61), channel_id=1, source_target_pairs={{1,2},{3,4},{5,6},{7,8},{9,10},{11,12},{13,14},{15,0},{2,1},{4,3},... | collective-permute-start | bytes 1179656 | tf_op jit(solution)/shard_map/ppermute | solution.py:306
  57.6 18.8 %collective-permute-start.11 = (f32[3,16,8,256]{3,2,1,0:T(8,128)S(1)}, f32[3,16,8,256]{3,2,1,0:T(8,128)S(1)}, u32[]{:S(2)}, u32[]{:S(2)}) collective-permute-start(f32[3,16,8,256]{3,2,1,0:T(8,128)S(1)} %get-tuple-element.62), channel_id=1, source_target_pairs={{0,1},{1,0},{2,3},{3,2},{4,5},{5,4},{6,7},{7,6},{8,9},{9,8},{10,11... | collective-permute-start | bytes 1179656 | tf_op jit(solution)/shard_map/ppermute | solution.py:311
  69.9 14.9 %collective-permute-start.20 = (f32[3,16,8,256]{3,2,1,0:T(8,128)S(1)}, f32[3,16,8,256]{3,2,1,0:T(8,128)S(1)}, u32[]{:S(2)}, u32[]{:S(2)}) collective-permute-start(f32[3,16,8,256]{3,2,1,0:T(8,128)S(1)} %get-tuple-element.73), channel_id=1, source_target_pairs={{1,2},{3,4},{5,6},{7,8},{9,10},{11,12},{13,14},{15,0},{2,1},{4,3},... | collective-permute-start | bytes 1179656 | tf_op jit(solution)/shard_map/ppermute | solution.py:306
  70.6 14.2 %collective-permute-start.21 = (f32[3,16,8,256]{3,2,1,0:T(8,128)S(1)}, f32[3,16,8,256]{3,2,1,0:T(8,128)S(1)}, u32[]{:S(2)}, u32[]{:S(2)}) collective-permute-start(f32[3,16,8,256]{3,2,1,0:T(8,128)S(1)} %get-tuple-element.74), channel_id=1, source_target_pairs={{0,1},{1,0},{2,3},{3,2},{4,5},{5,4},{6,7},{7,6},{8,9},{9,8},{10,11... | collective-permute-start | bytes 1179656 | tf_op jit(solution)/shard_map/ppermute | solution.py:311
  78.3 11.1 %collective-permute-start.14 = (f32[3,16,8,256]{3,2,1,0:T(8,128)S(1)}, f32[3,16,8,256]{3,2,1,0:T(8,128)S(1)}, u32[]{:S(2)}, u32[]{:S(2)}) collective-permute-start(f32[3,16,8,256]{3,2,1,0:T(8,128)S(1)} %get-tuple-element.65), channel_id=1, source_target_pairs={{1,2},{3,4},{5,6},{7,8},{9,10},{11,12},{13,14},{15,0},{2,1},{4,3},... | collective-permute-start | bytes 1179656 | tf_op jit(solution)/shard_map/ppermute | solution.py:306
  79.0 10.4 %collective-permute-start.15 = (f32[3,16,8,256]{3,2,1,0:T(8,128)S(1)}, f32[3,16,8,256]{3,2,1,0:T(8,128)S(1)}, u32[]{:S(2)}, u32[]{:S(2)}) collective-permute-start(f32[3,16,8,256]{3,2,1,0:T(8,128)S(1)} %get-tuple-element.66), channel_id=1, source_target_pairs={{0,1},{1,0},{2,3},{3,2},{4,5},{5,4},{6,7},{7,6},{8,9},{9,8},{10,11... | collective-permute-start | bytes 1179656 | tf_op jit(solution)/shard_map/ppermute | solution.py:311
  86.7 15.7 %collective-permute-start.24 = (f32[3,16,8,256]{3,2,1,0:T(8,128)S(1)}, f32[3,16,8,256]{3,2,1,0:T(8,128)S(1)}, u32[]{:S(2)}, u32[]{:S(2)}) collective-permute-start(f32[3,16,8,256]{3,2,1,0:T(8,128)S(1)} %get-tuple-element.79), channel_id=1, source_target_pairs={{1,2},{3,4},{5,6},{7,8},{9,10},{11,12},{13,14},{15,0},{2,1},{4,3},... | collective-permute-start | bytes 1179656 | tf_op jit(solution)/shard_map/ppermute | solution.py:306
  87.8 14.6 %collective-permute-start.25 = (f32[3,16,8,256]{3,2,1,0:T(8,128)S(1)}, f32[3,16,8,256]{3,2,1,0:T(8,128)S(1)}, u32[]{:S(2)}, u32[]{:S(2)}) collective-permute-start(f32[3,16,8,256]{3,2,1,0:T(8,128)S(1)} %get-tuple-element.80), channel_id=1, source_target_pairs={{0,1},{1,0},{2,3},{3,2},{4,5},{5,4},{6,7},{7,6},{8,9},{9,8},{10,11... | collective-permute-start | bytes 1179656 | tf_op jit(solution)/shard_map/ppermute | solution.py:311
  91.3 19.6 %collective-permute-start.18 = (f32[3,16,8,256]{3,2,1,0:T(8,128)S(1)}, f32[3,16,8,256]{3,2,1,0:T(8,128)S(1)}, u32[]{:S(2)}, u32[]{:S(2)}) collective-permute-start(f32[3,16,8,256]{3,2,1,0:T(8,128)S(1)} %get-tuple-element.71), channel_id=1, source_target_pairs={{1,2},{3,4},{5,6},{7,8},{9,10},{11,12},{13,14},{15,0},{2,1},{4,3},... | collective-permute-start | bytes 1179656 | tf_op jit(solution)/shard_map/ppermute | solution.py:306
  91.9 19.0 %collective-permute-start.19 = (f32[3,16,8,256]{3,2,1,0:T(8,128)S(1)}, f32[3,16,8,256]{3,2,1,0:T(8,128)S(1)}, u32[]{:S(2)}, u32[]{:S(2)}) collective-permute-start(f32[3,16,8,256]{3,2,1,0:T(8,128)S(1)} %get-tuple-element.72), channel_id=1, source_target_pairs={{0,1},{1,0},{2,3},{3,2},{4,5},{5,4},{6,7},{7,6},{8,9},{9,8},{10,11... | collective-permute-start | bytes 1179656 | tf_op jit(solution)/shard_map/ppermute | solution.py:311
  104.3 16.4 %collective-permute-start.26 = (f32[3,16,8,256]{3,2,1,0:T(8,128)S(1)}, f32[3,16,8,256]{3,2,1,0:T(8,128)S(1)}, u32[]{:S(2)}, u32[]{:S(2)}) collective-permute-start(f32[3,16,8,256]{3,2,1,0:T(8,128)S(1)} %get-tuple-element.82), channel_id=1, source_target_pairs={{1,2},{3,4},{5,6},{7,8},{9,10},{11,12},{13,14},{15,0},{2,1},{4,3},... | collective-permute-start | bytes 1179656 | tf_op jit(solution)/shard_map/ppermute | solution.py:306
  105.4 15.4 %collective-permute-start.27 = (f32[3,16,8,256]{3,2,1,0:T(8,128)S(1)}, f32[3,16,8,256]{3,2,1,0:T(8,128)S(1)}, u32[]{:S(2)}, u32[]{:S(2)}) collective-permute-start(f32[3,16,8,256]{3,2,1,0:T(8,128)S(1)} %get-tuple-element.83), channel_id=1, source_target_pairs={{0,1},{1,0},{2,3},{3,2},{4,5},{5,4},{6,7},{7,6},{8,9},{9,8},{10,11... | collective-permute-start | bytes 1179656 | tf_op jit(solution)/shard_map/ppermute | solution.py:311
  112.8 10.7 %collective-permute-start.22 = (f32[3,16,8,256]{3,2,1,0:T(8,128)S(1)}, f32[3,16,8,256]{3,2,1,0:T(8,128)S(1)}, u32[]{:S(2)}, u32[]{:S(2)}) collective-permute-start(f32[3,16,8,256]{3,2,1,0:T(8,128)S(1)} %get-tuple-element.77), channel_id=1, source_target_pairs={{1,2},{3,4},{5,6},{7,8},{9,10},{11,12},{13,14},{15,0},{2,1},{4,3},... | collective-permute-start | bytes 1179656 | tf_op jit(solution)/shard_map/ppermute | solution.py:306
  113.8 9.7 %collective-permute-start.23 = (f32[3,16,8,256]{3,2,1,0:T(8,128)S(1)}, f32[3,16,8,256]{3,2,1,0:T(8,128)S(1)}, u32[]{:S(2)}, u32[]{:S(2)}) collective-permute-start(f32[3,16,8,256]{3,2,1,0:T(8,128)S(1)} %get-tuple-element.78), channel_id=1, source_target_pairs={{0,1},{1,0},{2,3},{3,2},{4,5},{5,4},{6,7},{7,6},{8,9},{9,8},{10,11... | collective-permute-start | bytes 1179656 | tf_op jit(solution)/shard_map/ppermute | solution.py:311

commit v5 on v4

--- a/solution.py
+++ b/solution.py
@@ -63,21 +63,15 @@
 
 def along_lanes(cell):
     length = cell.shape[1]
-
-    def back(v):
-        return pltpu.roll(v, 1, 1)
-
-    def ahead(v):
-        return pltpu.roll(v, length - 1, 1)
-
-    d = ahead(cell) - cell
-    x = d - back(d)
-    y = ahead(x)
-    a, b, c = smoothness(x, y, x * x, y * y)
-    q6 = (y - x) * (1.0 / 6.0)
-    r6 = q6 - back(q6)
-    minus, negated_plus = face_pair(d, q6, 0.25 * (x + y), back(a), b, ahead(c), r6, ahead(r6))
-    return back(minus), negated_plus
+    cells = [cell if k == 0 else pltpu.roll(cell, -k % length, 1) for k in range(-2, 4)]
+    d = [cells[i + 1] - cells[i] for i in range(5)]
+    e = [d[i + 1] - d[i] for i in range(4)]
+    squares = [v * v for v in e]
+    a, b, c = [smoothness(e[i], e[i + 1], squares[i], squares[i + 1])[i] for i in range(3)]
+    q6 = [(e[i + 1] - e[i]) * (1.0 / 6.0) for i in range(3)]
+    s4 = 0.25 * (e[1] + e[2])
+    minus, negated_plus = face_pair(d[2], q6[1], s4, a, b, c, q6[1] - q6[0], q6[2] - q6[1])
+    return pltpu.roll(minus, 1, 1), negated_plus
 
 
 def upwind(pair, positive):
@@ -271,7 +265,7 @@
         near_out[0, t] = jnp.where(even, ends[1], ends[0])
         return carry
 
-    lax.fori_loop(0, tiles, loop, 0, unroll=4)
+    lax.fori_loop(0, tiles, loop, 0, unroll=16)
 
 
 def sweep_part(parity, far, mid, near, weight, fixed):
@@ -361,21 +355,25 @@
             else:
                 local = local_part(pieces, speed)
         results = []
+        if last:
+            updated = jnp.zeros((layers, SUB) + level.shape[1:2] + level.shape[3:], jnp.float32)
         for i in range(len(pieces)):
+            if last and i > 0:
+                updated, pieces[i] = lax.optimization_barrier((updated, pieces[i]))
             if kind == "first":
                 others = (rise, fall, speed)
             elif kind == "reinit":
                 others = (local, marker[i])
             else:
                 others = (local, speed, level)
-            results.append(finish_part(kind, last, bounds[i], parity, pieces[i], halos[i][0], halos[i][1], others))
-        if last:
-            pieces = results
-        else:
+            result = finish_part(kind, last, bounds[i], parity, pieces[i], halos[i][0], halos[i][1], others)
+            if last:
+                updated = updated.at[:, :, bounds[i] : bounds[i + 1]].set(result.transpose(0, 2, 1, 3))
+            results.append(result)
+        if not last:
             pieces = [r[0] for r in results]
             sides = [r[1:] for r in results]
-    updated = jnp.concatenate(pieces, axis=1)
-    return (unfold_rows(speed), unfold_rows(updated))
+    return (unfold_rows(speed), updated.reshape(level_set.shape))
 
 
 def solution(mesh):

time: 127 us -> 126 us (level)
  waiting for transfers between devices: 33.2 us -> 37 us
  Pallas kernels: 52.5 us -> 49.9 us
  starting transfers between devices: 30.5 us -> 28.8 us
    ppermute x14, waiting for transfers between devices: 33.1 us -> 36.9 us  [swap_far(): lax.ppermute(array, 'gx', [(i, (i + 1) % count) for i in odd] + [((i + 1)...]
    pallas_call x4, Pallas kernels: 5.15 us -> 3.4 us  [sweep_part(): pl.pallas_call(sweep_body, in_specs=[pl.BlockSpec(memory_space=pltpu.SMEM...]
    ppermute x14, starting transfers between devices: 14.7 us -> 13.1 us  [swap_far(): lax.ppermute(array, 'gx', [(i, (i + 1) % count) for i in odd] + [((i + 1)...]
    scatter x0 -> x3, local copies, waits for them, and re-layouts: none -> 1.42 us  [per_device(): updated.at[:, :, bounds[i]:bounds[i + 1]].set(result.transpose(0, 2, 1, 3))]
    transpose x2 -> x1, local copies, waits for them, and re-layouts: 2.59 us -> 1.29 us  [unfold_rows(): return array.transpose(0, 2, 1, 3).reshape(layers, tiles * SUB, lanes)]
  transfers between devices with their start and end apart: 28 -> 28, of which waited for: 8 -> 9; matrix products, arithmetic and copies ran while one was open for 5% -> 5% of each run, Pallas kernels for 40% -> 38%
where the time goes in v5:
time: 126 us
  Pallas kernels  49.9 us (40%)
  waiting for transfers between devices  37 us (29%)
  starting transfers between devices  28.8 us (23%)
  local copies, waits for them, and re-layouts  5.18 us (4%)
  other arithmetic  4.28 us (3%)
    ppermute x14, waiting for transfers between devices, swap_far(): lax.ppermute(array, 'gx', [(i, (i + 1) % count) for i in odd] + [((i + 1)...  36.9 us
    pallas_call x5, Pallas kernels, local_part(): pl.pallas_call(functools.partial(local_body, len(pieces), both, block), g...  27.9 us
    pallas_call x10, Pallas kernels, finish_part(): pl.pallas_call(functools.partial(finish_body, kind, last), grid=(per // b...  18.6 us
    ppermute x14, starting transfers between devices, swap_near(): lax.ppermute(array, 'gx', [(i, i + 1 - 2 * (i % 2)) for i in range(count)])  15.7 us
    ppermute x14, starting transfers between devices, swap_far(): lax.ppermute(array, 'gx', [(i, (i + 1) % count) for i in odd] + [((i + 1)...  13.1 us
    pallas_call x4, Pallas kernels, sweep_part(): pl.pallas_call(sweep_body, in_specs=[pl.BlockSpec(memory_space=pltpu.SMEM...  3.4 us
  transfers between devices with their start and end apart: 28, of which 9 were waited for; matrix products, arithmetic and copies ran while one was open for 5% of the time, Pallas kernels for 38%

profile of v5, /device:TPU:1, one launch (start us, length us, event | category | flops | bytes accessed | tf_op | source)
XLA Modules:
  0.0 126.1 jit_solution(8563600780851543819)
XLA Ops:
  0.6 1.3 %fusion.9 = (f32[1,256,256]{2,1,0:T(8,128)S(1)}, f32[1,256,256]{2,1,0:T(8,128)S(1)}, f32[1,256,256]{2,1,0:T(8,128)S(1)}, f32[1,256,256]{2,1,0:T(8,128)S(1)}) fusion(s32[4,256,256]{2,1,0:T(8,128)} %param.9, pred[]{:T(512)S(6)} %eq.3, f32[4,256,256]{2,1,0:T(8,128)} %param.8), kind=kLoop, calls=%fused_computation.30 | loop fusion | flops 786432 | bytes 2097153 | tf_op jit(solution)/shard_map/jit(_where)/select_n | solution.py:324
  1.9 0.3 copy_bitcast_fusion.2
  2.3 2.7 %collective-permute-start = (f32[1,32,8,256]{3,2,1,0:T(8,128)S(1)}, f32[1,32,8,256]{3,2,1,0:T(8,128)S(1)}, u32[]{:S(2)}, u32[]{:S(2)}) collective-permute-start(f32[1,32,8,256]{3,2,1,0:T(8,128)S(1)} %get-tuple-element.131.far_ref), channel_id=1, source_target_pairs={{1,2},{3,4},{5,6},{7,8},{9,10},{11,12},{13,14},{15,0},{2,1},{4,3},... | collective-permute-start | bytes 786440 | tf_op jit(solution)/shard_map/ppermute | solution.py:300
  4.9 2.9 %collective-permute-start.1 = (f32[1,32,8,256]{3,2,1,0:T(8,128)S(1)}, f32[1,32,8,256]{3,2,1,0:T(8,128)S(1)}, u32[]{:S(2)}, u32[]{:S(2)}) collective-permute-start(f32[1,32,8,256]{3,2,1,0:T(8,128)S(1)} %get-tuple-element.130.near_ref), channel_id=1, source_target_pairs={{0,1},{1,0},{2,3},{3,2},{4,5},{5,4},{6,7},{7,6},{8,9},{9,8},{10,11... | collective-permute-start | bytes 786440 | tf_op jit(solution)/shard_map/ppermute | solution.py:305
  7.8 0.1 convert_element_type.21
  7.9 0.6 copy.37
  8.5 0.6 copy-done
  9.1 1.2 bitcast_multiply_fusion.fixed_ref
  10.3 0.1 slice_select_fusion
  10.4 0.6 copy.38
  11.1 1.0 sweep_part.4
  12.1 0.2 fusion.4.far_ref
  12.3 1.5 %collective-permute-start.2 = (f32[1,32,8,256]{3,2,1,0:T(8,128)S(1)}, f32[1,32,8,256]{3,2,1,0:T(8,128)S(1)}, u32[]{:S(2)}, u32[]{:S(2)}) collective-permute-start(f32[1,32,8,256]{3,2,1,0:T(8,128)S(1)} %fusion.4.far_ref), channel_id=1, source_target_pairs={{1,2},{3,4},{5,6},{7,8},{9,10},{11,12},{13,14},{15,0},{2,1},{4,3},... | collective-permute-start | bytes 786440 | tf_op jit(solution)/shard_map/ppermute | solution.py:300
  13.8 0.2 fusion.near_ref
  14.0 2.9 %collective-permute-start.3 = (f32[1,32,8,256]{3,2,1,0:T(8,128)S(1)}, f32[1,32,8,256]{3,2,1,0:T(8,128)S(1)}, u32[]{:S(2)}, u32[]{:S(2)}) collective-permute-start(f32[1,32,8,256]{3,2,1,0:T(8,128)S(1)} %fusion.near_ref), channel_id=1, source_target_pairs={{0,1},{1,0},{2,3},{3,2},{4,5},{5,4},{6,7},{7,6},{8,9},{9,8},{10,11... | collective-permute-start | bytes 786440 | tf_op jit(solution)/shard_map/ppermute | solution.py:305
  17.0 5.6 %local_part.5 = (f32[4,32,8,256]{3,2,1,0:T(8,128)S(1)}, f32[4,32,8,256]{3,2,1,0:T(8,128)S(1)}) custom-call(f32[4,32,8,256]{3,2,1,0:T(8,128)S(1)} %bitcast.64), custom_call_target="tpu_custom_call" | custom-call | flops 34078720 | bytes 3145728 | tf_op jit(solution)/shard_map/local_part/pallas_call | solution.py:149
  22.6 0.8 sweep_part.5
  23.4 0.2 collective-permute-done.2
  23.7 0.2 fusion.5.far_ref
  23.9 2.5 %collective-permute-start.4 = (f32[1,32,8,256]{3,2,1,0:T(8,128)S(1)}, f32[1,32,8,256]{3,2,1,0:T(8,128)S(1)}, u32[]{:S(2)}, u32[]{:S(2)}) collective-permute-start(f32[1,32,8,256]{3,2,1,0:T(8,128)S(1)} %fusion.5.far_ref), channel_id=1, source_target_pairs={{1,2},{3,4},{5,6},{7,8},{9,10},{11,12},{13,14},{15,0},{2,1},{4,3},... | collective-permute-start | bytes 786440 | tf_op jit(solution)/shard_map/ppermute | solution.py:300
  26.4 0.2 fusion.1.near_ref
  26.6 1.8 %collective-permute-start.5 = (f32[1,32,8,256]{3,2,1,0:T(8,128)S(1)}, f32[1,32,8,256]{3,2,1,0:T(8,128)S(1)}, u32[]{:S(2)}, u32[]{:S(2)}) collective-permute-start(f32[1,32,8,256]{3,2,1,0:T(8,128)S(1)} %fusion.1.near_ref), channel_id=1, source_target_pairs={{0,1},{1,0},{2,3},{3,2},{4,5},{5,4},{6,7},{7,6},{8,9},{9,8},{10,11... | collective-permute-start | bytes 786440 | tf_op jit(solution)/shard_map/ppermute | solution.py:305
  28.6 0.8 sweep_part.6
  29.4 12.9 %collective-permute-done.4 = f32[1,32,8,256]{3,2,1,0:T(8,128)S(1)} collective-permute-done((f32[1,32,8,256]{3,2,1,0:T(8,128)S(1)}, f32[1,32,8,256]{3,2,1,0:T(8,128)S(1)}, u32[]{:S(2)}, u32[]{:S(2)}) %collective-permute-start.4) | collective-permute-done | bytes 262176 | tf_op jit(solution)/shard_map/ppermute | solution.py:300
  42.3 0.2 fusion.6.far_ref
  42.5 0.7 collective-permute-start.6
  43.3 0.2 fusion.2.near_ref
  43.6 0.8 sweep_part.7
  44.4 5.0 %collective-permute-done.6 = f32[1,32,8,256]{3,2,1,0:T(8,128)S(1)} collective-permute-done((f32[1,32,8,256]{3,2,1,0:T(8,128)S(1)}, f32[1,32,8,256]{3,2,1,0:T(8,128)S(1)}, u32[]{:S(2)}, u32[]{:S(2)}) %collective-permute-start.6) | collective-permute-done | bytes 262176 | tf_op jit(solution)/shard_map/ppermute | solution.py:300
  49.4 0.4 broadcast_select_fusion.3
  49.7 0.2 pad_maximum_fusion
  49.9 1.9 %finish_part.10 = (f32[4,16,8,256]{3,2,1,0:T(8,128)S(1)}, f32[3,16,8,256]{3,2,1,0:T(8,128)S(1)}, f32[3,16,8,256]{3,2,1,0:T(8,128)S(1)}) custom-call(s32[1]{0:T(128)} %bitcast.parity_ref.refs_0_, f32[4,16,8,256]{3,2,1,0:T(8,128)S(1)} %get-tuple-element.117.refs_1_, f32[3,16,8,256]{3,2,1,0:T(8,128)S(1)} %collective-permute-done.8.refs_2_, ...), custom_call_target="tpu_custom_call" | custom-call | flops 10485760 | bytes 4194304 | tf_op jit(solution)/shard_map/finish_part/pallas_call | solution.py:224
  51.8 0.7 collective-permute-start.10
  52.6 2.7 %collective-permute-start.11 = (f32[3,16,8,256]{3,2,1,0:T(8,128)S(1)}, f32[3,16,8,256]{3,2,1,0:T(8,128)S(1)}, u32[]{:S(2)}, u32[]{:S(2)}) collective-permute-start(f32[3,16,8,256]{3,2,1,0:T(8,128)S(1)} %get-tuple-element.88), channel_id=1, source_target_pairs={{0,1},{1,0},{2,3},{3,2},{4,5},{5,4},{6,7},{7,6},{8,9},{9,8},{10,11... | collective-permute-start | bytes 1179656 | tf_op jit(solution)/shard_map/ppermute | solution.py:305
  55.2 1.9 %finish_part.11 = (f32[4,16,8,256]{3,2,1,0:T(8,128)S(1)}, f32[3,16,8,256]{3,2,1,0:T(8,128)S(1)}, f32[3,16,8,256]{3,2,1,0:T(8,128)S(1)}) custom-call(s32[1]{0:T(128)} %bitcast.parity_ref.refs_0_, f32[4,16,8,256]{3,2,1,0:T(8,128)S(1)} %get-tuple-element.116.refs_1_, f32[3,16,8,256]{3,2,1,0:T(8,128)S(1)} %collective-permute-done.12.refs_2_, ...), custom_call_target="tpu_custom_call" | custom-call | flops 10485760 | bytes 4194304 | tf_op jit(solution)/shard_map/finish_part/pallas_call | solution.py:224
  57.2 1.6 %collective-permute-start.17 = (f32[3,16,8,256]{3,2,1,0:T(8,128)S(1)}, f32[3,16,8,256]{3,2,1,0:T(8,128)S(1)}, u32[]{:S(2)}, u32[]{:S(2)}) collective-permute-start(f32[3,16,8,256]{3,2,1,0:T(8,128)S(1)} %get-tuple-element.94), channel_id=1, source_target_pairs={{0,1},{1,0},{2,3},{3,2},{4,5},{5,4},{6,7},{7,6},{8,9},{9,8},{10,11... | collective-permute-start | bytes 1179656 | tf_op jit(solution)/shard_map/ppermute | solution.py:305
  58.8 5.6 %local_part.6.refs_4_ = f32[4,32,8,256]{3,2,1,0:T(8,128)S(1)} custom-call(f32[4,16,8,256]{3,2,1,0:T(8,128)S(1)} %get-tuple-element.86.refs_0_.refs_1_, f32[4,16,8,256]{3,2,1,0:T(8,128)S(1)} %get-tuple-element.89.refs_1_, f32[4,32,8,256]{3,2,1,0:T(8,128)S(1)} %get-tuple-element.118.refs_6_.refs_2_.refs_5_), custom_call_target="tpu_custom_call" | custom-call | flops 34078720 | bytes 3145728 | tf_op jit(solution)/shard_map/local_part/pallas_call | solution.py:149
  64.4 3.1 %collective-permute-done.10.refs_2_ = f32[3,16,8,256]{3,2,1,0:T(8,128)S(1)} collective-permute-done((f32[3,16,8,256]{3,2,1,0:T(8,128)S(1)}, f32[3,16,8,256]{3,2,1,0:T(8,128)S(1)}, u32[]{:S(2)}, u32[]{:S(2)}) %collective-permute-start.10) | collective-permute-done | bytes 393248 | tf_op jit(solution)/shard_map/ppermute | solution.py:300
  67.5 1.9 %finish_part.12 = (f32[4,16,8,256]{3,2,1,0:T(8,128)S(1)}, f32[3,16,8,256]{3,2,1,0:T(8,128)S(1)}, f32[3,16,8,256]{3,2,1,0:T(8,128)S(1)}) custom-call(s32[1]{0:T(128)} %bitcast.parity_ref.refs_0_, f32[4,16,8,256]{3,2,1,0:T(8,128)S(1)} %get-tuple-element.86.refs_0_.refs_1_, f32[3,16,8,256]{3,2,1,0:T(8,128)S(1)} %collective-permute-done.10.refs_2_, ...), custom_call_target="tpu_custom_call" | custom-call | flops 10485760 | bytes 4194304 | tf_op jit(solution)/shard_map/finish_part/pallas_call | solution.py:224
  69.4 0.7 collective-permute-start.14
  70.2 5.8 %collective-permute-done.16.refs_2_ = f32[3,16,8,256]{3,2,1,0:T(8,128)S(1)} collective-permute-done((f32[3,16,8,256]{3,2,1,0:T(8,128)S(1)}, f32[3,16,8,256]{3,2,1,0:T(8,128)S(1)}, u32[]{:S(2)}, u32[]{:S(2)}) %collective-permute-start.16) | collective-permute-done | bytes 393248 | tf_op jit(solution)/shard_map/ppermute | solution.py:300
  75.9 1.9 %finish_part.13 = (f32[4,16,8,256]{3,2,1,0:T(8,128)S(1)}, f32[3,16,8,256]{3,2,1,0:T(8,128)S(1)}, f32[3,16,8,256]{3,2,1,0:T(8,128)S(1)}) custom-call(s32[1]{0:T(128)} %bitcast.parity_ref.refs_0_, f32[4,16,8,256]{3,2,1,0:T(8,128)S(1)} %get-tuple-element.89.refs_1_, f32[3,16,8,256]{3,2,1,0:T(8,128)S(1)} %collective-permute-done.16.refs_2_, ...), custom_call_target="tpu_custom_call" | custom-call | flops 10485760 | bytes 4194304 | tf_op jit(solution)/shard_map/finish_part/pallas_call | solution.py:224
  77.8 0.7 collective-permute-start.20
  78.6 5.6 %local_part.7.refs_4_ = f32[4,32,8,256]{3,2,1,0:T(8,128)S(1)} custom-call(f32[4,16,8,256]{3,2,1,0:T(8,128)S(1)} %get-tuple-element.90.refs_0_.refs_1_, f32[4,16,8,256]{3,2,1,0:T(8,128)S(1)} %get-tuple-element.95.refs_1_, f32[4,32,8,256]{3,2,1,0:T(8,128)S(1)} %get-tuple-element.118.refs_6_.refs_2_.refs_5_), custom_call_target="tpu_custom_call" | custom-call | flops 34078720 | bytes 3145728 | tf_op jit(solution)/shard_map/local_part/pallas_call | solution.py:149
  84.2 0.2 collective-permute-done.14.refs_2_
  84.4 1.9 %finish_part.14 = (f32[4,16,8,256]{3,2,1,0:T(8,128)S(1)}, f32[3,16,8,256]{3,2,1,0:T(8,128)S(1)}, f32[3,16,8,256]{3,2,1,0:T(8,128)S(1)}) custom-call(s32[1]{0:T(128)} %bitcast.parity_ref.refs_0_, f32[4,16,8,256]{3,2,1,0:T(8,128)S(1)} %get-tuple-element.90.refs_0_.refs_1_, f32[3,16,8,256]{3,2,1,0:T(8,128)S(1)} %collective-permute-done.14.refs_2_, ...), custom_call_target="tpu_custom_call" | custom-call | flops 10485760 | bytes 4194304 | tf_op jit(solution)/shard_map/finish_part/pallas_call | solution.py:224
  86.3 1.0 collective-permute-start.18
  87.3 2.0 %collective-permute-start.19 = (f32[3,16,8,256]{3,2,1,0:T(8,128)S(1)}, f32[3,16,8,256]{3,2,1,0:T(8,128)S(1)}, u32[]{:S(2)}, u32[]{:S(2)}) collective-permute-start(f32[3,16,8,256]{3,2,1,0:T(8,128)S(1)} %get-tuple-element.98), channel_id=1, source_target_pairs={{0,1},{1,0},{2,3},{3,2},{4,5},{5,4},{6,7},{7,6},{8,9},{9,8},{10,11... | collective-permute-start | bytes 1179656 | tf_op jit(solution)/shard_map/ppermute | solution.py:305
  89.2 1.9 %finish_part.15 = (f32[4,16,8,256]{3,2,1,0:T(8,128)S(1)}, f32[3,16,8,256]{3,2,1,0:T(8,128)S(1)}, f32[3,16,8,256]{3,2,1,0:T(8,128)S(1)}) custom-call(s32[1]{0:T(128)} %bitcast.parity_ref.refs_0_, f32[4,16,8,256]{3,2,1,0:T(8,128)S(1)} %get-tuple-element.95.refs_1_, f32[3,16,8,256]{3,2,1,0:T(8,128)S(1)} %collective-permute-done.20.refs_2_, ...), custom_call_target="tpu_custom_call" | custom-call | flops 10485760 | bytes 4194304 | tf_op jit(solution)/shard_map/finish_part/pallas_call | solution.py:224
  91.1 0.3 collective-permute-start.24
  91.4 1.7 %collective-permute-start.25 = (f32[3,16,8,256]{3,2,1,0:T(8,128)S(1)}, f32[3,16,8,256]{3,2,1,0:T(8,128)S(1)}, u32[]{:S(2)}, u32[]{:S(2)}) collective-permute-start(f32[3,16,8,256]{3,2,1,0:T(8,128)S(1)} %get-tuple-element.106), channel_id=1, source_target_pairs={{0,1},{1,0},{2,3},{3,2},{4,5},{5,4},{6,7},{7,6},{8,9},{9,8},{10,11... | collective-permute-start | bytes 1179656 | tf_op jit(solution)/shard_map/ppermute | solution.py:305
  93.2 5.6 %local_part.8.refs_4_ = f32[4,32,8,256]{3,2,1,0:T(8,128)S(1)} custom-call(f32[4,16,8,256]{3,2,1,0:T(8,128)S(1)} %get-tuple-element.96.refs_0_.refs_1_.refs_5_, f32[4,16,8,256]{3,2,1,0:T(8,128)S(1)} %get-tuple-element.101.refs_1_.refs_5_, f32[4,32,8,256]{3,2,1,0:T(8,128)S(1)} %constant_dynamic-update-slice_fusion.refs_2_), custom_call_target="tpu_custom_call" | custom-call | flops 34078720 | bytes 3145728 | tf_op jit(solution)/shard_map/local_part/pallas_call | solution.py:149
  98.8 3.1 %collective-permute-done.18.refs_2_ = f32[3,16,8,256]{3,2,1,0:T(8,128)S(1)} collective-permute-done((f32[3,16,8,256]{3,2,1,0:T(8,128)S(1)}, f32[3,16,8,256]{3,2,1,0:T(8,128)S(1)}, u32[]{:S(2)}, u32[]{:S(2)}) %collective-permute-start.18) | collective-permute-done | bytes 393248 | tf_op jit(solution)/shard_map/ppermute | solution.py:300
  102.0 1.9 %finish_part.16 = (f32[4,16,8,256]{3,2,1,0:T(8,128)S(1)}, f32[3,16,8,256]{3,2,1,0:T(8,128)S(1)}, f32[3,16,8,256]{3,2,1,0:T(8,128)S(1)}) custom-call(s32[1]{0:T(128)} %bitcast.parity_ref.refs_0_, f32[4,16,8,256]{3,2,1,0:T(8,128)S(1)} %get-tuple-element.96.refs_0_.refs_1_.refs_5_, f32[3,16,8,256]{3,2,1,0:T(8,128)S(1)} %collective-permute-done.18.refs_2_, ...), custom_call_target="tpu_custom_call" | custom-call | flops 10485760 | bytes 4194304 | tf_op jit(solution)/shard_map/finish_part/pallas_call | solution.py:224
  103.8 1.0 collective-permute-start.22
  104.8 5.6 %collective-permute-done.24.refs_2_ = f32[3,16,8,256]{3,2,1,0:T(8,128)S(1)} collective-permute-done((f32[3,16,8,256]{3,2,1,0:T(8,128)S(1)}, f32[3,16,8,256]{3,2,1,0:T(8,128)S(1)}, u32[]{:S(2)}, u32[]{:S(2)}) %collective-permute-start.24) | collective-permute-done | bytes 393248 | tf_op jit(solution)/shard_map/ppermute | solution.py:300
  110.4 1.9 %finish_part.17 = (f32[4,16,8,256]{3,2,1,0:T(8,128)S(1)}, f32[3,16,8,256]{3,2,1,0:T(8,128)S(1)}, f32[3,16,8,256]{3,2,1,0:T(8,128)S(1)}) custom-call(s32[1]{0:T(128)} %bitcast.parity_ref.refs_0_, f32[4,16,8,256]{3,2,1,0:T(8,128)S(1)} %get-tuple-element.101.refs_1_.refs_5_, f32[3,16,8,256]{3,2,1,0:T(8,128)S(1)} %collective-permute-done.24.refs_2_, ...), custom_call_target="tpu_custom_call" | custom-call | flops 10485760 | bytes 4194304 | tf_op jit(solution)/shard_map/finish_part/pallas_call | solution.py:224
  112.3 1.0 collective-permute-start.26
  113.3 1.3 %copy.12 = f32[4,8,32,256]{3,2,1,0:T(8,128)} copy(f32[4,8,32,256]{3,1,2,0:T(8,128)S(1)} %get-tuple-element.119) | data formatting | bytes 2097152 | tf_op jit(solution)/shard_map/transpose | solution.py:294
  114.6 5.6 %local_part.9.refs_4_ = f32[4,32,8,256]{3,2,1,0:T(8,128)S(1)} custom-call(f32[4,16,8,256]{3,2,1,0:T(8,128)S(1)} %get-tuple-element.102.refs_0_.refs_1_, f32[4,16,8,256]{3,2,1,0:T(8,128)S(1)} %get-tuple-element.109.refs_1_, f32[4,32,8,256]{3,2,1,0:T(8,128)S(1)} %constant_dynamic-update-slice_fusion.refs_2_), custom_call_target="tpu_custom_call" | custom-call | flops 34078720 | bytes 3145728 | tf_op jit(solution)/shard_map/local_part/pallas_call | solution.py:149
  120.2 1.8 %finish_part.18 = f32[4,16,8,256]{3,2,1,0:T(8,128)S(1)} custom-call(s32[1]{0:T(128)} %bitcast.parity_ref.refs_0_, f32[4,16,8,256]{3,2,1,0:T(8,128)S(1)} %get-tuple-element.102.refs_0_.refs_1_, f32[3,16,8,256]{3,2,1,0:T(8,128)S(1)} %collective-permute-done.22.refs_2_, f32[3,16,8,256]{3,2,1,0:T(8,128)S(1)} %collective-permute-done.23.refs_3_, ...), custom_call_target="tpu_custom_call" | custom-call | flops 10485760 | bytes 4194304 | tf_op jit(solution)/shard_map/finish_part/pallas_call | solution.py:224
  122.0 1.0 collective-permute-done.26.refs_2_
  123.0 1.8 %finish_part.19 = f32[4,16,8,256]{3,2,1,0:T(8,128)S(1)} custom-call(s32[1]{0:T(128)} %bitcast.parity_ref.refs_0_, f32[4,16,8,256]{3,2,1,0:T(8,128)S(1)} %get-tuple-element.109.refs_1_, f32[3,16,8,256]{3,2,1,0:T(8,128)S(1)} %collective-permute-done.26.refs_2_, f32[3,16,8,256]{3,2,1,0:T(8,128)S(1)} %collective-permute-done.27.refs_3_, ...), custom_call_target="tpu_custom_call" | custom-call | flops 10485760 | bytes 4194304 | tf_op jit(solution)/shard_map/finish_part/pallas_call | solution.py:224
  124.8 1.3 %copy.13 = f32[4,8,32,256]{3,2,1,0:T(8,128)} copy(f32[4,8,32,256]{3,1,2,0:T(8,128)S(1)} %bitcast_dynamic-update-slice_fusion) | data formatting | bytes 2097152 | tf_op jit(solution)/shard_map/scatter | solution.py:371
  (42 shorter events, 0.9 us)
Async XLA Ops:
  1.9 5.9 %copy-start.1 = (s32[4,256,256]{2,1,0:T(8,128)S(1)}, s32[4,256,256]{2,1,0:T(8,128)}, u32[]{:S(2)}) copy-start(s32[4,256,256]{2,1,0:T(8,128)} %param.9) | copy-start | bytes 3145732
  2.3 9.8 %collective-permute-start = (f32[1,32,8,256]{3,2,1,0:T(8,128)S(1)}, f32[1,32,8,256]{3,2,1,0:T(8,128)S(1)}, u32[]{:S(2)}, u32[]{:S(2)}) collective-permute-start(f32[1,32,8,256]{3,2,1,0:T(8,128)S(1)} %get-tuple-element.131.far_ref), channel_id=1, source_target_pairs={{1,2},{3,4},{5,6},{7,8},{9,10},{11,12},{13,14},{15,0},{2,1},{4,3},... | collective-permute-start | bytes 786440 | tf_op jit(solution)/shard_map/ppermute | solution.py:300
  4.9 3.0 %copy-start.2 = (f32[4,256,256]{2,1,0:T(8,128)S(1)}, f32[4,256,256]{2,1,0:T(8,128)}, u32[]{:S(2)}) copy-start(f32[4,256,256]{2,1,0:T(8,128)} %param.7) | copy-start | bytes 3145732
  4.9 8.9 %collective-permute-start.1 = (f32[1,32,8,256]{3,2,1,0:T(8,128)S(1)}, f32[1,32,8,256]{3,2,1,0:T(8,128)S(1)}, u32[]{:S(2)}, u32[]{:S(2)}) collective-permute-start(f32[1,32,8,256]{3,2,1,0:T(8,128)S(1)} %get-tuple-element.130.near_ref), channel_id=1, source_target_pairs={{0,1},{1,0},{2,3},{3,2},{4,5},{5,4},{6,7},{7,6},{8,9},{9,8},{10,11... | collective-permute-start | bytes 786440 | tf_op jit(solution)/shard_map/ppermute | solution.py:305
  7.9 1.2 copy-start
  12.3 11.4 %collective-permute-start.2 = (f32[1,32,8,256]{3,2,1,0:T(8,128)S(1)}, f32[1,32,8,256]{3,2,1,0:T(8,128)S(1)}, u32[]{:S(2)}, u32[]{:S(2)}) collective-permute-start(f32[1,32,8,256]{3,2,1,0:T(8,128)S(1)} %fusion.4.far_ref), channel_id=1, source_target_pairs={{1,2},{3,4},{5,6},{7,8},{9,10},{11,12},{13,14},{15,0},{2,1},{4,3},... | collective-permute-start | bytes 786440 | tf_op jit(solution)/shard_map/ppermute | solution.py:300
  14.0 12.4 %collective-permute-start.3 = (f32[1,32,8,256]{3,2,1,0:T(8,128)S(1)}, f32[1,32,8,256]{3,2,1,0:T(8,128)S(1)}, u32[]{:S(2)}, u32[]{:S(2)}) collective-permute-start(f32[1,32,8,256]{3,2,1,0:T(8,128)S(1)} %fusion.near_ref), channel_id=1, source_target_pairs={{0,1},{1,0},{2,3},{3,2},{4,5},{5,4},{6,7},{7,6},{8,9},{9,8},{10,11... | collective-permute-start | bytes 786440 | tf_op jit(solution)/shard_map/ppermute | solution.py:305
  17.0 33.0 %collective-permute-start.8 = (f32[3,16,8,256]{3,2,1,0:T(8,128)S(1)}, f32[3,16,8,256]{3,2,1,0:T(8,128)S(1)}, u32[]{:S(2)}, u32[]{:S(2)}) collective-permute-start(f32[3,16,8,256]{3,2,1,0:T(8,128)S(1)} %get-tuple-element.129), channel_id=1, source_target_pairs={{1,2},{3,4},{5,6},{7,8},{9,10},{11,12},{13,14},{15,0},{2,1},{4,3},... | collective-permute-start | bytes 1179656 | tf_op jit(solution)/shard_map/ppermute | solution.py:300
  23.9 18.5 %collective-permute-start.4 = (f32[1,32,8,256]{3,2,1,0:T(8,128)S(1)}, f32[1,32,8,256]{3,2,1,0:T(8,128)S(1)}, u32[]{:S(2)}, u32[]{:S(2)}) collective-permute-start(f32[1,32,8,256]{3,2,1,0:T(8,128)S(1)} %fusion.5.far_ref), channel_id=1, source_target_pairs={{1,2},{3,4},{5,6},{7,8},{9,10},{11,12},{13,14},{15,0},{2,1},{4,3},... | collective-permute-start | bytes 786440 | tf_op jit(solution)/shard_map/ppermute | solution.py:300
  26.6 16.7 %collective-permute-start.5 = (f32[1,32,8,256]{3,2,1,0:T(8,128)S(1)}, f32[1,32,8,256]{3,2,1,0:T(8,128)S(1)}, u32[]{:S(2)}, u32[]{:S(2)}) collective-permute-start(f32[1,32,8,256]{3,2,1,0:T(8,128)S(1)} %fusion.1.near_ref), channel_id=1, source_target_pairs={{0,1},{1,0},{2,3},{3,2},{4,5},{5,4},{6,7},{7,6},{8,9},{9,8},{10,11... | collective-permute-start | bytes 786440 | tf_op jit(solution)/shard_map/ppermute | solution.py:305
  28.5 21.5 %collective-permute-start.9 = (f32[3,16,8,256]{3,2,1,0:T(8,128)S(1)}, f32[3,16,8,256]{3,2,1,0:T(8,128)S(1)}, u32[]{:S(2)}, u32[]{:S(2)}) collective-permute-start(f32[3,16,8,256]{3,2,1,0:T(8,128)S(1)} %get-tuple-element.127), channel_id=1, source_target_pairs={{0,1},{1,0},{2,3},{3,2},{4,5},{5,4},{6,7},{7,6},{8,9},{9,8},{10,11... | collective-permute-start | bytes 1179656 | tf_op jit(solution)/shard_map/ppermute | solution.py:305
  28.5 26.7 %collective-permute-start.12 = (f32[3,16,8,256]{3,2,1,0:T(8,128)S(1)}, f32[3,16,8,256]{3,2,1,0:T(8,128)S(1)}, u32[]{:S(2)}, u32[]{:S(2)}) collective-permute-start(f32[3,16,8,256]{3,2,1,0:T(8,128)S(1)} %get-tuple-element.128), channel_id=1, source_target_pairs={{1,2},{3,4},{5,6},{7,8},{9,10},{11,12},{13,14},{15,0},{2,1},{4,3},... | collective-permute-start | bytes 1179656 | tf_op jit(solution)/shard_map/ppermute | solution.py:300
  42.5 6.8 %collective-permute-start.6 = (f32[1,32,8,256]{3,2,1,0:T(8,128)S(1)}, f32[1,32,8,256]{3,2,1,0:T(8,128)S(1)}, u32[]{:S(2)}, u32[]{:S(2)}) collective-permute-start(f32[1,32,8,256]{3,2,1,0:T(8,128)S(1)} %fusion.6.far_ref), channel_id=1, source_target_pairs={{1,2},{3,4},{5,6},{7,8},{9,10},{11,12},{13,14},{15,0},{2,1},{4,3},... | collective-permute-start | bytes 786440 | tf_op jit(solution)/shard_map/ppermute | solution.py:300
  43.4 5.9 %collective-permute-start.7 = (f32[1,32,8,256]{3,2,1,0:T(8,128)S(1)}, f32[1,32,8,256]{3,2,1,0:T(8,128)S(1)}, u32[]{:S(2)}, u32[]{:S(2)}) collective-permute-start(f32[1,32,8,256]{3,2,1,0:T(8,128)S(1)} %fusion.2.near_ref), channel_id=1, source_target_pairs={{0,1},{1,0},{2,3},{3,2},{4,5},{5,4},{6,7},{7,6},{8,9},{9,8},{10,11... | collective-permute-start | bytes 786440 | tf_op jit(solution)/shard_map/ppermute | solution.py:305
  49.4 5.9 %collective-permute-start.13 = (f32[3,16,8,256]{3,2,1,0:T(8,128)S(1)}, f32[3,16,8,256]{3,2,1,0:T(8,128)S(1)}, u32[]{:S(2)}, u32[]{:S(2)}) collective-permute-start(f32[3,16,8,256]{3,2,1,0:T(8,128)S(1)} %get-tuple-element.126), channel_id=1, source_target_pairs={{0,1},{1,0},{2,3},{3,2},{4,5},{5,4},{6,7},{7,6},{8,9},{9,8},{10,11... | collective-permute-start | bytes 1179656 | tf_op jit(solution)/shard_map/ppermute | solution.py:305
  51.8 15.7 %collective-permute-start.10 = (f32[3,16,8,256]{3,2,1,0:T(8,128)S(1)}, f32[3,16,8,256]{3,2,1,0:T(8,128)S(1)}, u32[]{:S(2)}, u32[]{:S(2)}) collective-permute-start(f32[3,16,8,256]{3,2,1,0:T(8,128)S(1)} %get-tuple-element.87), channel_id=1, source_target_pairs={{1,2},{3,4},{5,6},{7,8},{9,10},{11,12},{13,14},{15,0},{2,1},{4,3},... | collective-permute-start | bytes 1179656 | tf_op jit(solution)/shard_map/ppermute | solution.py:300
  52.6 15.0 %collective-permute-start.11 = (f32[3,16,8,256]{3,2,1,0:T(8,128)S(1)}, f32[3,16,8,256]{3,2,1,0:T(8,128)S(1)}, u32[]{:S(2)}, u32[]{:S(2)}) collective-permute-start(f32[3,16,8,256]{3,2,1,0:T(8,128)S(1)} %get-tuple-element.88), channel_id=1, source_target_pairs={{0,1},{1,0},{2,3},{3,2},{4,5},{5,4},{6,7},{7,6},{8,9},{9,8},{10,11... | collective-permute-start | bytes 1179656 | tf_op jit(solution)/shard_map/ppermute | solution.py:305
  57.1 18.8 %collective-permute-start.16 = (f32[3,16,8,256]{3,2,1,0:T(8,128)S(1)}, f32[3,16,8,256]{3,2,1,0:T(8,128)S(1)}, u32[]{:S(2)}, u32[]{:S(2)}) collective-permute-start(f32[3,16,8,256]{3,2,1,0:T(8,128)S(1)} %get-tuple-element.93), channel_id=1, source_target_pairs={{1,2},{3,4},{5,6},{7,8},{9,10},{11,12},{13,14},{15,0},{2,1},{4,3},... | collective-permute-start | bytes 1179656 | tf_op jit(solution)/shard_map/ppermute | solution.py:300
  57.2 18.8 %collective-permute-start.17 = (f32[3,16,8,256]{3,2,1,0:T(8,128)S(1)}, f32[3,16,8,256]{3,2,1,0:T(8,128)S(1)}, u32[]{:S(2)}, u32[]{:S(2)}) collective-permute-start(f32[3,16,8,256]{3,2,1,0:T(8,128)S(1)} %get-tuple-element.94), channel_id=1, source_target_pairs={{0,1},{1,0},{2,3},{3,2},{4,5},{5,4},{6,7},{7,6},{8,9},{9,8},{10,11... | collective-permute-start | bytes 1179656 | tf_op jit(solution)/shard_map/ppermute | solution.py:305
  69.4 14.9 %collective-permute-start.14 = (f32[3,16,8,256]{3,2,1,0:T(8,128)S(1)}, f32[3,16,8,256]{3,2,1,0:T(8,128)S(1)}, u32[]{:S(2)}, u32[]{:S(2)}) collective-permute-start(f32[3,16,8,256]{3,2,1,0:T(8,128)S(1)} %get-tuple-element.91), channel_id=1, source_target_pairs={{1,2},{3,4},{5,6},{7,8},{9,10},{11,12},{13,14},{15,0},{2,1},{4,3},... | collective-permute-start | bytes 1179656 | tf_op jit(solution)/shard_map/ppermute | solution.py:300
  70.2 14.2 %collective-permute-start.15 = (f32[3,16,8,256]{3,2,1,0:T(8,128)S(1)}, f32[3,16,8,256]{3,2,1,0:T(8,128)S(1)}, u32[]{:S(2)}, u32[]{:S(2)}) collective-permute-start(f32[3,16,8,256]{3,2,1,0:T(8,128)S(1)} %get-tuple-element.92), channel_id=1, source_target_pairs={{0,1},{1,0},{2,3},{3,2},{4,5},{5,4},{6,7},{7,6},{8,9},{9,8},{10,11... | collective-permute-start | bytes 1179656 | tf_op jit(solution)/shard_map/ppermute | solution.py:305
  77.8 11.4 %collective-permute-start.20 = (f32[3,16,8,256]{3,2,1,0:T(8,128)S(1)}, f32[3,16,8,256]{3,2,1,0:T(8,128)S(1)}, u32[]{:S(2)}, u32[]{:S(2)}) collective-permute-start(f32[3,16,8,256]{3,2,1,0:T(8,128)S(1)} %get-tuple-element.99), channel_id=1, source_target_pairs={{1,2},{3,4},{5,6},{7,8},{9,10},{11,12},{13,14},{15,0},{2,1},{4,3},... | collective-permute-start | bytes 1179656 | tf_op jit(solution)/shard_map/ppermute | solution.py:300
  78.6 10.6 %collective-permute-start.21 = (f32[3,16,8,256]{3,2,1,0:T(8,128)S(1)}, f32[3,16,8,256]{3,2,1,0:T(8,128)S(1)}, u32[]{:S(2)}, u32[]{:S(2)}) collective-permute-start(f32[3,16,8,256]{3,2,1,0:T(8,128)S(1)} %get-tuple-element.100), channel_id=1, source_target_pairs={{0,1},{1,0},{2,3},{3,2},{4,5},{5,4},{6,7},{7,6},{8,9},{9,8},{10,11... | collective-permute-start | bytes 1179656 | tf_op jit(solution)/shard_map/ppermute | solution.py:305
  86.3 15.7 %collective-permute-start.18 = (f32[3,16,8,256]{3,2,1,0:T(8,128)S(1)}, f32[3,16,8,256]{3,2,1,0:T(8,128)S(1)}, u32[]{:S(2)}, u32[]{:S(2)}) collective-permute-start(f32[3,16,8,256]{3,2,1,0:T(8,128)S(1)} %get-tuple-element.97), channel_id=1, source_target_pairs={{1,2},{3,4},{5,6},{7,8},{9,10},{11,12},{13,14},{15,0},{2,1},{4,3},... | collective-permute-start | bytes 1179656 | tf_op jit(solution)/shard_map/ppermute | solution.py:300
  87.3 14.7 %collective-permute-start.19 = (f32[3,16,8,256]{3,2,1,0:T(8,128)S(1)}, f32[3,16,8,256]{3,2,1,0:T(8,128)S(1)}, u32[]{:S(2)}, u32[]{:S(2)}) collective-permute-start(f32[3,16,8,256]{3,2,1,0:T(8,128)S(1)} %get-tuple-element.98), channel_id=1, source_target_pairs={{0,1},{1,0},{2,3},{3,2},{4,5},{5,4},{6,7},{7,6},{8,9},{9,8},{10,11... | collective-permute-start | bytes 1179656 | tf_op jit(solution)/shard_map/ppermute | solution.py:305
  91.1 19.3 %collective-permute-start.24 = (f32[3,16,8,256]{3,2,1,0:T(8,128)S(1)}, f32[3,16,8,256]{3,2,1,0:T(8,128)S(1)}, u32[]{:S(2)}, u32[]{:S(2)}) collective-permute-start(f32[3,16,8,256]{3,2,1,0:T(8,128)S(1)} %get-tuple-element.105), channel_id=1, source_target_pairs={{1,2},{3,4},{5,6},{7,8},{9,10},{11,12},{13,14},{15,0},{2,1},{4,3},... | collective-permute-start | bytes 1179656 | tf_op jit(solution)/shard_map/ppermute | solution.py:300
  91.4 19.0 %collective-permute-start.25 = (f32[3,16,8,256]{3,2,1,0:T(8,128)S(1)}, f32[3,16,8,256]{3,2,1,0:T(8,128)S(1)}, u32[]{:S(2)}, u32[]{:S(2)}) collective-permute-start(f32[3,16,8,256]{3,2,1,0:T(8,128)S(1)} %get-tuple-element.106), channel_id=1, source_target_pairs={{0,1},{1,0},{2,3},{3,2},{4,5},{5,4},{6,7},{7,6},{8,9},{9,8},{10,11... | collective-permute-start | bytes 1179656 | tf_op jit(solution)/shard_map/ppermute | solution.py:305
  103.8 16.3 %collective-permute-start.22 = (f32[3,16,8,256]{3,2,1,0:T(8,128)S(1)}, f32[3,16,8,256]{3,2,1,0:T(8,128)S(1)}, u32[]{:S(2)}, u32[]{:S(2)}) collective-permute-start(f32[3,16,8,256]{3,2,1,0:T(8,128)S(1)} %get-tuple-element.103), channel_id=1, source_target_pairs={{1,2},{3,4},{5,6},{7,8},{9,10},{11,12},{13,14},{15,0},{2,1},{4,3},... | collective-permute-start | bytes 1179656 | tf_op jit(solution)/shard_map/ppermute | solution.py:300
  104.8 15.3 %collective-permute-start.23 = (f32[3,16,8,256]{3,2,1,0:T(8,128)S(1)}, f32[3,16,8,256]{3,2,1,0:T(8,128)S(1)}, u32[]{:S(2)}, u32[]{:S(2)}) collective-permute-start(f32[3,16,8,256]{3,2,1,0:T(8,128)S(1)} %get-tuple-element.104), channel_id=1, source_target_pairs={{0,1},{1,0},{2,3},{3,2},{4,5},{5,4},{6,7},{7,6},{8,9},{9,8},{10,11... | collective-permute-start | bytes 1179656 | tf_op jit(solution)/shard_map/ppermute | solution.py:305
  112.3 10.8 %collective-permute-start.26 = (f32[3,16,8,256]{3,2,1,0:T(8,128)S(1)}, f32[3,16,8,256]{3,2,1,0:T(8,128)S(1)}, u32[]{:S(2)}, u32[]{:S(2)}) collective-permute-start(f32[3,16,8,256]{3,2,1,0:T(8,128)S(1)} %get-tuple-element.110), channel_id=1, source_target_pairs={{1,2},{3,4},{5,6},{7,8},{9,10},{11,12},{13,14},{15,0},{2,1},{4,3},... | collective-permute-start | bytes 1179656 | tf_op jit(solution)/shard_map/ppermute | solution.py:300
  113.3 9.8 %collective-permute-start.27 = (f32[3,16,8,256]{3,2,1,0:T(8,128)S(1)}, f32[3,16,8,256]{3,2,1,0:T(8,128)S(1)}, u32[]{:S(2)}, u32[]{:S(2)}) collective-permute-start(f32[3,16,8,256]{3,2,1,0:T(8,128)S(1)} %get-tuple-element.111), channel_id=1, source_target_pairs={{0,1},{1,0},{2,3},{3,2},{4,5},{5,4},{6,7},{7,6},{8,9},{9,8},{10,11... | collective-permute-start | bytes 1179656 | tf_op jit(solution)/shard_map/ppermute | solution.py:305

commit v6 on v5

--- a/solution.py
+++ b/solution.py
@@ -347,7 +347,8 @@
     for number, kind in enumerate(kinds):
         last = number == len(kinds) - 1
         if number > 0:
-            halos = [(swap_far(far), swap_near(near)) for far, near in sides]
+            from_near = [swap_near(near) for far, near in sides]
+            halos = list(zip([swap_far(far) for far, near in sides], from_near))
             if kind == "reinit" and marker is None:
                 marker = pieces
             if kind == "reinit":

time: 126 us -> 126 us (level)
  no operation moved by 1% of the time
where the time goes in v6:
time: 126 us
  Pallas kernels  49.9 us (40%)
  waiting for transfers between devices  37 us (29%)
  starting transfers between devices  28.8 us (23%)
  local copies, waits for them, and re-layouts  5.18 us (4%)
  other arithmetic  4.28 us (3%)
    ppermute x14, waiting for transfers between devices, swap_far(): lax.ppermute(array, 'gx', [(i, (i + 1) % count) for i in odd] + [((i + 1)...  36.9 us
    pallas_call x5, Pallas kernels, local_part(): pl.pallas_call(functools.partial(local_body, len(pieces), both, block), g...  27.9 us
    pallas_call x10, Pallas kernels, finish_part(): pl.pallas_call(functools.partial(finish_body, kind, last), grid=(per // b...  18.6 us
    ppermute x14, starting transfers between devices, swap_near(): lax.ppermute(array, 'gx', [(i, i + 1 - 2 * (i % 2)) for i in range(count)])  15.7 us
    ppermute x14, starting transfers between devices, swap_far(): lax.ppermute(array, 'gx', [(i, (i + 1) % count) for i in odd] + [((i + 1)...  13.1 us
    pallas_call x4, Pallas kernels, sweep_part(): pl.pallas_call(sweep_body, in_specs=[pl.BlockSpec(memory_space=pltpu.SMEM...  3.4 us
  transfers between devices with their start and end apart: 28, of which 9 were waited for; matrix products, arithmetic and copies ran while one was open for 5% of the time, Pallas kernels for 38%

profile of v6, /device:TPU:1, one launch (start us, length us, event | category | flops | bytes accessed | tf_op | source)
XLA Modules:
  0.0 126.1 jit_solution(8563600780851543819)
XLA Ops:
  0.6 1.3 %fusion.9 = (f32[1,256,256]{2,1,0:T(8,128)S(1)}, f32[1,256,256]{2,1,0:T(8,128)S(1)}, f32[1,256,256]{2,1,0:T(8,128)S(1)}, f32[1,256,256]{2,1,0:T(8,128)S(1)}) fusion(s32[4,256,256]{2,1,0:T(8,128)} %param.9, pred[]{:T(512)S(6)} %eq.3, f32[4,256,256]{2,1,0:T(8,128)} %param.8), kind=kLoop, calls=%fused_computation.30 | loop fusion | flops 786432 | bytes 2097153 | tf_op jit(solution)/shard_map/jit(_where)/select_n | solution.py:324
  1.9 0.3 copy_bitcast_fusion.2
  2.3 2.7 %collective-permute-start = (f32[1,32,8,256]{3,2,1,0:T(8,128)S(1)}, f32[1,32,8,256]{3,2,1,0:T(8,128)S(1)}, u32[]{:S(2)}, u32[]{:S(2)}) collective-permute-start(f32[1,32,8,256]{3,2,1,0:T(8,128)S(1)} %get-tuple-element.131.far_ref), channel_id=1, source_target_pairs={{1,2},{3,4},{5,6},{7,8},{9,10},{11,12},{13,14},{15,0},{2,1},{4,3},... | collective-permute-start | bytes 786440 | tf_op jit(solution)/shard_map/ppermute | solution.py:300
  4.9 2.9 %collective-permute-start.1 = (f32[1,32,8,256]{3,2,1,0:T(8,128)S(1)}, f32[1,32,8,256]{3,2,1,0:T(8,128)S(1)}, u32[]{:S(2)}, u32[]{:S(2)}) collective-permute-start(f32[1,32,8,256]{3,2,1,0:T(8,128)S(1)} %get-tuple-element.130.near_ref), channel_id=1, source_target_pairs={{0,1},{1,0},{2,3},{3,2},{4,5},{5,4},{6,7},{7,6},{8,9},{9,8},{10,11... | collective-permute-start | bytes 786440 | tf_op jit(solution)/shard_map/ppermute | solution.py:305
  7.8 0.1 convert_element_type.21
  7.9 0.6 copy.37
  8.5 0.6 copy-done
  9.1 1.2 bitcast_multiply_fusion.fixed_ref
  10.3 0.1 slice_select_fusion
  10.4 0.6 copy.38
  11.1 1.0 sweep_part.4
  12.1 0.2 fusion.4.far_ref
  12.3 1.5 %collective-permute-start.2 = (f32[1,32,8,256]{3,2,1,0:T(8,128)S(1)}, f32[1,32,8,256]{3,2,1,0:T(8,128)S(1)}, u32[]{:S(2)}, u32[]{:S(2)}) collective-permute-start(f32[1,32,8,256]{3,2,1,0:T(8,128)S(1)} %fusion.4.far_ref), channel_id=1, source_target_pairs={{1,2},{3,4},{5,6},{7,8},{9,10},{11,12},{13,14},{15,0},{2,1},{4,3},... | collective-permute-start | bytes 786440 | tf_op jit(solution)/shard_map/ppermute | solution.py:300
  13.8 0.2 fusion.near_ref
  14.0 2.9 %collective-permute-start.3 = (f32[1,32,8,256]{3,2,1,0:T(8,128)S(1)}, f32[1,32,8,256]{3,2,1,0:T(8,128)S(1)}, u32[]{:S(2)}, u32[]{:S(2)}) collective-permute-start(f32[1,32,8,256]{3,2,1,0:T(8,128)S(1)} %fusion.near_ref), channel_id=1, source_target_pairs={{0,1},{1,0},{2,3},{3,2},{4,5},{5,4},{6,7},{7,6},{8,9},{9,8},{10,11... | collective-permute-start | bytes 786440 | tf_op jit(solution)/shard_map/ppermute | solution.py:305
  17.0 5.6 %local_part.5 = (f32[4,32,8,256]{3,2,1,0:T(8,128)S(1)}, f32[4,32,8,256]{3,2,1,0:T(8,128)S(1)}) custom-call(f32[4,32,8,256]{3,2,1,0:T(8,128)S(1)} %bitcast.64), custom_call_target="tpu_custom_call" | custom-call | flops 34078720 | bytes 3145728 | tf_op jit(solution)/shard_map/local_part/pallas_call | solution.py:149
  22.6 0.8 sweep_part.5
  23.4 0.2 collective-permute-done.2
  23.7 0.2 fusion.5.far_ref
  23.9 2.5 %collective-permute-start.4 = (f32[1,32,8,256]{3,2,1,0:T(8,128)S(1)}, f32[1,32,8,256]{3,2,1,0:T(8,128)S(1)}, u32[]{:S(2)}, u32[]{:S(2)}) collective-permute-start(f32[1,32,8,256]{3,2,1,0:T(8,128)S(1)} %fusion.5.far_ref), channel_id=1, source_target_pairs={{1,2},{3,4},{5,6},{7,8},{9,10},{11,12},{13,14},{15,0},{2,1},{4,3},... | collective-permute-start | bytes 786440 | tf_op jit(solution)/shard_map/ppermute | solution.py:300
  26.4 0.2 fusion.1.near_ref
  26.6 1.8 %collective-permute-start.5 = (f32[1,32,8,256]{3,2,1,0:T(8,128)S(1)}, f32[1,32,8,256]{3,2,1,0:T(8,128)S(1)}, u32[]{:S(2)}, u32[]{:S(2)}) collective-permute-start(f32[1,32,8,256]{3,2,1,0:T(8,128)S(1)} %fusion.1.near_ref), channel_id=1, source_target_pairs={{0,1},{1,0},{2,3},{3,2},{4,5},{5,4},{6,7},{7,6},{8,9},{9,8},{10,11... | collective-permute-start | bytes 786440 | tf_op jit(solution)/shard_map/ppermute | solution.py:305
  28.6 0.8 sweep_part.6
  29.4 12.9 %collective-permute-done.4 = f32[1,32,8,256]{3,2,1,0:T(8,128)S(1)} collective-permute-done((f32[1,32,8,256]{3,2,1,0:T(8,128)S(1)}, f32[1,32,8,256]{3,2,1,0:T(8,128)S(1)}, u32[]{:S(2)}, u32[]{:S(2)}) %collective-permute-start.4) | collective-permute-done | bytes 262176 | tf_op jit(solution)/shard_map/ppermute | solution.py:300
  42.3 0.2 fusion.6.far_ref
  42.5 0.7 collective-permute-start.6
  43.3 0.2 fusion.2.near_ref
  43.6 0.8 sweep_part.7
  44.4 5.0 %collective-permute-done.6 = f32[1,32,8,256]{3,2,1,0:T(8,128)S(1)} collective-permute-done((f32[1,32,8,256]{3,2,1,0:T(8,128)S(1)}, f32[1,32,8,256]{3,2,1,0:T(8,128)S(1)}, u32[]{:S(2)}, u32[]{:S(2)}) %collective-permute-start.6) | collective-permute-done | bytes 262176 | tf_op jit(solution)/shard_map/ppermute | solution.py:300
  49.4 0.4 broadcast_select_fusion.3
  49.7 0.2 pad_maximum_fusion
  49.9 1.9 %finish_part.10 = (f32[4,16,8,256]{3,2,1,0:T(8,128)S(1)}, f32[3,16,8,256]{3,2,1,0:T(8,128)S(1)}, f32[3,16,8,256]{3,2,1,0:T(8,128)S(1)}) custom-call(s32[1]{0:T(128)} %bitcast.parity_ref.refs_0_, f32[4,16,8,256]{3,2,1,0:T(8,128)S(1)} %get-tuple-element.117.refs_1_, f32[3,16,8,256]{3,2,1,0:T(8,128)S(1)} %collective-permute-done.8.refs_2_, ...), custom_call_target="tpu_custom_call" | custom-call | flops 10485760 | bytes 4194304 | tf_op jit(solution)/shard_map/finish_part/pallas_call | solution.py:224
  51.8 0.7 collective-permute-start.10
  52.6 2.7 %collective-permute-start.11 = (f32[3,16,8,256]{3,2,1,0:T(8,128)S(1)}, f32[3,16,8,256]{3,2,1,0:T(8,128)S(1)}, u32[]{:S(2)}, u32[]{:S(2)}) collective-permute-start(f32[3,16,8,256]{3,2,1,0:T(8,128)S(1)} %get-tuple-element.88), channel_id=1, source_target_pairs={{0,1},{1,0},{2,3},{3,2},{4,5},{5,4},{6,7},{7,6},{8,9},{9,8},{10,11... | collective-permute-start | bytes 1179656 | tf_op jit(solution)/shard_map/ppermute | solution.py:305
  55.2 1.9 %finish_part.11 = (f32[4,16,8,256]{3,2,1,0:T(8,128)S(1)}, f32[3,16,8,256]{3,2,1,0:T(8,128)S(1)}, f32[3,16,8,256]{3,2,1,0:T(8,128)S(1)}) custom-call(s32[1]{0:T(128)} %bitcast.parity_ref.refs_0_, f32[4,16,8,256]{3,2,1,0:T(8,128)S(1)} %get-tuple-element.116.refs_1_, f32[3,16,8,256]{3,2,1,0:T(8,128)S(1)} %collective-permute-done.12.refs_2_, ...), custom_call_target="tpu_custom_call" | custom-call | flops 10485760 | bytes 4194304 | tf_op jit(solution)/shard_map/finish_part/pallas_call | solution.py:224
  57.2 1.6 %collective-permute-start.17 = (f32[3,16,8,256]{3,2,1,0:T(8,128)S(1)}, f32[3,16,8,256]{3,2,1,0:T(8,128)S(1)}, u32[]{:S(2)}, u32[]{:S(2)}) collective-permute-start(f32[3,16,8,256]{3,2,1,0:T(8,128)S(1)} %get-tuple-element.94), channel_id=1, source_target_pairs={{0,1},{1,0},{2,3},{3,2},{4,5},{5,4},{6,7},{7,6},{8,9},{9,8},{10,11... | collective-permute-start | bytes 1179656 | tf_op jit(solution)/shard_map/ppermute | solution.py:305
  58.8 5.6 %local_part.6.refs_4_ = f32[4,32,8,256]{3,2,1,0:T(8,128)S(1)} custom-call(f32[4,16,8,256]{3,2,1,0:T(8,128)S(1)} %get-tuple-element.86.refs_0_.refs_1_, f32[4,16,8,256]{3,2,1,0:T(8,128)S(1)} %get-tuple-element.89.refs_1_, f32[4,32,8,256]{3,2,1,0:T(8,128)S(1)} %get-tuple-element.118.refs_6_.refs_2_.refs_5_), custom_call_target="tpu_custom_call" | custom-call | flops 34078720 | bytes 3145728 | tf_op jit(solution)/shard_map/local_part/pallas_call | solution.py:149
  64.4 3.1 %collective-permute-done.10.refs_2_ = f32[3,16,8,256]{3,2,1,0:T(8,128)S(1)} collective-permute-done((f32[3,16,8,256]{3,2,1,0:T(8,128)S(1)}, f32[3,16,8,256]{3,2,1,0:T(8,128)S(1)}, u32[]{:S(2)}, u32[]{:S(2)}) %collective-permute-start.10) | collective-permute-done | bytes 393248 | tf_op jit(solution)/shard_map/ppermute | solution.py:300
  67.5 1.9 %finish_part.12 = (f32[4,16,8,256]{3,2,1,0:T(8,128)S(1)}, f32[3,16,8,256]{3,2,1,0:T(8,128)S(1)}, f32[3,16,8,256]{3,2,1,0:T(8,128)S(1)}) custom-call(s32[1]{0:T(128)} %bitcast.parity_ref.refs_0_, f32[4,16,8,256]{3,2,1,0:T(8,128)S(1)} %get-tuple-element.86.refs_0_.refs_1_, f32[3,16,8,256]{3,2,1,0:T(8,128)S(1)} %collective-permute-done.10.refs_2_, ...), custom_call_target="tpu_custom_call" | custom-call | flops 10485760 | bytes 4194304 | tf_op jit(solution)/shard_map/finish_part/pallas_call | solution.py:224
  69.4 0.7 collective-permute-start.14
  70.2 5.8 %collective-permute-done.16.refs_2_ = f32[3,16,8,256]{3,2,1,0:T(8,128)S(1)} collective-permute-done((f32[3,16,8,256]{3,2,1,0:T(8,128)S(1)}, f32[3,16,8,256]{3,2,1,0:T(8,128)S(1)}, u32[]{:S(2)}, u32[]{:S(2)}) %collective-permute-start.16) | collective-permute-done | bytes 393248 | tf_op jit(solution)/shard_map/ppermute | solution.py:300
  75.9 1.9 %finish_part.13 = (f32[4,16,8,256]{3,2,1,0:T(8,128)S(1)}, f32[3,16,8,256]{3,2,1,0:T(8,128)S(1)}, f32[3,16,8,256]{3,2,1,0:T(8,128)S(1)}) custom-call(s32[1]{0:T(128)} %bitcast.parity_ref.refs_0_, f32[4,16,8,256]{3,2,1,0:T(8,128)S(1)} %get-tuple-element.89.refs_1_, f32[3,16,8,256]{3,2,1,0:T(8,128)S(1)} %collective-permute-done.16.refs_2_, ...), custom_call_target="tpu_custom_call" | custom-call | flops 10485760 | bytes 4194304 | tf_op jit(solution)/shard_map/finish_part/pallas_call | solution.py:224
  77.8 0.7 collective-permute-start.20
  78.6 5.6 %local_part.7.refs_4_ = f32[4,32,8,256]{3,2,1,0:T(8,128)S(1)} custom-call(f32[4,16,8,256]{3,2,1,0:T(8,128)S(1)} %get-tuple-element.90.refs_0_.refs_1_, f32[4,16,8,256]{3,2,1,0:T(8,128)S(1)} %get-tuple-element.95.refs_1_, f32[4,32,8,256]{3,2,1,0:T(8,128)S(1)} %get-tuple-element.118.refs_6_.refs_2_.refs_5_), custom_call_target="tpu_custom_call" | custom-call | flops 34078720 | bytes 3145728 | tf_op jit(solution)/shard_map/local_part/pallas_call | solution.py:149
  84.2 0.2 collective-permute-done.14.refs_2_
  84.4 1.9 %finish_part.14 = (f32[4,16,8,256]{3,2,1,0:T(8,128)S(1)}, f32[3,16,8,256]{3,2,1,0:T(8,128)S(1)}, f32[3,16,8,256]{3,2,1,0:T(8,128)S(1)}) custom-call(s32[1]{0:T(128)} %bitcast.parity_ref.refs_0_, f32[4,16,8,256]{3,2,1,0:T(8,128)S(1)} %get-tuple-element.90.refs_0_.refs_1_, f32[3,16,8,256]{3,2,1,0:T(8,128)S(1)} %collective-permute-done.14.refs_2_, ...), custom_call_target="tpu_custom_call" | custom-call | flops 10485760 | bytes 4194304 | tf_op jit(solution)/shard_map/finish_part/pallas_call | solution.py:224
  86.3 1.0 collective-permute-start.18
  87.3 2.0 %collective-permute-start.19 = (f32[3,16,8,256]{3,2,1,0:T(8,128)S(1)}, f32[3,16,8,256]{3,2,1,0:T(8,128)S(1)}, u32[]{:S(2)}, u32[]{:S(2)}) collective-permute-start(f32[3,16,8,256]{3,2,1,0:T(8,128)S(1)} %get-tuple-element.98), channel_id=1, source_target_pairs={{0,1},{1,0},{2,3},{3,2},{4,5},{5,4},{6,7},{7,6},{8,9},{9,8},{10,11... | collective-permute-start | bytes 1179656 | tf_op jit(solution)/shard_map/ppermute | solution.py:305
  89.2 1.9 %finish_part.15 = (f32[4,16,8,256]{3,2,1,0:T(8,128)S(1)}, f32[3,16,8,256]{3,2,1,0:T(8,128)S(1)}, f32[3,16,8,256]{3,2,1,0:T(8,128)S(1)}) custom-call(s32[1]{0:T(128)} %bitcast.parity_ref.refs_0_, f32[4,16,8,256]{3,2,1,0:T(8,128)S(1)} %get-tuple-element.95.refs_1_, f32[3,16,8,256]{3,2,1,0:T(8,128)S(1)} %collective-permute-done.20.refs_2_, ...), custom_call_target="tpu_custom_call" | custom-call | flops 10485760 | bytes 4194304 | tf_op jit(solution)/shard_map/finish_part/pallas_call | solution.py:224
  91.1 0.3 collective-permute-start.24
  91.4 1.7 %collective-permute-start.25 = (f32[3,16,8,256]{3,2,1,0:T(8,128)S(1)}, f32[3,16,8,256]{3,2,1,0:T(8,128)S(1)}, u32[]{:S(2)}, u32[]{:S(2)}) collective-permute-start(f32[3,16,8,256]{3,2,1,0:T(8,128)S(1)} %get-tuple-element.106), channel_id=1, source_target_pairs={{0,1},{1,0},{2,3},{3,2},{4,5},{5,4},{6,7},{7,6},{8,9},{9,8},{10,11... | collective-permute-start | bytes 1179656 | tf_op jit(solution)/shard_map/ppermute | solution.py:305
  93.2 5.6 %local_part.8.refs_4_ = f32[4,32,8,256]{3,2,1,0:T(8,128)S(1)} custom-call(f32[4,16,8,256]{3,2,1,0:T(8,128)S(1)} %get-tuple-element.96.refs_0_.refs_1_.refs_5_, f32[4,16,8,256]{3,2,1,0:T(8,128)S(1)} %get-tuple-element.101.refs_1_.refs_5_, f32[4,32,8,256]{3,2,1,0:T(8,128)S(1)} %constant_dynamic-update-slice_fusion.refs_2_), custom_call_target="tpu_custom_call" | custom-call | flops 34078720 | bytes 3145728 | tf_op jit(solution)/shard_map/local_part/pallas_call | solution.py:149
  98.8 3.1 %collective-permute-done.18.refs_2_ = f32[3,16,8,256]{3,2,1,0:T(8,128)S(1)} collective-permute-done((f32[3,16,8,256]{3,2,1,0:T(8,128)S(1)}, f32[3,16,8,256]{3,2,1,0:T(8,128)S(1)}, u32[]{:S(2)}, u32[]{:S(2)}) %collective-permute-start.18) | collective-permute-done | bytes 393248 | tf_op jit(solution)/shard_map/ppermute | solution.py:300
  102.0 1.9 %finish_part.16 = (f32[4,16,8,256]{3,2,1,0:T(8,128)S(1)}, f32[3,16,8,256]{3,2,1,0:T(8,128)S(1)}, f32[3,16,8,256]{3,2,1,0:T(8,128)S(1)}) custom-call(s32[1]{0:T(128)} %bitcast.parity_ref.refs_0_, f32[4,16,8,256]{3,2,1,0:T(8,128)S(1)} %get-tuple-element.96.refs_0_.refs_1_.refs_5_, f32[3,16,8,256]{3,2,1,0:T(8,128)S(1)} %collective-permute-done.18.refs_2_, ...), custom_call_target="tpu_custom_call" | custom-call | flops 10485760 | bytes 4194304 | tf_op jit(solution)/shard_map/finish_part/pallas_call | solution.py:224
  103.8 1.0 collective-permute-start.22
  104.8 5.6 %collective-permute-done.24.refs_2_ = f32[3,16,8,256]{3,2,1,0:T(8,128)S(1)} collective-permute-done((f32[3,16,8,256]{3,2,1,0:T(8,128)S(1)}, f32[3,16,8,256]{3,2,1,0:T(8,128)S(1)}, u32[]{:S(2)}, u32[]{:S(2)}) %collective-permute-start.24) | collective-permute-done | bytes 393248 | tf_op jit(solution)/shard_map/ppermute | solution.py:300
  110.4 1.9 %finish_part.17 = (f32[4,16,8,256]{3,2,1,0:T(8,128)S(1)}, f32[3,16,8,256]{3,2,1,0:T(8,128)S(1)}, f32[3,16,8,256]{3,2,1,0:T(8,128)S(1)}) custom-call(s32[1]{0:T(128)} %bitcast.parity_ref.refs_0_, f32[4,16,8,256]{3,2,1,0:T(8,128)S(1)} %get-tuple-element.101.refs_1_.refs_5_, f32[3,16,8,256]{3,2,1,0:T(8,128)S(1)} %collective-permute-done.24.refs_2_, ...), custom_call_target="tpu_custom_call" | custom-call | flops 10485760 | bytes 4194304 | tf_op jit(solution)/shard_map/finish_part/pallas_call | solution.py:224
  112.3 1.0 collective-permute-start.26
  113.3 1.3 %copy.12 = f32[4,8,32,256]{3,2,1,0:T(8,128)} copy(f32[4,8,32,256]{3,1,2,0:T(8,128)S(1)} %get-tuple-element.119) | data formatting | bytes 2097152 | tf_op jit(solution)/shard_map/transpose | solution.py:294
  114.6 5.6 %local_part.9.refs_4_ = f32[4,32,8,256]{3,2,1,0:T(8,128)S(1)} custom-call(f32[4,16,8,256]{3,2,1,0:T(8,128)S(1)} %get-tuple-element.102.refs_0_.refs_1_, f32[4,16,8,256]{3,2,1,0:T(8,128)S(1)} %get-tuple-element.109.refs_1_, f32[4,32,8,256]{3,2,1,0:T(8,128)S(1)} %constant_dynamic-update-slice_fusion.refs_2_), custom_call_target="tpu_custom_call" | custom-call | flops 34078720 | bytes 3145728 | tf_op jit(solution)/shard_map/local_part/pallas_call | solution.py:149
  120.2 1.8 %finish_part.18 = f32[4,16,8,256]{3,2,1,0:T(8,128)S(1)} custom-call(s32[1]{0:T(128)} %bitcast.parity_ref.refs_0_, f32[4,16,8,256]{3,2,1,0:T(8,128)S(1)} %get-tuple-element.102.refs_0_.refs_1_, f32[3,16,8,256]{3,2,1,0:T(8,128)S(1)} %collective-permute-done.22.refs_2_, f32[3,16,8,256]{3,2,1,0:T(8,128)S(1)} %collective-permute-done.23.refs_3_, ...), custom_call_target="tpu_custom_call" | custom-call | flops 10485760 | bytes 4194304 | tf_op jit(solution)/shard_map/finish_part/pallas_call | solution.py:224
  122.0 1.0 collective-permute-done.26.refs_2_
  123.0 1.8 %finish_part.19 = f32[4,16,8,256]{3,2,1,0:T(8,128)S(1)} custom-call(s32[1]{0:T(128)} %bitcast.parity_ref.refs_0_, f32[4,16,8,256]{3,2,1,0:T(8,128)S(1)} %get-tuple-element.109.refs_1_, f32[3,16,8,256]{3,2,1,0:T(8,128)S(1)} %collective-permute-done.26.refs_2_, f32[3,16,8,256]{3,2,1,0:T(8,128)S(1)} %collective-permute-done.27.refs_3_, ...), custom_call_target="tpu_custom_call" | custom-call | flops 10485760 | bytes 4194304 | tf_op jit(solution)/shard_map/finish_part/pallas_call | solution.py:224
  124.8 1.3 %copy.13 = f32[4,8,32,256]{3,2,1,0:T(8,128)} copy(f32[4,8,32,256]{3,1,2,0:T(8,128)S(1)} %bitcast_dynamic-update-slice_fusion) | data formatting | bytes 2097152 | tf_op jit(solution)/shard_map/scatter | solution.py:372
  (42 shorter events, 0.9 us)
Async XLA Ops:
  1.9 5.9 %copy-start.1 = (s32[4,256,256]{2,1,0:T(8,128)S(1)}, s32[4,256,256]{2,1,0:T(8,128)}, u32[]{:S(2)}) copy-start(s32[4,256,256]{2,1,0:T(8,128)} %param.9) | copy-start | bytes 3145732
  2.3 9.8 %collective-permute-start = (f32[1,32,8,256]{3,2,1,0:T(8,128)S(1)}, f32[1,32,8,256]{3,2,1,0:T(8,128)S(1)}, u32[]{:S(2)}, u32[]{:S(2)}) collective-permute-start(f32[1,32,8,256]{3,2,1,0:T(8,128)S(1)} %get-tuple-element.131.far_ref), channel_id=1, source_target_pairs={{1,2},{3,4},{5,6},{7,8},{9,10},{11,12},{13,14},{15,0},{2,1},{4,3},... | collective-permute-start | bytes 786440 | tf_op jit(solution)/shard_map/ppermute | solution.py:300
  4.9 3.0 %copy-start.2 = (f32[4,256,256]{2,1,0:T(8,128)S(1)}, f32[4,256,256]{2,1,0:T(8,128)}, u32[]{:S(2)}) copy-start(f32[4,256,256]{2,1,0:T(8,128)} %param.7) | copy-start | bytes 3145732
  4.9 8.9 %collective-permute-start.1 = (f32[1,32,8,256]{3,2,1,0:T(8,128)S(1)}, f32[1,32,8,256]{3,2,1,0:T(8,128)S(1)}, u32[]{:S(2)}, u32[]{:S(2)}) collective-permute-start(f32[1,32,8,256]{3,2,1,0:T(8,128)S(1)} %get-tuple-element.130.near_ref), channel_id=1, source_target_pairs={{0,1},{1,0},{2,3},{3,2},{4,5},{5,4},{6,7},{7,6},{8,9},{9,8},{10,11... | collective-permute-start | bytes 786440 | tf_op jit(solution)/shard_map/ppermute | solution.py:305
  7.9 1.2 copy-start
  12.3 11.4 %collective-permute-start.2 = (f32[1,32,8,256]{3,2,1,0:T(8,128)S(1)}, f32[1,32,8,256]{3,2,1,0:T(8,128)S(1)}, u32[]{:S(2)}, u32[]{:S(2)}) collective-permute-start(f32[1,32,8,256]{3,2,1,0:T(8,128)S(1)} %fusion.4.far_ref), channel_id=1, source_target_pairs={{1,2},{3,4},{5,6},{7,8},{9,10},{11,12},{13,14},{15,0},{2,1},{4,3},... | collective-permute-start | bytes 786440 | tf_op jit(solution)/shard_map/ppermute | solution.py:300
  14.0 12.4 %collective-permute-start.3 = (f32[1,32,8,256]{3,2,1,0:T(8,128)S(1)}, f32[1,32,8,256]{3,2,1,0:T(8,128)S(1)}, u32[]{:S(2)}, u32[]{:S(2)}) collective-permute-start(f32[1,32,8,256]{3,2,1,0:T(8,128)S(1)} %fusion.near_ref), channel_id=1, source_target_pairs={{0,1},{1,0},{2,3},{3,2},{4,5},{5,4},{6,7},{7,6},{8,9},{9,8},{10,11... | collective-permute-start | bytes 786440 | tf_op jit(solution)/shard_map/ppermute | solution.py:305
  17.0 33.0 %collective-permute-start.8 = (f32[3,16,8,256]{3,2,1,0:T(8,128)S(1)}, f32[3,16,8,256]{3,2,1,0:T(8,128)S(1)}, u32[]{:S(2)}, u32[]{:S(2)}) collective-permute-start(f32[3,16,8,256]{3,2,1,0:T(8,128)S(1)} %get-tuple-element.129), channel_id=1, source_target_pairs={{1,2},{3,4},{5,6},{7,8},{9,10},{11,12},{13,14},{15,0},{2,1},{4,3},... | collective-permute-start | bytes 1179656 | tf_op jit(solution)/shard_map/ppermute | solution.py:300
  23.9 18.5 %collective-permute-start.4 = (f32[1,32,8,256]{3,2,1,0:T(8,128)S(1)}, f32[1,32,8,256]{3,2,1,0:T(8,128)S(1)}, u32[]{:S(2)}, u32[]{:S(2)}) collective-permute-start(f32[1,32,8,256]{3,2,1,0:T(8,128)S(1)} %fusion.5.far_ref), channel_id=1, source_target_pairs={{1,2},{3,4},{5,6},{7,8},{9,10},{11,12},{13,14},{15,0},{2,1},{4,3},... | collective-permute-start | bytes 786440 | tf_op jit(solution)/shard_map/ppermute | solution.py:300
  26.6 16.7 %collective-permute-start.5 = (f32[1,32,8,256]{3,2,1,0:T(8,128)S(1)}, f32[1,32,8,256]{3,2,1,0:T(8,128)S(1)}, u32[]{:S(2)}, u32[]{:S(2)}) collective-permute-start(f32[1,32,8,256]{3,2,1,0:T(8,128)S(1)} %fusion.1.near_ref), channel_id=1, source_target_pairs={{0,1},{1,0},{2,3},{3,2},{4,5},{5,4},{6,7},{7,6},{8,9},{9,8},{10,11... | collective-permute-start | bytes 786440 | tf_op jit(solution)/shard_map/ppermute | solution.py:305
  28.5 21.5 %collective-permute-start.9 = (f32[3,16,8,256]{3,2,1,0:T(8,128)S(1)}, f32[3,16,8,256]{3,2,1,0:T(8,128)S(1)}, u32[]{:S(2)}, u32[]{:S(2)}) collective-permute-start(f32[3,16,8,256]{3,2,1,0:T(8,128)S(1)} %get-tuple-element.127), channel_id=1, source_target_pairs={{0,1},{1,0},{2,3},{3,2},{4,5},{5,4},{6,7},{7,6},{8,9},{9,8},{10,11... | collective-permute-start | bytes 1179656 | tf_op jit(solution)/shard_map/ppermute | solution.py:305
  28.5 26.7 %collective-permute-start.12 = (f32[3,16,8,256]{3,2,1,0:T(8,128)S(1)}, f32[3,16,8,256]{3,2,1,0:T(8,128)S(1)}, u32[]{:S(2)}, u32[]{:S(2)}) collective-permute-start(f32[3,16,8,256]{3,2,1,0:T(8,128)S(1)} %get-tuple-element.128), channel_id=1, source_target_pairs={{1,2},{3,4},{5,6},{7,8},{9,10},{11,12},{13,14},{15,0},{2,1},{4,3},... | collective-permute-start | bytes 1179656 | tf_op jit(solution)/shard_map/ppermute | solution.py:300
  42.5 6.8 %collective-permute-start.6 = (f32[1,32,8,256]{3,2,1,0:T(8,128)S(1)}, f32[1,32,8,256]{3,2,1,0:T(8,128)S(1)}, u32[]{:S(2)}, u32[]{:S(2)}) collective-permute-start(f32[1,32,8,256]{3,2,1,0:T(8,128)S(1)} %fusion.6.far_ref), channel_id=1, source_target_pairs={{1,2},{3,4},{5,6},{7,8},{9,10},{11,12},{13,14},{15,0},{2,1},{4,3},... | collective-permute-start | bytes 786440 | tf_op jit(solution)/shard_map/ppermute | solution.py:300
  43.4 5.9 %collective-permute-start.7 = (f32[1,32,8,256]{3,2,1,0:T(8,128)S(1)}, f32[1,32,8,256]{3,2,1,0:T(8,128)S(1)}, u32[]{:S(2)}, u32[]{:S(2)}) collective-permute-start(f32[1,32,8,256]{3,2,1,0:T(8,128)S(1)} %fusion.2.near_ref), channel_id=1, source_target_pairs={{0,1},{1,0},{2,3},{3,2},{4,5},{5,4},{6,7},{7,6},{8,9},{9,8},{10,11... | collective-permute-start | bytes 786440 | tf_op jit(solution)/shard_map/ppermute | solution.py:305
  49.4 5.9 %collective-permute-start.13 = (f32[3,16,8,256]{3,2,1,0:T(8,128)S(1)}, f32[3,16,8,256]{3,2,1,0:T(8,128)S(1)}, u32[]{:S(2)}, u32[]{:S(2)}) collective-permute-start(f32[3,16,8,256]{3,2,1,0:T(8,128)S(1)} %get-tuple-element.126), channel_id=1, source_target_pairs={{0,1},{1,0},{2,3},{3,2},{4,5},{5,4},{6,7},{7,6},{8,9},{9,8},{10,11... | collective-permute-start | bytes 1179656 | tf_op jit(solution)/shard_map/ppermute | solution.py:305
  51.8 15.7 %collective-permute-start.10 = (f32[3,16,8,256]{3,2,1,0:T(8,128)S(1)}, f32[3,16,8,256]{3,2,1,0:T(8,128)S(1)}, u32[]{:S(2)}, u32[]{:S(2)}) collective-permute-start(f32[3,16,8,256]{3,2,1,0:T(8,128)S(1)} %get-tuple-element.87), channel_id=1, source_target_pairs={{1,2},{3,4},{5,6},{7,8},{9,10},{11,12},{13,14},{15,0},{2,1},{4,3},... | collective-permute-start | bytes 1179656 | tf_op jit(solution)/shard_map/ppermute | solution.py:300
  52.6 15.0 %collective-permute-start.11 = (f32[3,16,8,256]{3,2,1,0:T(8,128)S(1)}, f32[3,16,8,256]{3,2,1,0:T(8,128)S(1)}, u32[]{:S(2)}, u32[]{:S(2)}) collective-permute-start(f32[3,16,8,256]{3,2,1,0:T(8,128)S(1)} %get-tuple-element.88), channel_id=1, source_target_pairs={{0,1},{1,0},{2,3},{3,2},{4,5},{5,4},{6,7},{7,6},{8,9},{9,8},{10,11... | collective-permute-start | bytes 1179656 | tf_op jit(solution)/shard_map/ppermute | solution.py:305
  57.1 18.8 %collective-permute-start.16 = (f32[3,16,8,256]{3,2,1,0:T(8,128)S(1)}, f32[3,16,8,256]{3,2,1,0:T(8,128)S(1)}, u32[]{:S(2)}, u32[]{:S(2)}) collective-permute-start(f32[3,16,8,256]{3,2,1,0:T(8,128)S(1)} %get-tuple-element.93), channel_id=1, source_target_pairs={{1,2},{3,4},{5,6},{7,8},{9,10},{11,12},{13,14},{15,0},{2,1},{4,3},... | collective-permute-start | bytes 1179656 | tf_op jit(solution)/shard_map/ppermute | solution.py:300
  57.2 18.8 %collective-permute-start.17 = (f32[3,16,8,256]{3,2,1,0:T(8,128)S(1)}, f32[3,16,8,256]{3,2,1,0:T(8,128)S(1)}, u32[]{:S(2)}, u32[]{:S(2)}) collective-permute-start(f32[3,16,8,256]{3,2,1,0:T(8,128)S(1)} %get-tuple-element.94), channel_id=1, source_target_pairs={{0,1},{1,0},{2,3},{3,2},{4,5},{5,4},{6,7},{7,6},{8,9},{9,8},{10,11... | collective-permute-start | bytes 1179656 | tf_op jit(solution)/shard_map/ppermute | solution.py:305
  69.4 14.9 %collective-permute-start.14 = (f32[3,16,8,256]{3,2,1,0:T(8,128)S(1)}, f32[3,16,8,256]{3,2,1,0:T(8,128)S(1)}, u32[]{:S(2)}, u32[]{:S(2)}) collective-permute-start(f32[3,16,8,256]{3,2,1,0:T(8,128)S(1)} %get-tuple-element.91), channel_id=1, source_target_pairs={{1,2},{3,4},{5,6},{7,8},{9,10},{11,12},{13,14},{15,0},{2,1},{4,3},... | collective-permute-start | bytes 1179656 | tf_op jit(solution)/shard_map/ppermute | solution.py:300
  70.2 14.2 %collective-permute-start.15 = (f32[3,16,8,256]{3,2,1,0:T(8,128)S(1)}, f32[3,16,8,256]{3,2,1,0:T(8,128)S(1)}, u32[]{:S(2)}, u32[]{:S(2)}) collective-permute-start(f32[3,16,8,256]{3,2,1,0:T(8,128)S(1)} %get-tuple-element.92), channel_id=1, source_target_pairs={{0,1},{1,0},{2,3},{3,2},{4,5},{5,4},{6,7},{7,6},{8,9},{9,8},{10,11... | collective-permute-start | bytes 1179656 | tf_op jit(solution)/shard_map/ppermute | solution.py:305
  77.8 11.4 %collective-permute-start.20 = (f32[3,16,8,256]{3,2,1,0:T(8,128)S(1)}, f32[3,16,8,256]{3,2,1,0:T(8,128)S(1)}, u32[]{:S(2)}, u32[]{:S(2)}) collective-permute-start(f32[3,16,8,256]{3,2,1,0:T(8,128)S(1)} %get-tuple-element.99), channel_id=1, source_target_pairs={{1,2},{3,4},{5,6},{7,8},{9,10},{11,12},{13,14},{15,0},{2,1},{4,3},... | collective-permute-start | bytes 1179656 | tf_op jit(solution)/shard_map/ppermute | solution.py:300
  78.6 10.6 %collective-permute-start.21 = (f32[3,16,8,256]{3,2,1,0:T(8,128)S(1)}, f32[3,16,8,256]{3,2,1,0:T(8,128)S(1)}, u32[]{:S(2)}, u32[]{:S(2)}) collective-permute-start(f32[3,16,8,256]{3,2,1,0:T(8,128)S(1)} %get-tuple-element.100), channel_id=1, source_target_pairs={{0,1},{1,0},{2,3},{3,2},{4,5},{5,4},{6,7},{7,6},{8,9},{9,8},{10,11... | collective-permute-start | bytes 1179656 | tf_op jit(solution)/shard_map/ppermute | solution.py:305
  86.3 15.7 %collective-permute-start.18 = (f32[3,16,8,256]{3,2,1,0:T(8,128)S(1)}, f32[3,16,8,256]{3,2,1,0:T(8,128)S(1)}, u32[]{:S(2)}, u32[]{:S(2)}) collective-permute-start(f32[3,16,8,256]{3,2,1,0:T(8,128)S(1)} %get-tuple-element.97), channel_id=1, source_target_pairs={{1,2},{3,4},{5,6},{7,8},{9,10},{11,12},{13,14},{15,0},{2,1},{4,3},... | collective-permute-start | bytes 1179656 | tf_op jit(solution)/shard_map/ppermute | solution.py:300
  87.3 14.7 %collective-permute-start.19 = (f32[3,16,8,256]{3,2,1,0:T(8,128)S(1)}, f32[3,16,8,256]{3,2,1,0:T(8,128)S(1)}, u32[]{:S(2)}, u32[]{:S(2)}) collective-permute-start(f32[3,16,8,256]{3,2,1,0:T(8,128)S(1)} %get-tuple-element.98), channel_id=1, source_target_pairs={{0,1},{1,0},{2,3},{3,2},{4,5},{5,4},{6,7},{7,6},{8,9},{9,8},{10,11... | collective-permute-start | bytes 1179656 | tf_op jit(solution)/shard_map/ppermute | solution.py:305
  91.1 19.3 %collective-permute-start.24 = (f32[3,16,8,256]{3,2,1,0:T(8,128)S(1)}, f32[3,16,8,256]{3,2,1,0:T(8,128)S(1)}, u32[]{:S(2)}, u32[]{:S(2)}) collective-permute-start(f32[3,16,8,256]{3,2,1,0:T(8,128)S(1)} %get-tuple-element.105), channel_id=1, source_target_pairs={{1,2},{3,4},{5,6},{7,8},{9,10},{11,12},{13,14},{15,0},{2,1},{4,3},... | collective-permute-start | bytes 1179656 | tf_op jit(solution)/shard_map/ppermute | solution.py:300
  91.4 19.0 %collective-permute-start.25 = (f32[3,16,8,256]{3,2,1,0:T(8,128)S(1)}, f32[3,16,8,256]{3,2,1,0:T(8,128)S(1)}, u32[]{:S(2)}, u32[]{:S(2)}) collective-permute-start(f32[3,16,8,256]{3,2,1,0:T(8,128)S(1)} %get-tuple-element.106), channel_id=1, source_target_pairs={{0,1},{1,0},{2,3},{3,2},{4,5},{5,4},{6,7},{7,6},{8,9},{9,8},{10,11... | collective-permute-start | bytes 1179656 | tf_op jit(solution)/shard_map/ppermute | solution.py:305
  103.8 16.3 %collective-permute-start.22 = (f32[3,16,8,256]{3,2,1,0:T(8,128)S(1)}, f32[3,16,8,256]{3,2,1,0:T(8,128)S(1)}, u32[]{:S(2)}, u32[]{:S(2)}) collective-permute-start(f32[3,16,8,256]{3,2,1,0:T(8,128)S(1)} %get-tuple-element.103), channel_id=1, source_target_pairs={{1,2},{3,4},{5,6},{7,8},{9,10},{11,12},{13,14},{15,0},{2,1},{4,3},... | collective-permute-start | bytes 1179656 | tf_op jit(solution)/shard_map/ppermute | solution.py:300
  104.8 15.3 %collective-permute-start.23 = (f32[3,16,8,256]{3,2,1,0:T(8,128)S(1)}, f32[3,16,8,256]{3,2,1,0:T(8,128)S(1)}, u32[]{:S(2)}, u32[]{:S(2)}) collective-permute-start(f32[3,16,8,256]{3,2,1,0:T(8,128)S(1)} %get-tuple-element.104), channel_id=1, source_target_pairs={{0,1},{1,0},{2,3},{3,2},{4,5},{5,4},{6,7},{7,6},{8,9},{9,8},{10,11... | collective-permute-start | bytes 1179656 | tf_op jit(solution)/shard_map/ppermute | solution.py:305
  112.3 10.8 %collective-permute-start.26 = (f32[3,16,8,256]{3,2,1,0:T(8,128)S(1)}, f32[3,16,8,256]{3,2,1,0:T(8,128)S(1)}, u32[]{:S(2)}, u32[]{:S(2)}) collective-permute-start(f32[3,16,8,256]{3,2,1,0:T(8,128)S(1)} %get-tuple-element.110), channel_id=1, source_target_pairs={{1,2},{3,4},{5,6},{7,8},{9,10},{11,12},{13,14},{15,0},{2,1},{4,3},... | collective-permute-start | bytes 1179656 | tf_op jit(solution)/shard_map/ppermute | solution.py:300
  113.3 9.8 %collective-permute-start.27 = (f32[3,16,8,256]{3,2,1,0:T(8,128)S(1)}, f32[3,16,8,256]{3,2,1,0:T(8,128)S(1)}, u32[]{:S(2)}, u32[]{:S(2)}) collective-permute-start(f32[3,16,8,256]{3,2,1,0:T(8,128)S(1)} %get-tuple-element.111), channel_id=1, source_target_pairs={{0,1},{1,0},{2,3},{3,2},{4,5},{5,4},{6,7},{7,6},{8,9},{9,8},{10,11... | collective-permute-start | bytes 1179656 | tf_op jit(solution)/shard_map/ppermute | solution.py:305
